TPU v7x, 768 devices: a whole 4x8x12 slice. The times are simulated.
768 devices in a mesh: grp: 96 (over z, y), dev: 8 (over x, core).
Axes of the slice: x: 4, y: 8, z: 12, core: 2. Of those that a mesh axis runs over, the one named last changes fastest.
Arguments:
- source: float32 [64, 1536, 128], P('dev', 'grp'), may hold values from -8 to 8
- absorb: float32 [64, 1536, 128], P('dev', 'grp'), may hold values from 0.05 to 0.5
- conduct: float32 [64, 1536, 128], P('dev', 'grp'), may hold values from 0.3 to 3
Outputs:
- fine_solution: float32 [64, 1536, 128], P('dev', 'grp')
- fine_residual: float32 [64, 1536, 128], P('dev', 'grp')
All inputs are finite; a program needn't handle non-finite values.
Results may differ from a plain program's by a relative error of at most 0.0003.
Values sent between devices are 32-bit elements; how exact they have to be, the bound alone decides.
No kernel may reach another device: no remote copies, remote signals or barrier semaphores. Data moves between devices by JAX's collectives and lax.ppermute only.
A program may use at most 64 MiB of HBM per device.

v0:
```python
import jax
import jax.numpy as jnp
from jax import lax
from jax.sharding import PartitionSpec as P

CYCLES = 2
BOTTOM = 4


RELAX = 0.8
NEIGHBOURS = (
    (slice(2, None), slice(1, -1), slice(1, -1)),
    (slice(None, -2), slice(1, -1), slice(1, -1)),
    (slice(1, -1), slice(2, None), slice(1, -1)),
    (slice(1, -1), slice(None, -2), slice(1, -1)),
    (slice(1, -1), slice(1, -1), slice(2, None)),
    (slice(1, -1), slice(1, -1), slice(None, -2)),
)


def with_halo(array, sides, width):
    for axis, dim in sides:
        peers, length = (lax.axis_size(axis), array.shape[dim])
        up = [(i, (i + 1) % peers) for i in range(peers - 1)]
        down = [(j, i) for i, j in up]
        last = lax.slice_in_dim(array, length - width, length, axis=dim)
        leading = lax.slice_in_dim(array, 0, width, axis=dim)
        before = lax.ppermute(last, axis, up)
        after = lax.ppermute(leading, axis, down)
        array = jnp.concatenate([before, array, after], axis=dim)
    return array


def stencil_parts(padded_field, padded_coef):
    padded_field = jnp.pad(padded_field, ((0, 0), (0, 0), (1, 1)))
    padded_coef = jnp.pad(padded_coef, ((0, 0), (0, 0), (1, 1)))
    center_field = padded_field[1:-1, 1:-1, 1:-1]
    center_coef = padded_coef[1:-1, 1:-1, 1:-1]
    face_sum = jnp.zeros_like(center_field)
    beside = jnp.zeros_like(center_field)
    for window in NEIGHBOURS:
        face = (center_coef + padded_coef[window]) * 0.5
        face_sum = face_sum + face
        beside = beside + face * padded_field[window]
    return (center_field, face_sum, beside)


def relax_once(padded_field, padded_coef, absorb, rhs, spacing):
    center_field, face_sum, beside = stencil_parts(padded_field, padded_coef)
    diagonal = absorb + face_sum / spacing
    applied = diagonal * center_field - beside / spacing
    return center_field + RELAX * (rhs - applied) / diagonal


def residual_of(padded_field, padded_coef, absorb, rhs, spacing):
    center_field, face_sum, beside = stencil_parts(padded_field, padded_coef)
    diagonal = absorb + face_sum / spacing
    applied = diagonal * center_field - beside / spacing
    return rhs - applied


def restrict(field):
    size_x, size_y, size_z = field.shape
    blocks = field.reshape(size_x // 2, 2, size_y // 2, 2, size_z // 2, 2)
    return blocks.sum(axis=(1, 3, 5)) * 0.125


def prolong(field):
    return jnp.repeat(jnp.repeat(jnp.repeat(field, 2, 0), 2, 1), 2, 2)


def fine_layers(stacked, width):
    return with_halo(stacked, (("grp", 2), ("dev", 1)), width)


def coarse_layers(stacked):
    return with_halo(stacked, (("grp", 2), ("dev", 1)), 1)


def fine_loop(field):
    return fine_layers(field[None], 1)[0]


def coarse_loop(field):
    return coarse_layers(field[None])[0]


def local(source, absorb, conduct):
    absorb_mid = restrict(absorb)
    absorb_low = restrict(absorb_mid)
    conduct_mid = restrict(conduct)
    conduct_low = restrict(conduct_mid)
    coef_mid = coarse_loop(conduct_mid)
    coef_fine = fine_loop(conduct)

    def smooth_pair(field):
        for sweep_index in range(2):
            field = relax_once(fine_loop(field), coef_fine, absorb, source, 1.0)
        return field

    coef_low = coarse_loop(conduct_low)
    fine = jnp.zeros_like(source)
    for turn in range(CYCLES):
        fine = smooth_pair(fine)
        middle_rhs = restrict(residual_of(fine_loop(fine), coef_fine, absorb, source, 1.0))
        middle = jnp.zeros_like(middle_rhs)
        for sweep_index in range(2):
            middle = relax_once(coarse_loop(middle), coef_mid, absorb_mid, middle_rhs, 4.0)
        lowest_rhs = restrict(
            residual_of(coarse_loop(middle), coef_mid, absorb_mid, middle_rhs, 4.0)
        )
        lowest = jnp.zeros_like(lowest_rhs)
        for bottom_sweep_index in range(BOTTOM):
            lowest = relax_once(coarse_loop(lowest), coef_low, absorb_low, lowest_rhs, 16.0)
        middle = middle + prolong(lowest)
        for sweep_index in range(2):
            middle = relax_once(coarse_loop(middle), coef_mid, absorb_mid, middle_rhs, 4.0)
        fine = fine + prolong(middle)
        fine = smooth_pair(fine)
    final_residual = residual_of(fine_loop(fine), coef_fine, absorb, source, 1.0)
    return (fine, final_residual)


def solution(mesh):
    in_specs = (P("dev", "grp", None), P("dev", "grp", None), P("dev", "grp", None))
    out_specs = (P("dev", "grp", None), P("dev", "grp", None))
    return jax.shard_map(local, mesh=mesh, in_specs=in_specs, out_specs=out_specs, check_vma=False)
```

profile of v0, /device:TPU:505, one launch (start us, length us, event | category | flops | bytes accessed | tf_op | source)
XLA Modules:
  0.0 545.6 jit_solution(124441863952274546)
XLA Ops:
  3.6 5.6 %collective-permute-start.28 = (f32[1,2,1,32]{3,2,1,0:T(1,128)S(1)}, f32[1,2,1,32]{3,2,1,0:T(1,128)S(1)}, u32[]{:S(2)}, u32[]{:S(2)}) collective-permute-start(f32[1,2,1,32]{3,2,1,0:T(1,128)S(1)} %broadcast.156), channel_id=1, source_target_pairs={{0,8},{8,16},{16,24},{24,32},{32,40},{40,48},{48,56},{56,64},{64,7... | collective-permute-start | bytes 776 | tf_op jit(solution)/shard_map/ppermute | solution.py:28
  11.2 6.7 %collective-permute-start.12 = (f32[1,4,1,64]{3,1,2,0:T(4,128)S(1)}, f32[1,4,1,64]{3,1,2,0:T(4,128)S(1)}, u32[]{:S(2)}, u32[]{:S(2)}) collective-permute-start(f32[1,4,1,64]{3,1,2,0:T(4,128)S(1)} %broadcast.150), channel_id=1, source_target_pairs={{0,8},{8,16},{16,24},{24,32},{32,40},{40,48},{48,56},{56,64},{64,7... | collective-permute-start | bytes 3080 | tf_op jit(solution)/shard_map/ppermute | solution.py:28
  20.7 6.3 %reshape.86 = f32[4,2,8,2,64,2]{5,4,3,2,1,0:T(8,128)} reshape(f32[8,16,128]{2,1,0:T(8,128)} %param.5) | data formatting | bytes 131072 | tf_op jit(solution)/shard_map/reshape | solution.py:64
  30.3 5.6 %reshape.85 = f32[4,2,8,2,64,2]{5,4,3,2,1,0:T(8,128)} reshape(f32[8,16,128]{2,1,0:T(8,128)S(1)} %copy-done) | data formatting | bytes 131072 | tf_op jit(solution)/shard_map/reshape | solution.py:64
  38.6 6.7 %collective-permute-start = (f32[1,8,1,128]{3,1,2,0:T(8,128)S(1)}, f32[1,8,1,128]{3,1,2,0:T(8,128)S(1)}, u32[]{:S(2)}, u32[]{:S(2)}) collective-permute-start(f32[1,8,1,128]{3,1,2,0:T(8,128)S(1)} %broadcast.147), channel_id=1, source_target_pairs={{0,8},{8,16},{16,24},{24,32},{32,40},{40,48},{48,56},{56,64},{64,7... | collective-permute-start | bytes 12296 | tf_op jit(solution)/shard_map/ppermute | solution.py:28
  50.6 5.2 collective-permute-start.20
  56.0 5.9 %collective-permute-start.2 = (f32[1,1,18,128]{3,2,1,0:T(8,128)S(1)}, f32[1,1,18,128]{3,2,1,0:T(8,128)S(1)}, u32[]{:S(2)}, u32[]{:S(2)}) collective-permute-start(f32[1,1,18,128]{3,2,1,0:T(8,128)S(1)} %get-tuple-element.39), channel_id=1, source_target_pairs={{0,1},{1,2},{2,3},{3,4},{4,5},{5,6},{6,7},{8,9},{9,10},{10,11},{11... | collective-permute-start | bytes 27656 | tf_op jit(solution)/shard_map/ppermute | solution.py:28
  72.6 5.6 %collective-permute-start.36 = (f32[1,2,1,32]{3,2,1,0:T(1,128)S(1)}, f32[1,2,1,32]{3,2,1,0:T(1,128)S(1)}, u32[]{:S(2)}, u32[]{:S(2)}) collective-permute-start(f32[1,2,1,32]{3,2,1,0:T(1,128)S(1)} %get-tuple-element.152), channel_id=1, source_target_pairs={{0,8},{8,16},{16,24},{24,32},{32,40},{40,48},{48,56},{56,64},{64,7... | collective-permute-start | bytes 776 | tf_op jit(solution)/shard_map/ppermute | solution.py:28
  88.0 5.3 collective-permute-start.30
  116.8 5.0 collective-permute-start.18
  127.0 5.6 %reshape.84 = f32[4,2,8,2,64,2]{5,4,3,2,1,0:T(8,128)} reshape(f32[8,16,128]{2,1,0:T(8,128)S(1)} %fusion.26) | data formatting | bytes 131072 | tf_op jit(solution)/shard_map/reshape | solution.py:64
  141.0 5.7 %collective-permute-done.25 = f32[1,4,1,64]{3,2,1,0:T(1,128)S(1)} collective-permute-done((f32[1,4,1,64]{3,2,1,0:T(1,128)S(1)}, f32[1,4,1,64]{3,2,1,0:T(1,128)S(1)}, u32[]{:S(2)}, u32[]{:S(2)}) %collective-permute-start.25) | collective-permute-done | bytes 1056 | tf_op jit(solution)/shard_map/ppermute | solution.py:29
  168.0 4.8 collective-permute-start.34
  183.9 4.3 collective-permute-done.41
  201.6 4.3 collective-permute-done.45
  219.4 4.3 collective-permute-done.49
  237.3 4.3 collective-permute-done.53
  255.1 4.3 collective-permute-done.57
  273.4 4.3 collective-permute-done.61
  291.3 4.3 collective-permute-done.65
  309.2 4.3 collective-permute-done.69
  327.0 4.3 collective-permute-done.73
  344.9 4.3 collective-permute-done.77
  357.5 5.6 %reshape.94 = f32[4,2,8,2,64,2]{5,4,3,2,1,0:T(8,128)} reshape(f32[8,16,128]{2,1,0:T(8,128)S(1)} %fusion.68) | data formatting | bytes 131072 | tf_op jit(solution)/shard_map/reshape | solution.py:64
  370.9 4.3 collective-permute-done.81
  388.7 4.3 collective-permute-done.85
  424.9 4.3 collective-permute-done.93
  460.6 4.3 collective-permute-done.101
  478.4 4.3 collective-permute-done.105
  496.7 4.3 collective-permute-done.109
  514.6 4.3 collective-permute-done.113
  532.4 4.3 collective-permute-done.117
  (395 shorter events, 386.0 us)
Async XLA Ops:
  0.6 37.9 %collective-permute-start.29 = (f32[1,2,1,32]{3,2,1,0:T(1,128)S(1)}, f32[1,2,1,32]{3,2,1,0:T(1,128)S(1)}, u32[]{:S(2)}, u32[]{:S(2)}) collective-permute-start(f32[1,2,1,32]{3,2,1,0:T(1,128)S(1)} %broadcast.156), channel_id=1, source_target_pairs={{8,0},{16,8},{24,16},{32,24},{40,32},{48,40},{56,48},{64,56},{72,6... | collective-permute-start | bytes 776 | tf_op jit(solution)/shard_map/ppermute | solution.py:29
  3.6 41.6 %collective-permute-start.28 = (f32[1,2,1,32]{3,2,1,0:T(1,128)S(1)}, f32[1,2,1,32]{3,2,1,0:T(1,128)S(1)}, u32[]{:S(2)}, u32[]{:S(2)}) collective-permute-start(f32[1,2,1,32]{3,2,1,0:T(1,128)S(1)} %broadcast.156), channel_id=1, source_target_pairs={{0,8},{8,16},{16,24},{24,32},{32,40},{40,48},{48,56},{56,64},{64,7... | collective-permute-start | bytes 776 | tf_op jit(solution)/shard_map/ppermute | solution.py:28
  9.3 84.1 %collective-permute-start.13 = (f32[1,4,1,64]{3,1,2,0:T(4,128)S(1)}, f32[1,4,1,64]{3,1,2,0:T(4,128)S(1)}, u32[]{:S(2)}, u32[]{:S(2)}) collective-permute-start(f32[1,4,1,64]{3,1,2,0:T(4,128)S(1)} %broadcast.150), channel_id=1, source_target_pairs={{8,0},{16,8},{24,16},{32,24},{40,32},{48,40},{56,48},{64,56},{72,6... | collective-permute-start | bytes 3080 | tf_op jit(solution)/shard_map/ppermute | solution.py:29
  11.2 84.1 %collective-permute-start.12 = (f32[1,4,1,64]{3,1,2,0:T(4,128)S(1)}, f32[1,4,1,64]{3,1,2,0:T(4,128)S(1)}, u32[]{:S(2)}, u32[]{:S(2)}) collective-permute-start(f32[1,4,1,64]{3,1,2,0:T(4,128)S(1)} %broadcast.150), channel_id=1, source_target_pairs={{0,8},{8,16},{16,24},{24,32},{32,40},{40,48},{48,56},{56,64},{64,7... | collective-permute-start | bytes 3080 | tf_op jit(solution)/shard_map/ppermute | solution.py:28
  17.9 29.3 %collective-permute-start.1 = (f32[1,8,1,128]{3,1,2,0:T(8,128)S(1)}, f32[1,8,1,128]{3,1,2,0:T(8,128)S(1)}, u32[]{:S(2)}, u32[]{:S(2)}) collective-permute-start(f32[1,8,1,128]{3,1,2,0:T(8,128)S(1)} %broadcast.147), channel_id=1, source_target_pairs={{8,0},{16,8},{24,16},{32,24},{40,32},{48,40},{56,48},{64,56},{72,6... | collective-permute-start | bytes 12296 | tf_op jit(solution)/shard_map/ppermute | solution.py:29
  38.6 12.0 %collective-permute-start = (f32[1,8,1,128]{3,1,2,0:T(8,128)S(1)}, f32[1,8,1,128]{3,1,2,0:T(8,128)S(1)}, u32[]{:S(2)}, u32[]{:S(2)}) collective-permute-start(f32[1,8,1,128]{3,1,2,0:T(8,128)S(1)} %broadcast.147), channel_id=1, source_target_pairs={{0,8},{8,16},{16,24},{24,32},{32,40},{40,48},{48,56},{56,64},{64,7... | collective-permute-start | bytes 12296 | tf_op jit(solution)/shard_map/ppermute | solution.py:28
  45.2 10.7 %collective-permute-start.4 = (f32[1,8,1,128]{3,1,2,0:T(8,128)S(1)}, f32[1,8,1,128]{3,1,2,0:T(8,128)S(1)}, u32[]{:S(2)}, u32[]{:S(2)}) collective-permute-start(f32[1,8,1,128]{3,1,2,0:T(8,128)S(1)} %get-tuple-element.81), channel_id=1, source_target_pairs={{0,8},{8,16},{16,24},{24,32},{32,40},{40,48},{48,56},{56,64},{64,7... | collective-permute-start | bytes 12296 | tf_op jit(solution)/shard_map/ppermute | solution.py:28
  47.2 14.7 %collective-permute-start.5 = (f32[1,8,1,128]{3,1,2,0:T(8,128)S(1)}, f32[1,8,1,128]{3,1,2,0:T(8,128)S(1)}, u32[]{:S(2)}, u32[]{:S(2)}) collective-permute-start(f32[1,8,1,128]{3,1,2,0:T(8,128)S(1)} %get-tuple-element.82), channel_id=1, source_target_pairs={{8,0},{16,8},{24,16},{32,24},{40,32},{48,40},{56,48},{64,56},{72,6... | collective-permute-start | bytes 12296 | tf_op jit(solution)/shard_map/ppermute | solution.py:29
  50.6 27.8 %collective-permute-start.20 = (f32[1,4,1,64]{3,2,1,0:T(1,128)S(1)}, f32[1,4,1,64]{3,2,1,0:T(1,128)S(1)}, u32[]{:S(2)}, u32[]{:S(2)}) collective-permute-start(f32[1,4,1,64]{3,2,1,0:T(1,128)S(1)} %get-tuple-element.122), channel_id=1, source_target_pairs={{0,8},{8,16},{16,24},{24,32},{32,40},{40,48},{48,56},{56,64},{64,7... | collective-permute-start | bytes 3080 | tf_op jit(solution)/shard_map/ppermute | solution.py:28
  56.0 7.9 %collective-permute-start.2 = (f32[1,1,18,128]{3,2,1,0:T(8,128)S(1)}, f32[1,1,18,128]{3,2,1,0:T(8,128)S(1)}, u32[]{:S(2)}, u32[]{:S(2)}) collective-permute-start(f32[1,1,18,128]{3,2,1,0:T(8,128)S(1)} %get-tuple-element.39), channel_id=1, source_target_pairs={{0,1},{1,2},{2,3},{3,4},{4,5},{5,6},{6,7},{8,9},{9,10},{10,11},{11... | collective-permute-start | bytes 27656 | tf_op jit(solution)/shard_map/ppermute | solution.py:28
  69.5 10.8 %collective-permute-start.21 = (f32[1,4,1,64]{3,2,1,0:T(1,128)S(1)}, f32[1,4,1,64]{3,2,1,0:T(1,128)S(1)}, u32[]{:S(2)}, u32[]{:S(2)}) collective-permute-start(f32[1,4,1,64]{3,2,1,0:T(1,128)S(1)} %get-tuple-element.123), channel_id=1, source_target_pairs={{8,0},{16,8},{24,16},{32,24},{40,32},{48,40},{56,48},{64,56},{72,6... | collective-permute-start | bytes 3080 | tf_op jit(solution)/shard_map/ppermute | solution.py:29
  72.6 66.4 %collective-permute-start.36 = (f32[1,2,1,32]{3,2,1,0:T(1,128)S(1)}, f32[1,2,1,32]{3,2,1,0:T(1,128)S(1)}, u32[]{:S(2)}, u32[]{:S(2)}) collective-permute-start(f32[1,2,1,32]{3,2,1,0:T(1,128)S(1)} %get-tuple-element.152), channel_id=1, source_target_pairs={{0,8},{8,16},{16,24},{24,32},{32,40},{40,48},{48,56},{56,64},{64,7... | collective-permute-start | bytes 776 | tf_op jit(solution)/shard_map/ppermute | solution.py:28
  80.3 7.7 %collective-permute-start.9 = (f32[1,8,1,128]{3,2,1,0:T(1,128)S(1)}, f32[1,8,1,128]{3,2,1,0:T(1,128)S(1)}, u32[]{:S(2)}, u32[]{:S(2)}) collective-permute-start(f32[1,8,1,128]{3,2,1,0:T(1,128)S(1)} %get-tuple-element.80), channel_id=1, source_target_pairs={{8,0},{16,8},{24,16},{32,24},{40,32},{48,40},{56,48},{64,56},{72,6... | collective-permute-start | bytes 12296 | tf_op jit(solution)/shard_map/ppermute | solution.py:29
  83.7 57.2 %collective-permute-start.37 = (f32[1,2,1,32]{3,2,1,0:T(1,128)S(1)}, f32[1,2,1,32]{3,2,1,0:T(1,128)S(1)}, u32[]{:S(2)}, u32[]{:S(2)}) collective-permute-start(f32[1,2,1,32]{3,2,1,0:T(1,128)S(1)} %get-tuple-element.153), channel_id=1, source_target_pairs={{8,0},{16,8},{24,16},{32,24},{40,32},{48,40},{56,48},{64,56},{72,6... | collective-permute-start | bytes 776 | tf_op jit(solution)/shard_map/ppermute | solution.py:29
  88.0 72.3 %collective-permute-start.30 = (f32[1,1,6,32]{3,2,1,0:T(8,128)S(1)}, f32[1,1,6,32]{3,2,1,0:T(8,128)S(1)}, u32[]{:S(2)}, u32[]{:S(2)}) collective-permute-start(f32[1,1,6,32]{3,2,1,0:T(8,128)S(1)} %get-tuple-element.138), channel_id=1, source_target_pairs={{0,1},{1,2},{2,3},{3,4},{4,5},{5,6},{6,7},{8,9},{9,10},{10,11},{11... | collective-permute-start | bytes 2312 | tf_op jit(solution)/shard_map/ppermute | solution.py:28
  107.1 7.7 %collective-permute-start.17 = (f32[1,8,1,128]{3,2,1,0:T(1,128)S(1)}, f32[1,8,1,128]{3,2,1,0:T(1,128)S(1)}, u32[]{:S(2)}, u32[]{:S(2)}) collective-permute-start(f32[1,8,1,128]{3,2,1,0:T(1,128)S(1)} %get-tuple-element.78), channel_id=1, source_target_pairs={{8,0},{16,8},{24,16},{32,24},{40,32},{48,40},{56,48},{64,56},{72,6... | collective-permute-start | bytes 12296 | tf_op jit(solution)/shard_map/ppermute | solution.py:29
  109.1 7.7 %collective-permute-start.14 = (f32[1,1,10,64]{3,1,2,0:T(1,128)S(1)}, f32[1,1,10,64]{3,1,2,0:T(1,128)S(1)}, u32[]{:S(2)}, u32[]{:S(2)}) collective-permute-start(f32[1,1,10,64]{3,1,2,0:T(1,128)S(1)} %get-tuple-element.101), channel_id=1, source_target_pairs={{0,1},{1,2},{2,3},{3,4},{4,5},{5,6},{6,7},{8,9},{9,10},{10,11},{11... | collective-permute-start | bytes 7688 | tf_op jit(solution)/shard_map/ppermute | solution.py:28
  123.8 39.8 %collective-permute-start.31 = (f32[1,1,6,32]{3,2,1,0:T(8,128)S(1)}, f32[1,1,6,32]{3,2,1,0:T(8,128)S(1)}, u32[]{:S(2)}, u32[]{:S(2)}) collective-permute-start(f32[1,1,6,32]{3,2,1,0:T(8,128)S(1)} %get-tuple-element.139), channel_id=1, source_target_pairs={{1,0},{2,1},{3,2},{4,3},{5,4},{6,5},{7,6},{9,8},{10,9},{11,10},{12... | collective-permute-start | bytes 2312 | tf_op jit(solution)/shard_map/ppermute | solution.py:29
  139.0 7.6 %collective-permute-start.25 = (f32[1,4,1,64]{3,2,1,0:T(1,128)S(1)}, f32[1,4,1,64]{3,2,1,0:T(1,128)S(1)}, u32[]{:S(2)}, u32[]{:S(2)}) collective-permute-start(f32[1,4,1,64]{3,2,1,0:T(1,128)S(1)} %get-tuple-element.121), channel_id=1, source_target_pairs={{8,0},{16,8},{24,16},{32,24},{40,32},{48,40},{56,48},{64,56},{72,6... | collective-permute-start | bytes 3080 | tf_op jit(solution)/shard_map/ppermute | solution.py:29
  146.7 9.6 %collective-permute-start.26 = (f32[1,1,10,64]{3,2,1,0:T(8,128)S(1)}, f32[1,1,10,64]{3,2,1,0:T(8,128)S(1)}, u32[]{:S(2)}, u32[]{:S(2)}) collective-permute-start(f32[1,1,10,64]{3,2,1,0:T(8,128)S(1)} %get-tuple-element.97), channel_id=1, source_target_pairs={{0,1},{1,2},{2,3},{3,4},{4,5},{5,6},{6,7},{8,9},{9,10},{10,11},{11... | collective-permute-start | bytes 7688 | tf_op jit(solution)/shard_map/ppermute | solution.py:28
  152.6 22.1 %collective-permute-start.38 = (f32[1,1,6,32]{3,2,1,0:T(8,128)S(1)}, f32[1,1,6,32]{3,2,1,0:T(8,128)S(1)}, u32[]{:S(2)}, u32[]{:S(2)}) collective-permute-start(f32[1,1,6,32]{3,2,1,0:T(8,128)S(1)} %get-tuple-element.136), channel_id=1, source_target_pairs={{0,1},{1,2},{2,3},{3,4},{4,5},{5,6},{6,7},{8,9},{9,10},{10,11},{11... | collective-permute-start | bytes 2312 | tf_op jit(solution)/shard_map/ppermute | solution.py:28
  156.3 18.4 %collective-permute-start.39 = (f32[1,1,6,32]{3,2,1,0:T(8,128)S(1)}, f32[1,1,6,32]{3,2,1,0:T(8,128)S(1)}, u32[]{:S(2)}, u32[]{:S(2)}) collective-permute-start(f32[1,1,6,32]{3,2,1,0:T(8,128)S(1)} %get-tuple-element.137), channel_id=1, source_target_pairs={{1,0},{2,1},{3,2},{4,3},{5,4},{6,5},{7,6},{9,8},{10,9},{11,10},{12... | collective-permute-start | bytes 2312 | tf_op jit(solution)/shard_map/ppermute | solution.py:29
  160.3 7.6 %collective-permute-start.33 = (f32[1,4,1,64]{3,2,1,0:T(1,128)S(1)}, f32[1,4,1,64]{3,2,1,0:T(1,128)S(1)}, u32[]{:S(2)}, u32[]{:S(2)}) collective-permute-start(f32[1,4,1,64]{3,2,1,0:T(1,128)S(1)} %get-tuple-element.119), channel_id=1, source_target_pairs={{8,0},{16,8},{24,16},{32,24},{40,32},{48,40},{56,48},{64,56},{72,6... | collective-permute-start | bytes 3080 | tf_op jit(solution)/shard_map/ppermute | solution.py:29
  234.0 7.6 %collective-permute-start.53 = (f32[1,4,1,64]{3,2,1,0:T(1,128)S(1)}, f32[1,4,1,64]{3,2,1,0:T(1,128)S(1)}, u32[]{:S(2)}, u32[]{:S(2)}) collective-permute-start(f32[1,4,1,64]{3,2,1,0:T(1,128)S(1)} %get-tuple-element.114), channel_id=1, source_target_pairs={{8,0},{16,8},{24,16},{32,24},{40,32},{48,40},{56,48},{64,56},{72,6... | collective-permute-start | bytes 3080 | tf_op jit(solution)/shard_map/ppermute | solution.py:29
  270.0 7.7 %collective-permute-start.61 = (f32[1,8,1,128]{3,2,1,0:T(1,128)S(1)}, f32[1,8,1,128]{3,2,1,0:T(1,128)S(1)}, u32[]{:S(2)}, u32[]{:S(2)}) collective-permute-start(f32[1,8,1,128]{3,2,1,0:T(1,128)S(1)} %get-tuple-element.76), channel_id=1, source_target_pairs={{8,0},{16,8},{24,16},{32,24},{40,32},{48,40},{56,48},{64,56},{72,6... | collective-permute-start | bytes 12296 | tf_op jit(solution)/shard_map/ppermute | solution.py:29
  287.9 7.7 %collective-permute-start.65 = (f32[1,8,1,128]{3,2,1,0:T(1,128)S(1)}, f32[1,8,1,128]{3,2,1,0:T(1,128)S(1)}, u32[]{:S(2)}, u32[]{:S(2)}) collective-permute-start(f32[1,8,1,128]{3,2,1,0:T(1,128)S(1)} %get-tuple-element.74), channel_id=1, source_target_pairs={{8,0},{16,8},{24,16},{32,24},{40,32},{48,40},{56,48},{64,56},{72,6... | collective-permute-start | bytes 12296 | tf_op jit(solution)/shard_map/ppermute | solution.py:29
  305.8 7.7 %collective-permute-start.69 = (f32[1,8,1,128]{3,2,1,0:T(1,128)S(1)}, f32[1,8,1,128]{3,2,1,0:T(1,128)S(1)}, u32[]{:S(2)}, u32[]{:S(2)}) collective-permute-start(f32[1,8,1,128]{3,2,1,0:T(1,128)S(1)} %get-tuple-element.72), channel_id=1, source_target_pairs={{8,0},{16,8},{24,16},{32,24},{40,32},{48,40},{56,48},{64,56},{72,6... | collective-permute-start | bytes 12296 | tf_op jit(solution)/shard_map/ppermute | solution.py:29
  323.7 7.7 %collective-permute-start.73 = (f32[1,8,1,128]{3,2,1,0:T(1,128)S(1)}, f32[1,8,1,128]{3,2,1,0:T(1,128)S(1)}, u32[]{:S(2)}, u32[]{:S(2)}) collective-permute-start(f32[1,8,1,128]{3,2,1,0:T(1,128)S(1)} %get-tuple-element.70), channel_id=1, source_target_pairs={{8,0},{16,8},{24,16},{32,24},{40,32},{48,40},{56,48},{64,56},{72,6... | collective-permute-start | bytes 12296 | tf_op jit(solution)/shard_map/ppermute | solution.py:29
  341.5 7.7 %collective-permute-start.77 = (f32[1,8,1,128]{3,2,1,0:T(1,128)S(1)}, f32[1,8,1,128]{3,2,1,0:T(1,128)S(1)}, u32[]{:S(2)}, u32[]{:S(2)}) collective-permute-start(f32[1,8,1,128]{3,2,1,0:T(1,128)S(1)} %get-tuple-element.68), channel_id=1, source_target_pairs={{8,0},{16,8},{24,16},{32,24},{40,32},{48,40},{56,48},{64,56},{72,6... | collective-permute-start | bytes 12296 | tf_op jit(solution)/shard_map/ppermute | solution.py:29
  493.3 7.7 %collective-permute-start.109 = (f32[1,8,1,128]{3,2,1,0:T(1,128)S(1)}, f32[1,8,1,128]{3,2,1,0:T(1,128)S(1)}, u32[]{:S(2)}, u32[]{:S(2)}) collective-permute-start(f32[1,8,1,128]{3,2,1,0:T(1,128)S(1)} %get-tuple-element.66), channel_id=1, source_target_pairs={{8,0},{16,8},{24,16},{32,24},{40,32},{48,40},{56,48},{64,56},{72,6... | collective-permute-start | bytes 12296 | tf_op jit(solution)/shard_map/ppermute | solution.py:29
  511.2 7.7 %collective-permute-start.113 = (f32[1,8,1,128]{3,2,1,0:T(1,128)S(1)}, f32[1,8,1,128]{3,2,1,0:T(1,128)S(1)}, u32[]{:S(2)}, u32[]{:S(2)}) collective-permute-start(f32[1,8,1,128]{3,2,1,0:T(1,128)S(1)} %get-tuple-element.64), channel_id=1, source_target_pairs={{8,0},{16,8},{24,16},{32,24},{40,32},{48,40},{56,48},{64,56},{72,6... | collective-permute-start | bytes 12296 | tf_op jit(solution)/shard_map/ppermute | solution.py:29
  529.1 7.7 %collective-permute-start.117 = (f32[1,8,1,128]{3,2,1,0:T(1,128)S(1)}, f32[1,8,1,128]{3,2,1,0:T(1,128)S(1)}, u32[]{:S(2)}, u32[]{:S(2)}) collective-permute-start(f32[1,8,1,128]{3,2,1,0:T(1,128)S(1)} %get-tuple-element.62), channel_id=1, source_target_pairs={{8,0},{16,8},{24,16},{32,24},{40,32},{48,40},{56,48},{64,56},{72,6... | collective-permute-start | bytes 12296 | tf_op jit(solution)/shard_map/ppermute | solution.py:29
  (91 other events, 565.6 us)
where the time goes:
time: 549 us; the launch traced here: 546 us
  starting transfers between devices  335 us (61%)
  waiting for transfers between devices  165 us (30%)
  local copies, waits for them, and re-layouts  27.7 us (5%)
  other arithmetic  15 us (3%)
    ppermute x60, starting transfers between devices, with_halo(): before = lax.ppermute(last, axis, up)  185 us
    ppermute x60, waiting for transfers between devices, with_halo(): after = lax.ppermute(leading, axis, down)  165 us
    ppermute x60, starting transfers between devices, with_halo(): after = lax.ppermute(leading, axis, down)  150 us
    reshape x6, local copies, waits for them, and re-layouts, restrict(): blocks = field.reshape(size_x // 2, 2, size_y // 2, 2, size_z // 2, 2)  24.1 us
  transfers between devices with their start and end apart: 120, of which 47 were waited for; matrix products, arithmetic and copies ran while one was open for 5% of the time, Pallas kernels for 0%

commit v1 on v0

v1 whole, which is shorter than its diff:
```python
import functools

import jax
import jax.numpy as jnp
from jax import lax
from jax.experimental import pallas as pl
from jax.experimental.pallas import tpu as pltpu
from jax.sharding import PartitionSpec as P

RELAX = 0.8
HALO = 9
ROWS = 16 + 2 * HALO
FX = 24
MROWS = 40
MX = 32
LROWS = 20
LX = 16
VMEM_LIMIT = 40 * 1024 * 1024

F32 = jnp.float32


def rows(lo, hi, body, step=2):
    count = (hi - lo) // step

    def several(i, carry):
        for t in range(step):
            body(lo + i * step + t)
        return carry

    if count > 0:
        lax.fori_loop(0, count, several, 0)
    for y in range(lo + count * step, hi):
        body(y)


def lanes(shape):
    return lax.broadcasted_iota(jnp.int32, shape, 1)


def planes(shape):
    return lax.broadcasted_iota(jnp.int32, shape, 0)


def up(value, axis, by):
    return pltpu.roll(value, value.shape[axis] - by, axis)


def down(value, axis, by):
    return pltpu.roll(value, by, axis)


class Level:
    def __init__(self, bx, by, bz, diag, inv, width):
        self.bx, self.by, self.bz, self.diag, self.inv, self.width = bx, by, bz, diag, inv, width

    def beside(self, u_ref, y):
        u = u_ref[y]
        bx = self.bx[y]
        bz = self.bz[y]
        acc = self.by[y] * u_ref[y + 1] + self.by[y - 1] * u_ref[y - 1]
        acc = acc + (bx * up(u, 0, 1) + down(bx * u, 0, 1))
        acc = acc + (bz * up(u, 1, self.width) + down(bz * u, 1, self.width))
        return u, acc

    def sweep(self, dst, src, rhs, lo, hi):
        def body(y):
            u, acc = self.beside(src, y)
            dst[y] = (1.0 - RELAX) * u + self.inv[y] * (rhs[y] + acc)

        rows(lo, hi, body)

    def residual(self, u_ref, rhs, y):
        u, acc = self.beside(u_ref, y)
        return rhs[y] - self.diag[y] * u + acc

    def build(self, conduct, absorb, lo, hi, spacing, closed, edges=None):
        shape = conduct.shape[1:]
        z, x = lanes(shape), planes(shape)
        half = 0.5 / spacing

        def body(y):
            c = conduct[y]
            xp, xm = up(c, 0, 1), down(c, 0, 1)
            if closed:
                xp = jnp.where(x == shape[0] - 1, 0.0, xp)
                xm = jnp.where(x == 0, 0.0, xm)
            else:
                left, right = edges
                xp = jnp.where(x == shape[0] - 1, right[y], xp)
                xm = jnp.where(x == 0, left[y], xm)
            zp = jnp.where(z >= shape[1] - self.width, 0.0, up(c, 1, self.width))
            zm = jnp.where(z < self.width, 0.0, down(c, 1, self.width))
            yp, ym = conduct[y + 1], conduct[y - 1]
            bx = (c + xp) * half
            self.bx[y] = jnp.where(x == shape[0] - 1, 0.0, bx) if closed else bx
            self.by[y] = (c + yp) * half
            self.bz[y] = jnp.where(z >= shape[1] - self.width, 0.0, (c + zp) * half)
            a = absorb[y]
            diag = a + (3.0 / spacing) * c + half * (((xp + xm) + (yp + ym)) + (zp + zm))
            if self.diag is not None:
                self.diag[y] = diag
            self.inv[y] = jnp.where(a > 0.0, RELAX / diag, 0.0)

        self.by[lo - 1] = (conduct[lo - 1] + conduct[lo]) * half
        rows(lo, hi, body)


def pair_lanes(t, width):
    first = (lanes(t.shape) // width) % 2 == 0
    return t + jnp.where(first, up(t, 1, width), down(t, 1, width))


def pair_planes(t):
    first = planes(t.shape) % 2 == 0
    return t + jnp.where(first, up(t, 0, 1), down(t, 0, 1))


def pack_rows(row_of):
    x, z = planes((8, 128)) % 2, lanes((8, 128)) % 2
    tiles = []
    for k in range(2):
        r = [row_of(4 * k + t) for t in range(4)]
        tiles.append(jnp.where(x == 0, jnp.where(z == 0, r[0], r[1]), jnp.where(z == 0, r[2], r[3])))
    return tiles


def restrict_own(fine_row):
    def row_of(j):
        t = fine_row(2 * j) + fine_row(2 * j + 1)
        return pair_planes(pair_lanes(t, 1)) * 0.125

    return pack_rows(row_of)


def restrict_low(fine_row, tmp, dst, lo, hi):
    def body(i):
        t = pair_lanes(fine_row(2 * i) + fine_row(2 * i + 1), 2)
        tmp[...] = t
        dst[i] = (tmp[pl.ds(0, LX, stride=2), :] + tmp[pl.ds(1, LX, stride=2), :]) * 0.125

    rows(lo, hi, body, 1)


def fine_kernel(scal, own, via_a, via_b, edge_l, edge_r,
                src, bx, by, bz, diag, inv, u2, pack,
                absorb, conduct, u1):
    even = scal[0] == 0

    def join(y):
        for arr, dst in ((0, src), (1, absorb), (2, conduct)):
            a, b = via_a[arr, y], via_b[arr, y]
            dst[y, 0:8, :] = jnp.where(even, b, a)
            dst[y, 8:16, :] = own[arr, y]
            dst[y, 16:24, :] = jnp.where(even, a, b)

    rows(0, ROWS, join)
    level = Level(bx, by, bz, diag, inv, 1)

    class Row:
        def __init__(self, ref):
            self.ref = ref

        def __getitem__(self, y):
            return self.ref[pl.ds(y, 1), :]

    level.build(conduct, absorb, 1, ROWS - 1, 1.0, False, (Row(edge_l), Row(edge_r)))

    def first(y):
        u1[y] = inv[y] * src[y]

    rows(1, ROWS - 1, first)
    zero = jnp.zeros((FX, 128), F32)
    for y in (0, 1, ROWS - 2, ROWS - 1):
        u2[y] = zero
    level.sweep(u2, u1, src, 2, ROWS - 2)
    tiles = restrict_own(lambda i: level.residual(u2, src, HALO + i)[8:16])
    tiles += restrict_own(lambda i: absorb[HALO + i, 8:16, :])
    tiles += restrict_own(lambda i: conduct[HALO + i, 8:16, :])
    for i, t in enumerate(tiles):
        pack[i] = t


def gather_rows(scal, mine, theirs, joined, arrays):
    pos, here, peers = scal[1], scal[2], scal[3]
    zero = jnp.zeros((8, 128), F32)
    for j in range(5):
        at = pos + (j - 2)
        there = here + (j - 2)
        inside = jnp.logical_and(there >= 0, there < peers)
        is_mine = jnp.logical_and(at >= 0, at < 4)

        def copy(source, start):
            for chip in range(4):
                for core in range(2):
                    for t in range(2 * arrays):
                        dev = 2 * chip + core
                        joined[j, t, 8 * dev:8 * dev + 8, :] = source[start * 4 + chip, core, t]

        @pl.when(jnp.logical_and(inside, is_mine))
        def _():
            copy(mine, at)

        @pl.when(jnp.logical_and(inside, jnp.logical_not(is_mine)))
        def _():
            copy(theirs, jnp.where(at < 0, at + 2, at - 4))

        @pl.when(jnp.logical_not(inside))
        def _():
            for dev in range(8):
                for t in range(2 * arrays):
                    joined[j, t, 8 * dev:8 * dev + 8, :] = zero


def unpack_rows(joined, tile, dst):
    z = lanes((MX, 128)) % 2 == 0

    def part(j):
        for k in range(2):
            for a in range(2):
                v = joined[j, tile + k, pl.ds(a, MX, stride=2), :]
                y = j * 8 + 4 * k + 2 * a
                dst[y] = jnp.where(z, v, down(v, 1, 1))
                dst[y + 1] = jnp.where(z, up(v, 1, 1), v)

    rows(0, 5, part, 1)


def coarse(mid, low, rhs, m1, m2, res, lrhs, l1, l2, tmp, shrink):
    k = shrink

    def first(y):
        m1[y] = mid.inv[y] * rhs[y]

    rows(2 + 2 * k, 38 - 2 * k, first)
    mid.sweep(m2, m1, rhs, 3 + 2 * k, 37 - 2 * k)
    restrict_low(lambda y: mid.residual(m2, rhs, y), tmp, lrhs, 2 + k, 18 - k)

    def low_first(y):
        l1[y] = low.inv[y] * lrhs[y]

    rows(2 + k, 18 - k, low_first)
    low.sweep(l2, l1, lrhs, 3 + k, 17 - k)
    low.sweep(l1, l2, lrhs, 4 + k, 16 - k)
    low.sweep(l2, l1, lrhs, 5 + k, 15 - k)

    def add(i):
        v = l2[i]
        for y in (2 * i, 2 * i + 1):
            for a in range(2):
                at = pl.ds(a, LX, stride=2)
                m2[y, at, :] = m2[y, at, :] + v

    rows(5 + k, 15 - k, add, 1)
    mid.sweep(m1, m2, rhs, 11 + 2 * k, 29 - 2 * k)
    mid.sweep(m2, m1, rhs, 12 + 2 * k, 28 - 2 * k)


def prolong_add(scal, m2, wide, u_ref, dst, lo, hi):
    begin = pl.multiple_of(scal[4] * 8, 8)
    zero = jnp.zeros((8, 128), F32)

    def body(m):
        v = m2[m]
        wide[m, 0:8, :] = zero
        wide[m, 72:80, :] = zero
        wide[m, pl.ds(8, MX, stride=2), :] = v
        wide[m, pl.ds(9, MX, stride=2), :] = v

    rows(lo, hi, body)

    def add(m):
        w = wide[m, pl.ds(begin, FX), :]
        for y in (2 * m - 32 + HALO, 2 * m - 31 + HALO):
            dst[y] = u_ref[y] + w

    rows(lo, hi, add)


def middle_kernel(scal, src, fbx, fby, fbz, fdiag, finv, u2, mine, theirs,
                  mbx, mby, mbz, mdiag, minv, lbx, lby, lbz, linv, u2_out, pack,
                  joined, rhs, absorb, conduct, m1, m2, lrhs, l1, l2, labsorb, lconduct, tmp, wide, fa, fb):
    fine = Level(fbx, fby, fbz, fdiag, finv, 1)
    mid = Level(mbx, mby, mbz, mdiag, minv, 2)
    low = Level(lbx, lby, lbz, None, linv, 4)
    gather_rows(scal, mine, theirs, joined, 3)
    unpack_rows(joined, 0, rhs)
    unpack_rows(joined, 2, absorb)
    unpack_rows(joined, 4, conduct)
    mid.build(conduct, absorb, 2, 38, 4.0, True)
    restrict_low(lambda y: absorb[y], tmp, labsorb, 1, 19)
    restrict_low(lambda y: conduct[y], tmp, lconduct, 1, 19)
    low.build(lconduct, labsorb, 2, 18, 16.0, True)
    coarse(mid, low, rhs, m1, m2, None, lrhs, l1, l2, tmp, 0)
    prolong_add(scal, m2, wide, u2, fa, 12, 28)
    fine.sweep(fb, fa, src, 3, ROWS - 3)
    fine.sweep(fa, fb, src, 4, ROWS - 4)
    fine.sweep(fb, fa, src, 5, ROWS - 5)
    zero = jnp.zeros((FX, 128), F32)
    for y in (*range(6), *range(ROWS - 6, ROWS)):
        u2_out[y] = zero
    fine.sweep(u2_out, fb, src, 6, ROWS - 6)
    tiles = restrict_own(lambda i: fine.residual(u2_out, src, HALO + i)[8:16])
    for i, t in enumerate(tiles):
        pack[i] = t


def last_kernel(scal, src, fbx, fby, fbz, fdiag, finv, u2, mine, theirs,
                mbx, mby, mbz, mdiag, minv, lbx, lby, lbz, linv,
                out, out_res,
                joined, rhs, m1, m2, lrhs, l1, l2, tmp, wide, fa, fb):
    fine = Level(fbx, fby, fbz, fdiag, finv, 1)
    mid = Level(mbx, mby, mbz, mdiag, minv, 2)
    low = Level(lbx, lby, lbz, None, linv, 4)
    gather_rows(scal, mine, theirs, joined, 1)
    unpack_rows(joined, 0, rhs)
    coarse(mid, low, rhs, m1, m2, None, lrhs, l1, l2, tmp, 1)
    prolong_add(scal, m2, wide, u2, fa, 14, 26)
    fine.sweep(fb, fa, src, 7, ROWS - 7)
    fine.sweep(fa, fb, src, 8, ROWS - 8)

    def finish(y):
        at = pl.ds(y, 8, stride=16)
        out[at, :] = fa[HALO + y, 8:16, :]
        out_res[at, :] = fine.residual(fa, src, HALO + y)[8:16]

    rows(0, 16, finish)


def call(kernel, outs, scratch, *args):
    return pl.pallas_call(
        kernel,
        out_shape=[jax.ShapeDtypeStruct(s, F32) for s in outs],
        in_specs=[pl.BlockSpec(memory_space=pltpu.SMEM)]
        + [pl.BlockSpec(memory_space=pltpu.VMEM)] * (len(args) - 1),
        out_specs=[pl.BlockSpec(memory_space=pltpu.VMEM)] * len(outs),
        scratch_shapes=[pltpu.VMEM(s, F32) for s in scratch],
        compiler_params=pltpu.CompilerParams(vmem_limit_bytes=VMEM_LIMIT),
    )(*args)


def other_core(array):
    return lax.ppermute(array, "dev", [(i, i ^ 1) for i in range(8)])


def spread(pack, core, pos, groups):
    partner = other_core(pack)
    first = core == 0
    pair = jnp.stack([jnp.where(first, pack, partner), jnp.where(first, partner, pack)])
    mine = lax.all_to_all(jnp.broadcast_to(pair, (16,) + pair.shape), ("grp", "dev"), 0, 0, axis_index_groups=groups)
    theirs = other_core(jnp.where(pos < 2, mine[8:], mine[:8]))
    return mine, theirs


def local(source, absorb, conduct):
    peers = lax.axis_size("grp")
    g, d = lax.axis_index("grp"), lax.axis_index("dev")
    core, chip = d % 2, d // 2
    pos = (g + 2 * core) % 4
    scal = jnp.stack([core, pos, g, jnp.int32(peers), d]).astype(jnp.int32)
    groups = [[(4 * b + p) % peers * 8 + 2 * c for p in range(4) for c in range(4)] for b in range(peers // 4)]
    groups += [[(4 * b + 2 + p) % peers * 8 + 2 * c + 1 for p in range(4) for c in range(4)] for b in range(peers // 4)]

    fine = jnp.stack([source, absorb, conduct]).transpose(0, 2, 1, 3)
    ahead = [(i, i + 1) for i in range(peers - 1)]
    back = [(j, i) for i, j in ahead]
    before = lax.ppermute(fine[:, 16 - HALO:], "grp", ahead)
    after = lax.ppermute(fine[:, :HALO], "grp", back)
    fine = jnp.concatenate([before, fine, after], axis=1)
    via_b = lax.ppermute(fine, "dev", [(1, 2), (2, 1), (3, 4), (4, 3), (5, 6), (6, 5)])
    ends = jnp.stack([fine[2, :, 0], fine[2, :, 7]])
    via_c = lax.ppermute(ends, "dev", [(0, 2), (2, 0), (1, 3), (3, 1), (4, 6), (6, 4), (5, 7), (7, 5)])
    via_d = lax.ppermute(ends, "dev", [(2, 4), (4, 2), (3, 5), (5, 3)])
    via_a = other_core(fine)
    edge_r = jnp.where(chip % 2 == 0, via_c[0], via_d[0])
    edge_l = jnp.where(chip % 2 == 0, via_d[1], via_c[1])

    block, wide_mid, wide_low = (ROWS, FX, 128), (MROWS, MX, 128), (LROWS, LX, 128)
    *state, pack = call(
        fine_kernel, [block] * 7 + [(6, 8, 128)], [block] * 3, scal, fine, via_a, via_b, edge_l, edge_r
    )
    mine, theirs = spread(pack, core, pos, groups)
    *coefs, u2, pack = call(
        middle_kernel,
        [wide_mid] * 5 + [wide_low] * 4 + [block, (2, 8, 128)],
        [(5, 6, 64, 128)] + [wide_mid] * 5 + [wide_low] * 5 + [(MX, 128), (MROWS, 80, 128), block, block],
        scal, *state, mine, theirs,
    )
    mine, theirs = spread(pack, core, pos, groups)
    out, res = call(
        last_kernel,
        [(128, 128), (128, 128)],
        [(5, 2, 64, 128)] + [wide_mid] * 3 + [wide_low] * 3 + [(MX, 128), (MROWS, 80, 128), block, block],
        scal, *state[:6], u2, mine, theirs, *coefs,
    )
    return out.reshape(8, 16, 128), res.reshape(8, 16, 128)


def solution(mesh):
    spec = P("dev", "grp", None)
    return jax.shard_map(local, mesh=mesh, in_specs=(spec,) * 3, out_specs=(spec,) * 2, check_vma=False)
```

time: 549 us -> 125 us (0.23)
  the two profiles are of different devices: /device:TPU:505 before, /device:TPU:1 now
where the time goes in v1:
time: 125 us; the launch traced here: 124 us
  starting transfers between devices  46 us (37%)
  Pallas kernels  34.3 us (27%)
  waiting for transfers between devices  23.6 us (19%)
  blocking collectives  16.1 us (13%)
  local copies, waits for them, and re-layouts  2.08 us (2%)
    pallas_call x3, Pallas kernels, call(): pl.pallas_call(kernel, out_shape=[jax.ShapeDtypeStruct(s, F32) for s in o...  34.3 us
    all_to_all x1, starting transfers between devices, spread(): lax.all_to_all(jnp.broadcast_to(pair, (16,) + pair.shape), ('grp', 'dev')...  17.5 us
    all_to_all x1, blocking collectives, spread(): lax.all_to_all(jnp.broadcast_to(pair, (16,) + pair.shape), ('grp', 'dev')...  16.1 us
    ppermute x5, starting transfers between devices, other_core(): return lax.ppermute(array, 'dev', [(i, i ^ 1) for i in range(8)])  14.8 us
    all_to_all x1, waiting for transfers between devices, spread(): lax.all_to_all(jnp.broadcast_to(pair, (16,) + pair.shape), ('grp', 'dev')...  11.7 us
    ppermute x1, starting transfers between devices, local(): lax.ppermute(fine, 'dev', [(1, 2), (2, 1), (3, 4), (4, 3), (5, 6), (6, 5)])  5.8 us
    ppermute x5, waiting for transfers between devices, other_core(): return lax.ppermute(array, 'dev', [(i, i ^ 1) for i in range(8)])  4.84 us
    ppermute x1, starting transfers between devices, local(): before = lax.ppermute(fine[:, 16 - HALO:], 'grp', ahead)  4.04 us
  transfers between devices with their start and end apart: 11, of which 8 were waited for; matrix products, arithmetic and copies ran while one was open for 0% of the time, Pallas kernels for 0%

profile of v1, /device:TPU:1, one launch (start us, length us, event | category | flops | bytes accessed | tf_op | source)
XLA Modules:
  0.0 124.1 jit_solution(13012528522072768557)
XLA Ops:
  0.6 0.9 maximum_bitcast_fusion
  1.6 4.0 %collective-permute-start = (f32[3,9,8,128]{3,1,2,0:T(8,128)S(1)}, f32[3,9,8,128]{3,1,2,0:T(8,128)S(1)}, u32[]{:S(2)}, u32[]{:S(2)}) collective-permute-start(f32[3,9,8,128]{3,1,2,0:T(8,128)S(1)} %get-tuple-element.46), channel_id=1, source_target_pairs={{0,8},{8,16},{16,24},{24,32},{32,40},{40,48},{48,56},{56,64},{64,7... | collective-permute-start | bytes 331784 | tf_op jit(solution)/shard_map/ppermute | solution.py:367
  5.6 1.3 %collective-permute-start.1 = (f32[3,9,8,128]{3,1,2,0:T(8,128)S(1)}, f32[3,9,8,128]{3,1,2,0:T(8,128)S(1)}, u32[]{:S(2)}, u32[]{:S(2)}) collective-permute-start(f32[3,9,8,128]{3,1,2,0:T(8,128)S(1)} %get-tuple-element.47), channel_id=1, source_target_pairs={{8,0},{16,8},{24,16},{32,24},{40,32},{48,40},{56,48},{64,56},{72,6... | collective-permute-start | bytes 331784 | tf_op jit(solution)/shard_map/ppermute | solution.py:368
  6.9 1.3 %collective-permute-done = f32[3,9,8,128]{3,1,2,0:T(8,128)S(1)} collective-permute-done((f32[3,9,8,128]{3,1,2,0:T(8,128)S(1)}, f32[3,9,8,128]{3,1,2,0:T(8,128)S(1)}, u32[]{:S(2)}, u32[]{:S(2)}) %collective-permute-start) | collective-permute-done | bytes 110624 | tf_op jit(solution)/shard_map/ppermute | solution.py:367
  8.2 3.8 %collective-permute-done.1 = f32[3,9,8,128]{3,1,2,0:T(8,128)S(1)} collective-permute-done((f32[3,9,8,128]{3,1,2,0:T(8,128)S(1)}, f32[3,9,8,128]{3,1,2,0:T(8,128)S(1)}, u32[]{:S(2)}, u32[]{:S(2)}) %collective-permute-start.1) | collective-permute-done | bytes 110624 | tf_op jit(solution)/shard_map/ppermute | solution.py:368
  12.1 0.1 pad_maximum_fusion
  12.1 5.8 %collective-permute-start.3 = (f32[3,34,8,128]{3,1,2,0:T(8,128)S(1)}, f32[3,34,8,128]{3,1,2,0:T(8,128)S(1)}, u32[]{:S(2)}, u32[]{:S(2)}) collective-permute-start(f32[3,34,8,128]{3,1,2,0:T(8,128)S(1)} %pad_maximum_fusion), channel_id=1, source_target_pairs={{1,2},{2,1},{3,4},{4,3},{5,6},{6,5},{9,10},{10,9},{11,12},{12,11},... | collective-permute-start | bytes 1253384 | tf_op jit(solution)/shard_map/ppermute | solution.py:370
  17.9 5.7 %collective-permute-start.2 = (f32[3,34,8,128]{3,1,2,0:T(8,128)S(1)}, f32[3,34,8,128]{3,1,2,0:T(8,128)S(1)}, u32[]{:S(2)}, u32[]{:S(2)}) collective-permute-start(f32[3,34,8,128]{3,1,2,0:T(8,128)S(1)} %pad_maximum_fusion), channel_id=1, source_target_pairs={{0,1},{1,0},{2,3},{3,2},{4,5},{5,4},{6,7},{7,6},{8,9},{9,8},{10,11... | collective-permute-start | bytes 1253384 | tf_op jit(solution)/shard_map/ppermute | solution.py:343
  23.7 1.9 %collective-permute-start.5 = (f32[2,34,128]{2,1,0:T(8,128)S(1)}, f32[2,34,128]{2,1,0:T(8,128)S(1)}, u32[]{:S(2)}, u32[]{:S(2)}) collective-permute-start(f32[2,34,128]{2,1,0:T(8,128)S(1)} %pad_maximum_fusion.2), channel_id=1, source_target_pairs={{0,2},{2,0},{1,3},{3,1},{4,6},{6,4},{5,7},{7,5},{8,10},{10,8},{9,1... | collective-permute-start | bytes 104456 | tf_op jit(solution)/shard_map/ppermute | solution.py:372
  25.6 0.7 collective-permute-start.4
  26.3 0.1 stack.52.scal
  26.4 0.1 copy.5.own
  26.5 1.9 %collective-permute-done.5 = f32[2,34,128]{2,1,0:T(8,128)S(1)} collective-permute-done((f32[2,34,128]{2,1,0:T(8,128)S(1)}, f32[2,34,128]{2,1,0:T(8,128)S(1)}, u32[]{:S(2)}, u32[]{:S(2)}) %collective-permute-start.5) | collective-permute-done | bytes 34848 | tf_op jit(solution)/shard_map/ppermute | solution.py:372
  28.4 0.0 collective-permute-done.4
  28.4 0.1 copy.7.via_b
  28.5 0.1 copy.6.via_a
  28.6 3.8 %shard_map.50 = (f32[34,24,128]{2,1,0:T(8,128)S(1)}, f32[34,24,128]{2,1,0:T(8,128)S(1)}, f32[34,24,128]{2,1,0:T(8,128)S(1)}, f32[34,24,128]{2,1,0:T(8,128)S(1)},...) custom-call(s32[5]{0:T(128)S(1)} %stack.52.scal, ...), custom_call_target="tpu_custom_call" | custom-call | tf_op jit(solution)/shard_map/pallas_call | solution.py:331
  32.4 0.8 copy-done
  33.2 3.1 %collective-permute-start.6 = (f32[6,8,128]{2,1,0:T(8,128)S(1)}, f32[6,8,128]{2,1,0:T(8,128)S(1)}, u32[]{:S(2)}, u32[]{:S(2)}) collective-permute-start(f32[6,8,128]{2,1,0:T(8,128)S(1)} %get-tuple-element.30), channel_id=1, source_target_pairs={{0,1},{1,0},{2,3},{3,2},{4,5},{5,4},{6,7},{7,6},{8,9},{9,8},{10,11... | collective-permute-start | bytes 73736 | tf_op jit(solution)/shard_map/ppermute | solution.py:343
  36.3 0.8 collective-permute-done.6
  37.1 1.0 broadcast_in_dim.6
  38.1 17.5 %all-to-all-start = ((f32[16,2,6,8,128]{4,3,2,1,0:T(8,128)}), f32[16,2,6,8,128]{4,3,2,1,0:T(8,128)S(1)}, u32[]{:S(2)}, u32[]{:S(2)}) async-start(f32[16,2,6,8,128]{4,3,2,1,0:T(8,128)} %broadcast_in_dim.6), calls=%async_computation | async-start | bytes 1572864 | tf_op jit(solution)/shard_map/all_to_all | solution.py:350
  55.6 11.7 %all-to-all-done.mine = f32[16,2,6,8,128]{4,3,2,1,0:T(8,128)S(1)} async-done(((f32[16,2,6,8,128]{4,3,2,1,0:T(8,128)}), f32[16,2,6,8,128]{4,3,2,1,0:T(8,128)S(1)}, u32[]{:S(2)}, u32[]{:S(2)}) %all-to-all-start) | async-done | bytes 786464 | tf_op jit(solution)/shard_map/all_to_all | solution.py:350
  67.3 2.1 %collective-permute-start.7 = (f32[8,2,6,8,128]{4,3,2,1,0:T(8,128)S(1)}, f32[8,2,6,8,128]{4,3,2,1,0:T(8,128)S(1)}, u32[]{:S(2)}, u32[]{:S(2)}) collective-permute-start(f32[8,2,6,8,128]{4,3,2,1,0:T(8,128)S(1)} %slice_select_fusion), channel_id=1, source_target_pairs={{0,1},{1,0},{2,3},{3,2},{4,5},{5,4},{6,7},{7,6},{8,9},{9,8},{10,11... | collective-permute-start | bytes 1179656 | tf_op jit(solution)/shard_map/ppermute | solution.py:343
  69.4 1.7 %collective-permute-done.7.theirs = f32[8,2,6,8,128]{4,3,2,1,0:T(8,128)S(1)} collective-permute-done((f32[8,2,6,8,128]{4,3,2,1,0:T(8,128)S(1)}, f32[8,2,6,8,128]{4,3,2,1,0:T(8,128)S(1)}, u32[]{:S(2)}, u32[]{:S(2)}) %collective-permute-start.7) | collective-permute-done | bytes 393248 | tf_op jit(solution)/shard_map/ppermute | solution.py:343
  71.1 20.0 %shard_map.51 = (f32[40,32,128]{2,1,0:T(8,128)S(1)}, f32[40,32,128]{2,1,0:T(8,128)S(1)}, f32[40,32,128]{2,1,0:T(8,128)S(1)}, f32[40,32,128]{2,1,0:T(8,128)S(1)},...) custom-call(s32[5]{0:T(128)S(1)} %stack.52.scal, ...), custom_call_target="tpu_custom_call" | custom-call | tf_op jit(solution)/shard_map/pallas_call | solution.py:331
  91.1 2.0 %collective-permute-start.8 = (f32[2,8,128]{2,1,0:T(8,128)S(1)}, f32[2,8,128]{2,1,0:T(8,128)S(1)}, u32[]{:S(2)}, u32[]{:S(2)}) collective-permute-start(f32[2,8,128]{2,1,0:T(8,128)S(1)} %get-tuple-element.32), channel_id=1, source_target_pairs={{0,1},{1,0},{2,3},{3,2},{4,5},{5,4},{6,7},{7,6},{8,9},{9,8},{10,11... | collective-permute-start | bytes 24584 | tf_op jit(solution)/shard_map/ppermute | solution.py:343
  93.1 1.0 collective-permute-done.8
  94.2 16.1 %all_to_all.10.mine = f32[16,2,2,8,128]{4,3,2,1,0:T(8,128)S(1)} all-to-all(f32[16,2,2,8,128]{4,3,2,1,0:T(8,128)S(1)} %broadcast_in_dim.7), channel_id=1, replica_groups={{0,2,4,6,8,10,12,14,16,18,20,22,24,26,28,30},{32,34,36,38,40,42,44,46,4..., dimensions={0} | all-to-all | bytes 524288 | tf_op jit(solution)/shard_map/all_to_all | solution.py:350
  110.3 1.9 %collective-permute-start.9 = (f32[8,2,2,8,128]{4,3,2,1,0:T(8,128)S(1)}, f32[8,2,2,8,128]{4,3,2,1,0:T(8,128)S(1)}, u32[]{:S(2)}, u32[]{:S(2)}) collective-permute-start(f32[8,2,2,8,128]{4,3,2,1,0:T(8,128)S(1)} %slice_select_fusion.1), channel_id=1, source_target_pairs={{0,1},{1,0},{2,3},{3,2},{4,5},{5,4},{6,7},{7,6},{8,9},{9,8},{10,11... | collective-permute-start | bytes 393224 | tf_op jit(solution)/shard_map/ppermute | solution.py:343
  112.3 1.3 %collective-permute-done.9.theirs = f32[8,2,2,8,128]{4,3,2,1,0:T(8,128)S(1)} collective-permute-done((f32[8,2,2,8,128]{4,3,2,1,0:T(8,128)S(1)}, f32[8,2,2,8,128]{4,3,2,1,0:T(8,128)S(1)}, u32[]{:S(2)}, u32[]{:S(2)}) %collective-permute-start.9) | collective-permute-done | bytes 131104 | tf_op jit(solution)/shard_map/ppermute | solution.py:343
  113.6 10.5 %shard_map.52 = (f32[128,128]{1,0:T(8,128)}, f32[128,128]{1,0:T(8,128)}) custom-call(s32[5]{0:T(128)S(1)} %stack.52.scal, f32[34,24,128]{2,1,0:T(8,128)S(1)} %get-tuple-element.23.src, f32[34,24,128]{2,1,0:T(8,128)S(1)} %get-tuple-element.24.fbx, f32[34,24,128]{2,1,0:T(8,128)S(1)} %get-tuple-element.25.fby, f32[34,24,128]{2,1,0:T(8,128)S(1)} %get-tuple-element.26.fbz, ...), custom_call_target="tpu_custom_call" | custom-call | tf_op jit(solution)/shard_map/pallas_call | solution.py:331
  (16 shorter events, 0.2 us)
Async XLA Ops:
  1.6 6.6 %collective-permute-start = (f32[3,9,8,128]{3,1,2,0:T(8,128)S(1)}, f32[3,9,8,128]{3,1,2,0:T(8,128)S(1)}, u32[]{:S(2)}, u32[]{:S(2)}) collective-permute-start(f32[3,9,8,128]{3,1,2,0:T(8,128)S(1)} %get-tuple-element.46), channel_id=1, source_target_pairs={{0,8},{8,16},{16,24},{24,32},{32,40},{40,48},{48,56},{56,64},{64,7... | collective-permute-start | bytes 331784 | tf_op jit(solution)/shard_map/ppermute | solution.py:367
  5.6 6.4 %collective-permute-start.1 = (f32[3,9,8,128]{3,1,2,0:T(8,128)S(1)}, f32[3,9,8,128]{3,1,2,0:T(8,128)S(1)}, u32[]{:S(2)}, u32[]{:S(2)}) collective-permute-start(f32[3,9,8,128]{3,1,2,0:T(8,128)S(1)} %get-tuple-element.47), channel_id=1, source_target_pairs={{8,0},{16,8},{24,16},{32,24},{40,32},{48,40},{56,48},{64,56},{72,6... | collective-permute-start | bytes 331784 | tf_op jit(solution)/shard_map/ppermute | solution.py:368
  12.1 16.3 %collective-permute-start.3 = (f32[3,34,8,128]{3,1,2,0:T(8,128)S(1)}, f32[3,34,8,128]{3,1,2,0:T(8,128)S(1)}, u32[]{:S(2)}, u32[]{:S(2)}) collective-permute-start(f32[3,34,8,128]{3,1,2,0:T(8,128)S(1)} %pad_maximum_fusion), channel_id=1, source_target_pairs={{1,2},{2,1},{3,4},{4,3},{5,6},{6,5},{9,10},{10,9},{11,12},{12,11},... | collective-permute-start | bytes 1253384 | tf_op jit(solution)/shard_map/ppermute | solution.py:370
  17.9 10.6 %collective-permute-start.2 = (f32[3,34,8,128]{3,1,2,0:T(8,128)S(1)}, f32[3,34,8,128]{3,1,2,0:T(8,128)S(1)}, u32[]{:S(2)}, u32[]{:S(2)}) collective-permute-start(f32[3,34,8,128]{3,1,2,0:T(8,128)S(1)} %pad_maximum_fusion), channel_id=1, source_target_pairs={{0,1},{1,0},{2,3},{3,2},{4,5},{5,4},{6,7},{7,6},{8,9},{9,8},{10,11... | collective-permute-start | bytes 1253384 | tf_op jit(solution)/shard_map/ppermute | solution.py:343
  23.7 4.7 %collective-permute-start.5 = (f32[2,34,128]{2,1,0:T(8,128)S(1)}, f32[2,34,128]{2,1,0:T(8,128)S(1)}, u32[]{:S(2)}, u32[]{:S(2)}) collective-permute-start(f32[2,34,128]{2,1,0:T(8,128)S(1)} %pad_maximum_fusion.2), channel_id=1, source_target_pairs={{0,2},{2,0},{1,3},{3,1},{4,6},{6,4},{5,7},{7,5},{8,10},{10,8},{9,1... | collective-permute-start | bytes 104456 | tf_op jit(solution)/shard_map/ppermute | solution.py:372
  25.6 2.8 %collective-permute-start.4 = (f32[2,34,128]{2,1,0:T(8,128)S(1)}, f32[2,34,128]{2,1,0:T(8,128)S(1)}, u32[]{:S(2)}, u32[]{:S(2)}) collective-permute-start(f32[2,34,128]{2,1,0:T(8,128)S(1)} %pad_maximum_fusion.2), channel_id=1, source_target_pairs={{2,4},{4,2},{3,5},{5,3},{10,12},{12,10},{11,13},{13,11},{18,20},{2... | collective-permute-start | bytes 104456 | tf_op jit(solution)/shard_map/ppermute | solution.py:373
  32.4 0.8 copy-start
  33.2 3.9 %collective-permute-start.6 = (f32[6,8,128]{2,1,0:T(8,128)S(1)}, f32[6,8,128]{2,1,0:T(8,128)S(1)}, u32[]{:S(2)}, u32[]{:S(2)}) collective-permute-start(f32[6,8,128]{2,1,0:T(8,128)S(1)} %get-tuple-element.30), channel_id=1, source_target_pairs={{0,1},{1,0},{2,3},{3,2},{4,5},{5,4},{6,7},{7,6},{8,9},{9,8},{10,11... | collective-permute-start | bytes 73736 | tf_op jit(solution)/shard_map/ppermute | solution.py:343
  38.1 29.2 %all-to-all-start = ((f32[16,2,6,8,128]{4,3,2,1,0:T(8,128)}), f32[16,2,6,8,128]{4,3,2,1,0:T(8,128)S(1)}, u32[]{:S(2)}, u32[]{:S(2)}) async-start(f32[16,2,6,8,128]{4,3,2,1,0:T(8,128)} %broadcast_in_dim.6), calls=%async_computation | async-start | bytes 1572864 | tf_op jit(solution)/shard_map/all_to_all | solution.py:350
  67.3 3.8 %copy-start.1 = (f32[34,24,128]{2,1,0:T(8,128)S(1)}, f32[34,24,128]{2,1,0:T(8,128)}, u32[]{:S(2)}) copy-start(f32[34,24,128]{2,1,0:T(8,128)} %copy-done) | copy-start | bytes 1253380
  67.3 3.7 %collective-permute-start.7 = (f32[8,2,6,8,128]{4,3,2,1,0:T(8,128)S(1)}, f32[8,2,6,8,128]{4,3,2,1,0:T(8,128)S(1)}, u32[]{:S(2)}, u32[]{:S(2)}) collective-permute-start(f32[8,2,6,8,128]{4,3,2,1,0:T(8,128)S(1)} %slice_select_fusion), channel_id=1, source_target_pairs={{0,1},{1,0},{2,3},{3,2},{4,5},{5,4},{6,7},{7,6},{8,9},{9,8},{10,11... | collective-permute-start | bytes 1179656 | tf_op jit(solution)/shard_map/ppermute | solution.py:343
  91.1 3.1 %collective-permute-start.8 = (f32[2,8,128]{2,1,0:T(8,128)S(1)}, f32[2,8,128]{2,1,0:T(8,128)S(1)}, u32[]{:S(2)}, u32[]{:S(2)}) collective-permute-start(f32[2,8,128]{2,1,0:T(8,128)S(1)} %get-tuple-element.32), channel_id=1, source_target_pairs={{0,1},{1,0},{2,3},{3,2},{4,5},{5,4},{6,7},{7,6},{8,9},{9,8},{10,11... | collective-permute-start | bytes 24584 | tf_op jit(solution)/shard_map/ppermute | solution.py:343
  110.3 3.2 %collective-permute-start.9 = (f32[8,2,2,8,128]{4,3,2,1,0:T(8,128)S(1)}, f32[8,2,2,8,128]{4,3,2,1,0:T(8,128)S(1)}, u32[]{:S(2)}, u32[]{:S(2)}) collective-permute-start(f32[8,2,2,8,128]{4,3,2,1,0:T(8,128)S(1)} %slice_select_fusion.1), channel_id=1, source_target_pairs={{0,1},{1,0},{2,3},{3,2},{4,5},{5,4},{6,7},{7,6},{8,9},{9,8},{10,11... | collective-permute-start | bytes 393224 | tf_op jit(solution)/shard_map/ppermute | solution.py:343

commit v2 on v1

v2 whole, which is shorter than its diff:
```python
import functools

import jax
import jax.numpy as jnp
from jax import lax
from jax.experimental import pallas as pl
from jax.experimental.pallas import tpu as pltpu
from jax.sharding import PartitionSpec as P

RELAX = 0.8
HALO = 9
ROWS = 16 + 2 * HALO
FX = 24
MROWS = 40
MX = 32
LROWS = 20
LX = 16
VMEM_LIMIT = 40 * 1024 * 1024

F32 = jnp.float32


def rows(lo, hi, body):
    body(lo, hi - lo)


def lanes(shape):
    return lax.broadcasted_iota(jnp.int32, shape, 1)


def planes(shape):
    return lax.broadcasted_iota(jnp.int32, shape, 0)


def up(value, axis, by):
    return pltpu.roll(value, value.shape[axis] - by, axis)


def down(value, axis, by):
    return pltpu.roll(value, by, axis)


class Level:
    def __init__(self, bx, by, bz, diag, inv, width):
        self.bx, self.by, self.bz, self.diag, self.inv, self.width = bx, by, bz, diag, inv, width

    def beside(self, u_ref, y, n):
        u = [u_ref[y - 1 + t] for t in range(n + 2)]
        by = [self.by[y - 1 + t] for t in range(n + 1)]
        flow = [by[t] * u[t + 1] for t in range(n + 1)]
        acc = []
        for t in range(n):
            here, bx, bz = u[t + 1], self.bx[y + t], self.bz[y + t]
            x = bx * up(here, 0, 1) + down(bx * here, 0, 1)
            z = bz * up(here, 1, self.width) + down(bz * here, 1, self.width)
            acc.append((by[t] * u[t] + by[t + 1] * u[t + 2]) + (x + z))
        return u[1:-1], acc

    def sweep(self, dst, src, rhs, lo, hi):
        def body(y, n):
            u, acc = self.beside(src, y, n)
            new = [(1.0 - RELAX) * u[t] + self.inv[y + t] * (rhs[y + t] + acc[t]) for t in range(n)]
            for t in range(n):
                dst[y + t] = new[t]

        rows(lo, hi, body)

    def residual(self, u_ref, rhs, y, n):
        u, acc = self.beside(u_ref, y, n)
        return [rhs[y + t] - self.diag[y + t] * u[t] + acc[t] for t in range(n)]

    def build(self, conduct, absorb, lo, hi, spacing, closed):
        shape = conduct.shape[1:]
        z, x = lanes(shape), planes(shape)
        half = 0.5 / spacing

        def body(y, n):
            c = [conduct[y - 1 + t] for t in range(n + 2)]
            done = []
            for t in range(n):
                here = c[t + 1]
                xp, xm = up(here, 0, 1), down(here, 0, 1)
                if closed:
                    xp = jnp.where(x == shape[0] - 1, 0.0, xp)
                    xm = jnp.where(x == 0, 0.0, xm)
                zp = jnp.where(z >= shape[1] - self.width, 0.0, up(here, 1, self.width))
                zm = jnp.where(z < self.width, 0.0, down(here, 1, self.width))
                bx = (here + xp) * half
                if closed:
                    bx = jnp.where(x == shape[0] - 1, 0.0, bx)
                by = (here + c[t + 2]) * half
                bz = jnp.where(z >= shape[1] - self.width, 0.0, (here + zp) * half)
                a = absorb[y + t]
                diag = a + (3.0 / spacing) * here + half * (((xp + xm) + (c[t] + c[t + 2])) + (zp + zm))
                done.append((bx, by, bz, diag, jnp.where(a > 0.0, RELAX / diag, 0.0)))
            for t in range(n):
                for ref, value in zip((self.bx, self.by, self.bz, self.diag, self.inv), done[t]):
                    if ref is not None:
                        ref[y + t] = value

        self.by[lo - 1] = (conduct[lo - 1] + conduct[lo]) * half
        rows(lo, hi, body)


def pair_lanes(t, width):
    first = (lanes(t.shape) // width) % 2 == 0
    return t + jnp.where(first, up(t, 1, width), down(t, 1, width))


def pair_planes(t):
    first = planes(t.shape) % 2 == 0
    return t + jnp.where(first, up(t, 0, 1), down(t, 0, 1))


def pack_rows(row_of):
    x, z = planes((8, 128)) % 2, lanes((8, 128)) % 2
    tiles = []
    for k in range(2):
        r = [row_of(4 * k + t) for t in range(4)]
        tiles.append(jnp.where(x == 0, jnp.where(z == 0, r[0], r[1]), jnp.where(z == 0, r[2], r[3])))
    return tiles


def restrict_own(r):
    def row_of(j):
        return pair_planes(pair_lanes(r[2 * j] + r[2 * j + 1], 1)) * 0.125

    return pack_rows(row_of)


def restrict_low(fine_rows, tmp, dst, lo, hi):
    def body(i, n):
        r = fine_rows(2 * i, 2 * n)
        for t in range(n):
            tmp[t] = pair_lanes(r[2 * t] + r[2 * t + 1], 2)
        for t in range(n):
            dst[i + t] = (tmp[t, pl.ds(0, LX, stride=2), :] + tmp[t, pl.ds(1, LX, stride=2), :]) * 0.125

    rows(lo, hi, body)


def scale(dst, factor, src, lo, hi):
    def body(y, n):
        new = [factor[y + t] * src[y + t] for t in range(n)]
        for t in range(n):
            dst[y + t] = new[t]

    rows(lo, hi, body)


def fine_kernel(scal, own, via_a, via_b,
                src, bx, by, bz, diag, inv, u1, pack, ends,
                absorb, conduct, u2):
    even = scal[0] == 0

    def join(y, n):
        for t in range(n):
            for arr, dst in ((0, src), (1, absorb), (2, conduct)):
                a, b = via_a[arr, y + t], via_b[arr, y + t]
                dst[y + t, 0:8, :] = jnp.where(even, b, a)
                dst[y + t, 8:16, :] = own[arr, y + t]
                dst[y + t, 16:24, :] = jnp.where(even, a, b)

    rows(0, ROWS, join)
    level = Level(bx, by, bz, diag, inv, 1)
    level.build(conduct, absorb, 1, ROWS - 1, 1.0, False)
    scale(u1, inv, src, 1, ROWS - 1)
    for y in range(1, ROWS - 1):
        for i, x in enumerate((8, 15)):
            ends[i, y - 1:y, :] = u1[y, x:x + 1, :]
    level.sweep(u2, u1, src, HALO - 1, ROWS - HALO + 1)
    tiles = restrict_own([r[8:16] for r in level.residual(u2, src, HALO, 16)])
    tiles += restrict_own([absorb[HALO + i, 8:16, :] for i in range(16)])
    tiles += restrict_own([conduct[HALO + i, 8:16, :] for i in range(16)])
    for i, t in enumerate(tiles):
        pack[i] = t


def gather_rows(scal, here, near, swapped, joined, arrays):
    even = scal[0] == 0

    def copy(j, source):
        for t in range(2 * arrays):
            for dev in range(8):
                joined[j, t, 8 * dev:8 * dev + 8, :] = source[dev, t]

    copy(2, here)
    for i in range(2):
        after, before = 3 + i, 1 - i

        @pl.when(even)
        def _():
            copy(after, near.at[i])
            copy(before, swapped.at[i])

        @pl.when(jnp.logical_not(even))
        def _():
            copy(after, swapped.at[i])
            copy(before, near.at[i])


def unpack_rows(joined, tile, dst):
    z = lanes((MX, 128)) % 2 == 0

    for j in range(5):
        for k in range(2):
            for a in range(2):
                v = joined[j, tile + k, pl.ds(a, MX, stride=2), :]
                y = j * 8 + 4 * k + 2 * a
                dst[y] = jnp.where(z, v, down(v, 1, 1))
                dst[y + 1] = jnp.where(z, up(v, 1, 1), v)


def coarse(mid, low, rhs, m1, m2, lrhs, l1, l2, tmp, k):
    scale(m1, mid.inv, rhs, 2 + 2 * k, 38 - 2 * k)
    mid.sweep(m2, m1, rhs, 3 + 2 * k, 37 - 2 * k)
    restrict_low(functools.partial(mid.residual, m2, rhs), tmp, lrhs, 2 + k, 18 - k)
    scale(l1, low.inv, lrhs, 2 + k, 18 - k)
    low.sweep(l2, l1, lrhs, 3 + k, 17 - k)
    low.sweep(l1, l2, lrhs, 4 + k, 16 - k)
    low.sweep(l2, l1, lrhs, 5 + k, 15 - k)

    for i in range(5 + k, 15 - k):
        v = l2[i]
        for y in (2 * i, 2 * i + 1):
            for a in range(2):
                at = pl.ds(a, LX, stride=2)
                m2[y, at, :] = m2[y, at, :] + v

    mid.sweep(m1, m2, rhs, 11 + 2 * k, 29 - 2 * k)
    mid.sweep(m2, m1, rhs, 12 + 2 * k, 28 - 2 * k)


def prolong_add(scal, m2, wide, u_ref, dst, lo, hi):
    begin = pl.multiple_of(scal[1] * 8, 8)
    zero = jnp.zeros((8, 128), F32)

    def body(m, n):
        for t in range(n):
            v = m2[m + t]
            wide[m + t, 0:8, :] = zero
            wide[m + t, 72:80, :] = zero
            wide[m + t, pl.ds(8, MX, stride=2), :] = v
            wide[m + t, pl.ds(9, MX, stride=2), :] = v

    rows(lo, hi, body)

    def add(m, n):
        y = 2 * m - 32 + HALO
        new = []
        for t in range(n):
            w = wide[m + t, pl.ds(begin, FX), :]
            new += [u_ref[y + 2 * t] + w, u_ref[y + 2 * t + 1] + w]
        for t in range(2 * n):
            dst[y + t] = new[t]

    rows(lo, hi, add)


def middle_kernel(scal, src, fbx, fby, fbz, fdiag, finv, u1, ends, here, near, swapped,
                  mbx, mby, mbz, mdiag, minv, lbx, lby, lbz, linv, u2_out, pack,
                  joined, rhs, absorb, conduct, m1, m2, lrhs, l1, l2, labsorb, lconduct, tmp, wide, fa, fb):
    fine = Level(fbx, fby, fbz, fdiag, finv, 1)
    mid = Level(mbx, mby, mbz, mdiag, minv, 2)
    low = Level(lbx, lby, lbz, None, linv, 4)
    gather_rows(scal, here, near, swapped, joined, 3)
    unpack_rows(joined, 0, rhs)
    unpack_rows(joined, 2, absorb)
    unpack_rows(joined, 4, conduct)
    mid.build(conduct, absorb, 2, 38, 4.0, True)
    restrict_low(lambda y, n: [absorb[y + t] for t in range(n)], tmp, labsorb, 1, 19)
    restrict_low(lambda y, n: [conduct[y + t] for t in range(n)], tmp, lconduct, 1, 19)
    low.build(lconduct, labsorb, 2, 18, 16.0, True)
    coarse(mid, low, rhs, m1, m2, lrhs, l1, l2, tmp, 0)
    x = planes((FX, 128))
    dev = scal[1]
    left, right = jnp.maximum(dev - 1, 0), jnp.minimum(dev + 1, 7)

    def first(y, n):
        new = []
        for t in range(n):
            at = pl.ds(y + t - 1, 1)
            u = jnp.where(x == 0, ends[left, at, :], jnp.where(x == FX - 1, ends[right, at, :], u1[y + t]))
            new.append(u)
        for t in range(n):
            fa[y + t] = new[t]

    rows(1, ROWS - 1, first)
    zero = jnp.zeros((FX, 128), F32)
    for y in (0, 1, ROWS - 2, ROWS - 1):
        fb[y] = zero
    fine.sweep(fb, fa, src, 2, ROWS - 2)
    prolong_add(scal, m2, wide, fb, fa, 12, 28)
    fine.sweep(fb, fa, src, 3, ROWS - 3)
    fine.sweep(fa, fb, src, 4, ROWS - 4)
    fine.sweep(fb, fa, src, 5, ROWS - 5)
    for y in (*range(6), *range(ROWS - 6, ROWS)):
        u2_out[y] = zero
    fine.sweep(u2_out, fb, src, 6, ROWS - 6)
    tiles = restrict_own([r[8:16] for r in fine.residual(u2_out, src, HALO, 16)])
    for i, t in enumerate(tiles):
        pack[i] = t


def last_kernel(scal, src, fbx, fby, fbz, fdiag, finv, u2, here, near, swapped,
                mbx, mby, mbz, mdiag, minv, lbx, lby, lbz, linv,
                out, out_res,
                joined, rhs, m1, m2, lrhs, l1, l2, tmp, wide, fa, fb):
    fine = Level(fbx, fby, fbz, fdiag, finv, 1)
    mid = Level(mbx, mby, mbz, mdiag, minv, 2)
    low = Level(lbx, lby, lbz, None, linv, 4)
    gather_rows(scal, here, near, swapped, joined, 1)
    unpack_rows(joined, 0, rhs)
    coarse(mid, low, rhs, m1, m2, lrhs, l1, l2, tmp, 1)
    prolong_add(scal, m2, wide, u2, fa, 14, 26)
    fine.sweep(fb, fa, src, 7, ROWS - 7)
    fine.sweep(fa, fb, src, 8, ROWS - 8)

    def finish(y, n):
        r = fine.residual(fa, src, HALO + y, n)
        for t in range(n):
            at = pl.ds(y + t, 8, stride=16)
            out[at, :] = fa[HALO + y + t, 8:16, :]
            out_res[at, :] = r[t][8:16]

    rows(0, 16, finish)


def call(kernel, outs, scratch, *args):
    return pl.pallas_call(
        kernel,
        out_shape=[jax.ShapeDtypeStruct(s, F32) for s in outs],
        in_specs=[pl.BlockSpec(memory_space=pltpu.SMEM)]
        + [pl.BlockSpec(memory_space=pltpu.VMEM)] * (len(args) - 1),
        out_specs=[pl.BlockSpec(memory_space=pltpu.VMEM)] * len(outs),
        scratch_shapes=[pltpu.VMEM(s, F32) for s in scratch],
        compiler_params=pltpu.CompilerParams(vmem_limit_bytes=VMEM_LIMIT),
    )(*args)


def other_core(array):
    return lax.ppermute(array, "dev", [(i, i ^ 1) for i in range(8)])


def spread(pack, ends=None):
    peers, devs = lax.axis_size("grp"), lax.axis_size("dev")

    def from_beside(array, by):
        pairs = []
        for g in range(peers):
            for d in range(devs):
                there = g + by if d % 2 == 0 else g - by
                if 0 <= there < peers:
                    pairs.append((there * devs + d, g * devs + d))
        return lax.ppermute(array, ("grp", "dev"), pairs)

    here = jnp.broadcast_to(pack, (devs,) + pack.shape)
    if ends is not None:
        d = lax.axis_index("dev")
        mine = jnp.where(jnp.arange(devs)[:, None, None] < d, ends[0], ends[1])
        here = jnp.concatenate([here, mine.reshape(devs, 4, 8, 128)], axis=1)
    here = lax.all_to_all(here, "dev", 0, 0)
    if ends is not None:
        ends = here[:, -4:].reshape(devs, 32, 128)
        here = here[:, :-4]
    near = jnp.stack([from_beside(here, 1), from_beside(here, 2)])
    return ends, here, near, other_core(near)


def local(source, absorb, conduct):
    peers = lax.axis_size("grp")
    d = lax.axis_index("dev")
    scal = jnp.stack([d % 2, d]).astype(jnp.int32)

    fine = jnp.stack([source, absorb, conduct]).transpose(0, 2, 1, 3)
    ahead = [(i, i + 1) for i in range(peers - 1)]
    back = [(j, i) for i, j in ahead]
    args = (source, absorb, conduct)
    before = lax.ppermute(jnp.stack([a[:, 16 - HALO:].transpose(1, 0, 2) for a in args]), "grp", ahead)
    after = lax.ppermute(jnp.stack([a[:, :HALO].transpose(1, 0, 2) for a in args]), "grp", back)
    fine = jnp.concatenate([before, fine, after], axis=1)
    via_b = lax.ppermute(fine, "dev", [(1, 2), (2, 1), (3, 4), (4, 3), (5, 6), (6, 5)])
    via_a = other_core(fine)
    block, wide_mid, wide_low = (ROWS, FX, 128), (MROWS, MX, 128), (LROWS, LX, 128)
    *state, u1, pack, ends = call(
        fine_kernel, [block] * 7 + [(6, 8, 128), (2, 32, 128)], [block] * 3, scal, fine, via_a, via_b
    )
    ends, *parts = spread(pack, ends)
    *coefs, u2, pack = call(
        middle_kernel,
        [wide_mid] * 5 + [wide_low] * 4 + [block, (2, 8, 128)],
        [(5, 6, 64, 128)] + [wide_mid] * 5 + [wide_low] * 5 + [(20, MX, 128), (MROWS, 80, 128), block, block],
        scal, *state, u1, ends, *parts,
    )
    _, *parts = spread(pack)
    out, res = call(
        last_kernel,
        [(128, 128), (128, 128)],
        [(5, 2, 64, 128)] + [wide_mid] * 3 + [wide_low] * 3 + [(20, MX, 128), (MROWS, 80, 128), block, block],
        scal, *state, u2, *parts, *coefs,
    )
    return out.reshape(8, 16, 128), res.reshape(8, 16, 128)


def solution(mesh):
    spec = P("dev", "grp", None)
    return jax.shard_map(local, mesh=mesh, in_specs=(spec,) * 3, out_specs=(spec,) * 2, check_vma=False)
```

time: 125 us -> 89.7 us (0.72)
  the two profiles are of different devices: /device:TPU:1 before, /device:TPU:521 now
where the time goes in v2:
time: 89.7 us; the launch traced here: 89.2 us
  starting transfers between devices  33.8 us (38%)
  waiting for transfers between devices  22.6 us (25%)
  blocking collectives  19.8 us (22%)
  Pallas kernels  9.95 us (11%)
  local copies, waits for them, and re-layouts  1.82 us (2%)
    all_to_all x2, blocking collectives, spread(): here = lax.all_to_all(here, 'dev', 0, 0)  19.8 us
    ppermute x4, starting transfers between devices, from_beside(): return lax.ppermute(array, ('grp', 'dev'), pairs)  12.5 us
    ppermute x3, starting transfers between devices, other_core(): return lax.ppermute(array, 'dev', [(i, i ^ 1) for i in range(8)])  11.5 us
    ppermute x4, waiting for transfers between devices, from_beside(): return lax.ppermute(array, ('grp', 'dev'), pairs)  11.1 us
    pallas_call x3, Pallas kernels, call(): pl.pallas_call(kernel, out_shape=[jax.ShapeDtypeStruct(s, F32) for s in o...  9.95 us
    ppermute x1, waiting for transfers between devices, local(): lax.ppermute(jnp.stack([a[:, 16 - HALO:].transpose(1, 0, 2) for a in args...  5.04 us
    ppermute x1, starting transfers between devices, local(): lax.ppermute(fine, 'dev', [(1, 2), (2, 1), (3, 4), (4, 3), (5, 6), (6, 5)])  4.55 us
    ppermute x1, waiting for transfers between devices, local(): lax.ppermute(fine, 'dev', [(1, 2), (2, 1), (3, 4), (4, 3), (5, 6), (6, 5)])  3.68 us
  transfers between devices with their start and end apart: 10, of which 8 were waited for; matrix products, arithmetic and copies ran while one was open for 0% of the time, Pallas kernels for 0%

profile of v2, /device:TPU:521, one launch (start us, length us, event | category | flops | bytes accessed | tf_op | source)
XLA Modules:
  0.0 89.2 jit_solution(7884566090170515639)
XLA Ops:
  0.6 0.0 copy-start
  0.6 0.9 %copy.22 = f32[8,16,128]{2,0,1:T(8,128)S(1)} copy(f32[8,16,128]{2,1,0:T(8,128)} %param.3) | data formatting | bytes 131072 | tf_op args[0]
  1.5 0.0 copy-done
  1.5 0.0 copy-start.1
  1.6 0.8 copy-done.1
  2.5 2.1 %collective-permute-start.1 = (f32[3,9,8,128]{3,2,1,0:T(8,128)S(1)}, f32[3,9,8,128]{3,2,1,0:T(8,128)S(1)}, u32[]{:S(2)}, u32[]{:S(2)}) collective-permute-start(f32[3,9,8,128]{3,2,1,0:T(8,128)S(1)} %pad_maximum_fusion.5), channel_id=1, source_target_pairs={{8,0},{16,8},{24,16},{32,24},{40,32},{48,40},{56,48},{64,56},{72,6... | collective-permute-start | bytes 331784 | tf_op jit(solution)/shard_map/ppermute | solution.py:380
  4.6 3.2 %collective-permute-start = (f32[3,9,8,128]{3,2,1,0:T(8,128)S(1)}, f32[3,9,8,128]{3,2,1,0:T(8,128)S(1)}, u32[]{:S(2)}, u32[]{:S(2)}) collective-permute-start(f32[3,9,8,128]{3,2,1,0:T(8,128)S(1)} %pad_maximum_fusion.4), channel_id=1, source_target_pairs={{0,8},{8,16},{16,24},{24,32},{32,40},{40,48},{48,56},{56,64},{64,7... | collective-permute-start | bytes 331784 | tf_op jit(solution)/shard_map/ppermute | solution.py:379
  7.8 0.5 collective-permute-done.1
  8.3 5.0 %collective-permute-done = f32[3,9,8,128]{3,2,1,0:T(8,128)S(1)} collective-permute-done((f32[3,9,8,128]{3,2,1,0:T(8,128)S(1)}, f32[3,9,8,128]{3,2,1,0:T(8,128)S(1)}, u32[]{:S(2)}, u32[]{:S(2)}) %collective-permute-start) | collective-permute-done | bytes 110624 | tf_op jit(solution)/shard_map/ppermute | solution.py:379
  13.4 4.6 %collective-permute-start.3 = (f32[3,34,8,128]{3,2,1,0:T(8,128)S(1)}, f32[3,34,8,128]{3,2,1,0:T(8,128)S(1)}, u32[]{:S(2)}, u32[]{:S(2)}) collective-permute-start(f32[3,34,8,128]{3,2,1,0:T(8,128)S(1)} %pad_maximum_fusion.own), channel_id=1, source_target_pairs={{1,2},{2,1},{3,4},{4,3},{5,6},{6,5},{9,10},{10,9},{11,12},{12,11},... | collective-permute-start | bytes 1253384 | tf_op jit(solution)/shard_map/ppermute | solution.py:382
  17.9 1.9 %collective-permute-start.2 = (f32[3,34,8,128]{3,2,1,0:T(8,128)S(1)}, f32[3,34,8,128]{3,2,1,0:T(8,128)S(1)}, u32[]{:S(2)}, u32[]{:S(2)}) collective-permute-start(f32[3,34,8,128]{3,2,1,0:T(8,128)S(1)} %pad_maximum_fusion.own), channel_id=1, source_target_pairs={{0,1},{1,0},{2,3},{3,2},{4,5},{5,4},{6,7},{7,6},{8,9},{9,8},{10,11... | collective-permute-start | bytes 1253384 | tf_op jit(solution)/shard_map/ppermute | solution.py:342
  19.9 0.1 pad_add_fusion.scal
  19.9 3.7 %collective-permute-done.3.via_b = f32[3,34,8,128]{3,2,1,0:T(8,128)S(1)} collective-permute-done((f32[3,34,8,128]{3,2,1,0:T(8,128)S(1)}, f32[3,34,8,128]{3,2,1,0:T(8,128)S(1)}, u32[]{:S(2)}, u32[]{:S(2)}) %collective-permute-start.3) | collective-permute-done | bytes 417824 | tf_op jit(solution)/shard_map/ppermute | solution.py:382
  23.6 0.0 collective-permute-done.2.via_a
  23.6 1.3 %shard_map.50 = (f32[34,24,128]{2,1,0:T(8,128)S(1)}, f32[34,24,128]{2,1,0:T(8,128)S(1)}, f32[34,24,128]{2,1,0:T(8,128)S(1)}, f32[34,24,128]{2,1,0:T(8,128)S(1)},...) custom-call(s32[2]{0:T(128)S(1)} %pad_add_fusion.scal, ...), custom_call_target="tpu_custom_call" | custom-call | tf_op jit(solution)/shard_map/pallas_call | solution.py:330
  25.0 0.1 broadcast_select_fusion
  25.1 12.2 %all_to_all.10 = f32[8,10,8,128]{3,2,1,0:T(8,128)S(1)} all-to-all(f32[8,10,8,128]{3,2,1,0:T(8,128)S(1)} %pad_maximum_fusion.2), channel_id=1, replica_groups=mesh['grp'=96,'dev'=8] {'dev'}, dimensions={0} | all-to-all | bytes 655360 | tf_op jit(solution)/shard_map/all_to_all | solution.py:362
  37.4 1.9 %collective-permute-start.5 = (f32[8,6,8,128]{3,2,1,0:T(8,128)S(1)}, f32[8,6,8,128]{3,2,1,0:T(8,128)S(1)}, u32[]{:S(2)}, u32[]{:S(2)}) collective-permute-start(f32[8,6,8,128]{3,2,1,0:T(8,128)S(1)} %slice.47.here), channel_id=1, source_target_pairs={{16,0},{18,2},{20,4},{22,6},{24,8},{26,10},{28,12},{30,14},{32,16}... | collective-permute-start | bytes 589832 | tf_op jit(solution)/shard_map/ppermute | solution.py:355
  39.3 5.2 %collective-permute-start.4 = (f32[8,6,8,128]{3,2,1,0:T(8,128)S(1)}, f32[8,6,8,128]{3,2,1,0:T(8,128)S(1)}, u32[]{:S(2)}, u32[]{:S(2)}) collective-permute-start(f32[8,6,8,128]{3,2,1,0:T(8,128)S(1)} %slice.47.here), channel_id=1, source_target_pairs={{8,0},{10,2},{12,4},{14,6},{16,8},{1,9},{18,10},{3,11},{20,12},{5,... | collective-permute-start | bytes 589832 | tf_op jit(solution)/shard_map/ppermute | solution.py:355
  44.5 3.6 %collective-permute-done.5 = f32[8,6,8,128]{3,2,1,0:T(8,128)S(1)} collective-permute-done((f32[8,6,8,128]{3,2,1,0:T(8,128)S(1)}, f32[8,6,8,128]{3,2,1,0:T(8,128)S(1)}, u32[]{:S(2)}, u32[]{:S(2)}) %collective-permute-start.5) | collective-permute-done | bytes 196640 | tf_op jit(solution)/shard_map/ppermute | solution.py:355
  48.1 3.7 %collective-permute-done.4 = f32[8,6,8,128]{3,2,1,0:T(8,128)S(1)} collective-permute-done((f32[8,6,8,128]{3,2,1,0:T(8,128)S(1)}, f32[8,6,8,128]{3,2,1,0:T(8,128)S(1)}, u32[]{:S(2)}, u32[]{:S(2)}) %collective-permute-start.4) | collective-permute-done | bytes 196640 | tf_op jit(solution)/shard_map/ppermute | solution.py:355
  51.9 2.6 %collective-permute-start.6 = (f32[2,8,6,8,128]{4,3,2,1,0:T(8,128)S(1)}, f32[2,8,6,8,128]{4,3,2,1,0:T(8,128)S(1)}, u32[]{:S(2)}, u32[]{:S(2)}) collective-permute-start(f32[2,8,6,8,128]{4,3,2,1,0:T(8,128)S(1)} %pad_maximum_fusion.1.near), channel_id=1, source_target_pairs={{0,1},{1,0},{2,3},{3,2},{4,5},{5,4},{6,7},{7,6},{8,9},{9,8},{10,11... | collective-permute-start | bytes 1179656 | tf_op jit(solution)/shard_map/ppermute | solution.py:342
  54.5 1.3 %collective-permute-done.6.swapped = f32[2,8,6,8,128]{4,3,2,1,0:T(8,128)S(1)} collective-permute-done((f32[2,8,6,8,128]{4,3,2,1,0:T(8,128)S(1)}, f32[2,8,6,8,128]{4,3,2,1,0:T(8,128)S(1)}, u32[]{:S(2)}, u32[]{:S(2)}) %collective-permute-start.6) | collective-permute-done | bytes 393248 | tf_op jit(solution)/shard_map/ppermute | solution.py:342
  55.8 5.2 %shard_map.51 = (f32[40,32,128]{2,1,0:T(8,128)S(1)}, f32[40,32,128]{2,1,0:T(8,128)S(1)}, f32[40,32,128]{2,1,0:T(8,128)S(1)}, f32[40,32,128]{2,1,0:T(8,128)S(1)},...) custom-call(s32[2]{0:T(128)S(1)} %pad_add_fusion.scal, ...), custom_call_target="tpu_custom_call" | custom-call | tf_op jit(solution)/shard_map/pallas_call | solution.py:330
  61.0 7.6 %all_to_all.11.here = f32[8,2,8,128]{3,2,1,0:T(8,128)S(1)} all-to-all(f32[8,2,8,128]{3,2,1,0:T(8,128)S(1)} %broadcast_in_dim.33), channel_id=1, replica_groups=mesh['grp'=96,'dev'=8] {'dev'}, dimensions={0} | all-to-all | bytes 131072 | tf_op jit(solution)/shard_map/all_to_all | solution.py:362
  68.6 2.4 %collective-permute-start.8 = (f32[8,2,8,128]{3,2,1,0:T(8,128)S(1)}, f32[8,2,8,128]{3,2,1,0:T(8,128)S(1)}, u32[]{:S(2)}, u32[]{:S(2)}) collective-permute-start(f32[8,2,8,128]{3,2,1,0:T(8,128)S(1)} %all_to_all.11.here), channel_id=1, source_target_pairs={{16,0},{18,2},{20,4},{22,6},{24,8},{26,10},{28,12},{30,14},{32,16}... | collective-permute-start | bytes 196616 | tf_op jit(solution)/shard_map/ppermute | solution.py:355
  71.0 2.9 %collective-permute-start.7 = (f32[8,2,8,128]{3,2,1,0:T(8,128)S(1)}, f32[8,2,8,128]{3,2,1,0:T(8,128)S(1)}, u32[]{:S(2)}, u32[]{:S(2)}) collective-permute-start(f32[8,2,8,128]{3,2,1,0:T(8,128)S(1)} %all_to_all.11.here), channel_id=1, source_target_pairs={{8,0},{10,2},{12,4},{14,6},{16,8},{1,9},{18,10},{3,11},{20,12},{5,... | collective-permute-start | bytes 196616 | tf_op jit(solution)/shard_map/ppermute | solution.py:355
  74.0 3.8 %collective-permute-done.8 = f32[8,2,8,128]{3,2,1,0:T(8,128)S(1)} collective-permute-done((f32[8,2,8,128]{3,2,1,0:T(8,128)S(1)}, f32[8,2,8,128]{3,2,1,0:T(8,128)S(1)}, u32[]{:S(2)}, u32[]{:S(2)}) %collective-permute-start.8) | collective-permute-done | bytes 65568 | tf_op jit(solution)/shard_map/ppermute | solution.py:355
  77.8 0.0 collective-permute-done.7
  77.8 7.0 %collective-permute-start.9 = (f32[2,8,2,8,128]{4,3,2,1,0:T(8,128)S(1)}, f32[2,8,2,8,128]{4,3,2,1,0:T(8,128)S(1)}, u32[]{:S(2)}, u32[]{:S(2)}) collective-permute-start(f32[2,8,2,8,128]{4,3,2,1,0:T(8,128)S(1)} %pad_maximum_fusion.3.near), channel_id=1, source_target_pairs={{0,1},{1,0},{2,3},{3,2},{4,5},{5,4},{6,7},{7,6},{8,9},{9,8},{10,11... | collective-permute-start | bytes 393224 | tf_op jit(solution)/shard_map/ppermute | solution.py:342
  84.8 1.0 %collective-permute-done.9.swapped = f32[2,8,2,8,128]{4,3,2,1,0:T(8,128)S(1)} collective-permute-done((f32[2,8,2,8,128]{4,3,2,1,0:T(8,128)S(1)}, f32[2,8,2,8,128]{4,3,2,1,0:T(8,128)S(1)}, u32[]{:S(2)}, u32[]{:S(2)}) %collective-permute-start.9) | collective-permute-done | bytes 131104 | tf_op jit(solution)/shard_map/ppermute | solution.py:342
  85.7 3.5 %shard_map.52 = (f32[128,128]{1,0:T(8,128)}, f32[128,128]{1,0:T(8,128)}) custom-call(s32[2]{0:T(128)S(1)} %pad_add_fusion.scal, f32[34,24,128]{2,1,0:T(8,128)S(1)} %get-tuple-element.24.src, f32[34,24,128]{2,1,0:T(8,128)S(1)} %get-tuple-element.25.fbx, f32[34,24,128]{2,1,0:T(8,128)S(1)} %get-tuple-element.26.fby, f32[34,24,128]{2,1,0:T(8,128)S(1)} %get-tuple-element.27.fbz, ...), custom_call_target="tpu_custom_call" | custom-call | tf_op jit(solution)/shard_map/pallas_call | solution.py:330
  (17 shorter events, 0.2 us)
Async XLA Ops:
  0.6 0.9 %copy-start = (f32[8,16,128]{2,1,0:T(8,128)S(1)}, f32[8,16,128]{2,1,0:T(8,128)}, u32[]{:S(2)}) copy-start(f32[8,16,128]{2,1,0:T(8,128)} %param.4) | copy-start | bytes 196612
  1.5 0.8 copy-start.1
  2.5 5.8 %collective-permute-start.1 = (f32[3,9,8,128]{3,2,1,0:T(8,128)S(1)}, f32[3,9,8,128]{3,2,1,0:T(8,128)S(1)}, u32[]{:S(2)}, u32[]{:S(2)}) collective-permute-start(f32[3,9,8,128]{3,2,1,0:T(8,128)S(1)} %pad_maximum_fusion.5), channel_id=1, source_target_pairs={{8,0},{16,8},{24,16},{32,24},{40,32},{48,40},{56,48},{64,56},{72,6... | collective-permute-start | bytes 331784 | tf_op jit(solution)/shard_map/ppermute | solution.py:380
  4.6 8.8 %collective-permute-start = (f32[3,9,8,128]{3,2,1,0:T(8,128)S(1)}, f32[3,9,8,128]{3,2,1,0:T(8,128)S(1)}, u32[]{:S(2)}, u32[]{:S(2)}) collective-permute-start(f32[3,9,8,128]{3,2,1,0:T(8,128)S(1)} %pad_maximum_fusion.4), channel_id=1, source_target_pairs={{0,8},{8,16},{16,24},{24,32},{32,40},{40,48},{48,56},{56,64},{64,7... | collective-permute-start | bytes 331784 | tf_op jit(solution)/shard_map/ppermute | solution.py:379
  13.4 10.3 %collective-permute-start.3 = (f32[3,34,8,128]{3,2,1,0:T(8,128)S(1)}, f32[3,34,8,128]{3,2,1,0:T(8,128)S(1)}, u32[]{:S(2)}, u32[]{:S(2)}) collective-permute-start(f32[3,34,8,128]{3,2,1,0:T(8,128)S(1)} %pad_maximum_fusion.own), channel_id=1, source_target_pairs={{1,2},{2,1},{3,4},{4,3},{5,6},{6,5},{9,10},{10,9},{11,12},{12,11},... | collective-permute-start | bytes 1253384 | tf_op jit(solution)/shard_map/ppermute | solution.py:382
  17.9 5.7 %collective-permute-start.2 = (f32[3,34,8,128]{3,2,1,0:T(8,128)S(1)}, f32[3,34,8,128]{3,2,1,0:T(8,128)S(1)}, u32[]{:S(2)}, u32[]{:S(2)}) collective-permute-start(f32[3,34,8,128]{3,2,1,0:T(8,128)S(1)} %pad_maximum_fusion.own), channel_id=1, source_target_pairs={{0,1},{1,0},{2,3},{3,2},{4,5},{5,4},{6,7},{7,6},{8,9},{9,8},{10,11... | collective-permute-start | bytes 1253384 | tf_op jit(solution)/shard_map/ppermute | solution.py:342
  37.4 10.7 %collective-permute-start.5 = (f32[8,6,8,128]{3,2,1,0:T(8,128)S(1)}, f32[8,6,8,128]{3,2,1,0:T(8,128)S(1)}, u32[]{:S(2)}, u32[]{:S(2)}) collective-permute-start(f32[8,6,8,128]{3,2,1,0:T(8,128)S(1)} %slice.47.here), channel_id=1, source_target_pairs={{16,0},{18,2},{20,4},{22,6},{24,8},{26,10},{28,12},{30,14},{32,16}... | collective-permute-start | bytes 589832 | tf_op jit(solution)/shard_map/ppermute | solution.py:355
  39.3 12.5 %collective-permute-start.4 = (f32[8,6,8,128]{3,2,1,0:T(8,128)S(1)}, f32[8,6,8,128]{3,2,1,0:T(8,128)S(1)}, u32[]{:S(2)}, u32[]{:S(2)}) collective-permute-start(f32[8,6,8,128]{3,2,1,0:T(8,128)S(1)} %slice.47.here), channel_id=1, source_target_pairs={{8,0},{10,2},{12,4},{14,6},{16,8},{1,9},{18,10},{3,11},{20,12},{5,... | collective-permute-start | bytes 589832 | tf_op jit(solution)/shard_map/ppermute | solution.py:355
  51.9 3.9 %collective-permute-start.6 = (f32[2,8,6,8,128]{4,3,2,1,0:T(8,128)S(1)}, f32[2,8,6,8,128]{4,3,2,1,0:T(8,128)S(1)}, u32[]{:S(2)}, u32[]{:S(2)}) collective-permute-start(f32[2,8,6,8,128]{4,3,2,1,0:T(8,128)S(1)} %pad_maximum_fusion.1.near), channel_id=1, source_target_pairs={{0,1},{1,0},{2,3},{3,2},{4,5},{5,4},{6,7},{7,6},{8,9},{9,8},{10,11... | collective-permute-start | bytes 1179656 | tf_op jit(solution)/shard_map/ppermute | solution.py:342
  68.6 9.2 %collective-permute-start.8 = (f32[8,2,8,128]{3,2,1,0:T(8,128)S(1)}, f32[8,2,8,128]{3,2,1,0:T(8,128)S(1)}, u32[]{:S(2)}, u32[]{:S(2)}) collective-permute-start(f32[8,2,8,128]{3,2,1,0:T(8,128)S(1)} %all_to_all.11.here), channel_id=1, source_target_pairs={{16,0},{18,2},{20,4},{22,6},{24,8},{26,10},{28,12},{30,14},{32,16}... | collective-permute-start | bytes 196616 | tf_op jit(solution)/shard_map/ppermute | solution.py:355
  71.0 6.8 %collective-permute-start.7 = (f32[8,2,8,128]{3,2,1,0:T(8,128)S(1)}, f32[8,2,8,128]{3,2,1,0:T(8,128)S(1)}, u32[]{:S(2)}, u32[]{:S(2)}) collective-permute-start(f32[8,2,8,128]{3,2,1,0:T(8,128)S(1)} %all_to_all.11.here), channel_id=1, source_target_pairs={{8,0},{10,2},{12,4},{14,6},{16,8},{1,9},{18,10},{3,11},{20,12},{5,... | collective-permute-start | bytes 196616 | tf_op jit(solution)/shard_map/ppermute | solution.py:355
  77.8 7.9 %collective-permute-start.9 = (f32[2,8,2,8,128]{4,3,2,1,0:T(8,128)S(1)}, f32[2,8,2,8,128]{4,3,2,1,0:T(8,128)S(1)}, u32[]{:S(2)}, u32[]{:S(2)}) collective-permute-start(f32[2,8,2,8,128]{4,3,2,1,0:T(8,128)S(1)} %pad_maximum_fusion.3.near), channel_id=1, source_target_pairs={{0,1},{1,0},{2,3},{3,2},{4,5},{5,4},{6,7},{7,6},{8,9},{9,8},{10,11... | collective-permute-start | bytes 393224 | tf_op jit(solution)/shard_map/ppermute | solution.py:342

commit v3 on v2

--- a/solution.py
+++ b/solution.py
@@ -132,9 +132,10 @@
     def body(i, n):
         r = fine_rows(2 * i, 2 * n)
         for t in range(n):
-            tmp[t] = pair_lanes(r[2 * t] + r[2 * t + 1], 2)
-        for t in range(n):
-            dst[i + t] = (tmp[t, pl.ds(0, LX, stride=2), :] + tmp[t, pl.ds(1, LX, stride=2), :]) * 0.125
+            tmp[t] = r[2 * t] + r[2 * t + 1]
+        for t in range(n):
+            pair = tmp[t, pl.ds(0, LX, stride=2), :] + tmp[t, pl.ds(1, LX, stride=2), :]
+            dst[i + t] = pair_lanes(pair, 2) * 0.125
 
     rows(lo, hi, body)
 
@@ -165,9 +166,9 @@
     level = Level(bx, by, bz, diag, inv, 1)
     level.build(conduct, absorb, 1, ROWS - 1, 1.0, False)
     scale(u1, inv, src, 1, ROWS - 1)
-    for y in range(1, ROWS - 1):
+    for y in range(16):
         for i, x in enumerate((8, 15)):
-            ends[i, y - 1:y, :] = u1[y, x:x + 1, :]
+            ends[i, y:y + 1, :] = u1[HALO + y, x:x + 1, :]
     level.sweep(u2, u1, src, HALO - 1, ROWS - HALO + 1)
     tiles = restrict_own([r[8:16] for r in level.residual(u2, src, HALO, 16)])
     tiles += restrict_own([absorb[HALO + i, 8:16, :] for i in range(16)])
@@ -177,8 +178,6 @@
 
 
 def gather_rows(scal, here, near, swapped, joined, arrays):
-    even = scal[0] == 0
-
     def copy(j, source):
         for t in range(2 * arrays):
             for dev in range(8):
@@ -187,13 +186,14 @@
     copy(2, here)
     for i in range(2):
         after, before = 3 + i, 1 - i
-
-        @pl.when(even)
+        near_after = scal[2 + i] != 0
+
+        @pl.when(near_after)
         def _():
             copy(after, near.at[i])
             copy(before, swapped.at[i])
 
-        @pl.when(jnp.logical_not(even))
+        @pl.when(jnp.logical_not(near_after))
         def _():
             copy(after, swapped.at[i])
             copy(before, near.at[i])
@@ -276,16 +276,12 @@
     dev = scal[1]
     left, right = jnp.maximum(dev - 1, 0), jnp.minimum(dev + 1, 7)
 
-    def first(y, n):
-        new = []
-        for t in range(n):
-            at = pl.ds(y + t - 1, 1)
-            u = jnp.where(x == 0, ends[left, at, :], jnp.where(x == FX - 1, ends[right, at, :], u1[y + t]))
-            new.append(u)
-        for t in range(n):
-            fa[y + t] = new[t]
-
-    rows(1, ROWS - 1, first)
+    for y in range(1, ROWS - 1):
+        u = u1[y]
+        if 0 <= y - HALO < 16:
+            at = pl.ds(y - HALO, 1)
+            u = jnp.where(x == 0, ends[left, at, :], jnp.where(x == FX - 1, ends[right, at, :], u))
+        fa[y] = u
     zero = jnp.zeros((FX, 128), F32)
     for y in (0, 1, ROWS - 2, ROWS - 1):
         fb[y] = zero
@@ -342,6 +338,14 @@
     return lax.ppermute(array, "dev", [(i, i ^ 1) for i in range(8)])
 
 
+def one_away(g, core):
+    return 1 if g % 2 == core else -1
+
+
+def two_away(g, core):
+    return 2 if g // 2 % 2 != core else -2
+
+
 def spread(pack, ends=None):
     peers, devs = lax.axis_size("grp"), lax.axis_size("dev")
 
@@ -349,7 +353,7 @@
         pairs = []
         for g in range(peers):
             for d in range(devs):
-                there = g + by if d % 2 == 0 else g - by
+                there = g + by(g, d % 2)
                 if 0 <= there < peers:
                     pairs.append((there * devs + d, g * devs + d))
         return lax.ppermute(array, ("grp", "dev"), pairs)
@@ -358,32 +362,38 @@
     if ends is not None:
         d = lax.axis_index("dev")
         mine = jnp.where(jnp.arange(devs)[:, None, None] < d, ends[0], ends[1])
-        here = jnp.concatenate([here, mine.reshape(devs, 4, 8, 128)], axis=1)
+        here = jnp.concatenate([here, mine.reshape(devs, 2, 8, 128)], axis=1)
     here = lax.all_to_all(here, "dev", 0, 0)
     if ends is not None:
-        ends = here[:, -4:].reshape(devs, 32, 128)
-        here = here[:, :-4]
-    near = jnp.stack([from_beside(here, 1), from_beside(here, 2)])
+        ends = here[:, -2:].reshape(devs, 16, 128)
+        here = here[:, :-2]
+    near = jnp.stack([from_beside(here, one_away), from_beside(here, two_away)])
     return ends, here, near, other_core(near)
 
 
 def local(source, absorb, conduct):
     peers = lax.axis_size("grp")
     d = lax.axis_index("dev")
-    scal = jnp.stack([d % 2, d]).astype(jnp.int32)
+    g, core = lax.axis_index("grp"), d % 2
+    scal = jnp.stack([core, d, g % 2 == core, g // 2 % 2 != core]).astype(jnp.int32)
 
     fine = jnp.stack([source, absorb, conduct]).transpose(0, 2, 1, 3)
-    ahead = [(i, i + 1) for i in range(peers - 1)]
-    back = [(j, i) for i, j in ahead]
-    args = (source, absorb, conduct)
-    before = lax.ppermute(jnp.stack([a[:, 16 - HALO:].transpose(1, 0, 2) for a in args]), "grp", ahead)
-    after = lax.ppermute(jnp.stack([a[:, :HALO].transpose(1, 0, 2) for a in args]), "grp", back)
+    even = g % 2 == 0
+    first, last = fine[:, :HALO], fine[:, 16 - HALO:]
+
+    def swap_rows(array, low):
+        pairs = [(i, i + 1) for i in range(low, peers - 1, 2)]
+        return lax.ppermute(array, "grp", pairs + [(j, i) for i, j in pairs])
+
+    one = swap_rows(jnp.where(even, last, first), 0)
+    two = swap_rows(jnp.where(even, first, last), 1)
+    before, after = jnp.where(even, two, one), jnp.where(even, one, two)
     fine = jnp.concatenate([before, fine, after], axis=1)
     via_b = lax.ppermute(fine, "dev", [(1, 2), (2, 1), (3, 4), (4, 3), (5, 6), (6, 5)])
     via_a = other_core(fine)
     block, wide_mid, wide_low = (ROWS, FX, 128), (MROWS, MX, 128), (LROWS, LX, 128)
     *state, u1, pack, ends = call(
-        fine_kernel, [block] * 7 + [(6, 8, 128), (2, 32, 128)], [block] * 3, scal, fine, via_a, via_b
+        fine_kernel, [block] * 7 + [(6, 8, 128), (2, 16, 128)], [block] * 3, scal, fine, via_a, via_b
     )
     ends, *parts = spread(pack, ends)
     *coefs, u2, pack = call(

time: 89.7 us -> 86.9 us (0.969)
  the two profiles are of different devices: /device:TPU:521 before, /device:TPU:513 now
where the time goes in v3:
time: 86.9 us; the launch traced here: 86.4 us
  starting transfers between devices  32.6 us (38%)
  waiting for transfers between devices  23.1 us (27%)
  blocking collectives  18.8 us (22%)
  Pallas kernels  9.63 us (11%)
  local copies, waits for them, and re-layouts  0.99 us (1%)
  between operations  0.92 us (1%)
    all_to_all x2, blocking collectives, spread(): here = lax.all_to_all(here, 'dev', 0, 0)  18.8 us
    ppermute x4, waiting for transfers between devices, from_beside(): return lax.ppermute(array, ('grp', 'dev'), pairs)  13.6 us
    ppermute x4, starting transfers between devices, from_beside(): return lax.ppermute(array, ('grp', 'dev'), pairs)  12 us
    pallas_call x3, Pallas kernels, call(): pl.pallas_call(kernel, out_shape=[jax.ShapeDtypeStruct(s, F32) for s in o...  9.63 us
    ppermute x2, starting transfers between devices, swap_rows(): return lax.ppermute(array, 'grp', pairs + [(j, i) for i, j in pairs])  8.22 us
    ppermute x3, starting transfers between devices, other_core(): return lax.ppermute(array, 'dev', [(i, i ^ 1) for i in range(8)])  7.27 us
    ppermute x1, starting transfers between devices, local(): lax.ppermute(fine, 'dev', [(1, 2), (2, 1), (3, 4), (4, 3), (5, 6), (6, 5)])  5.11 us
    ppermute x1, waiting for transfers between devices, local(): lax.ppermute(fine, 'dev', [(1, 2), (2, 1), (3, 4), (4, 3), (5, 6), (6, 5)])  3.64 us
  transfers between devices with their start and end apart: 10, of which 9 were waited for; matrix products, arithmetic and copies ran while one was open for 0% of the time, Pallas kernels for 0%

profile of v3, /device:TPU:513, one launch (start us, length us, event | category | flops | bytes accessed | tf_op | source)
XLA Modules:
  0.0 86.4 jit_solution(909057985345022350)
XLA Ops:
  0.7 0.0 copy-start
  0.7 0.0 copy-start.1
  0.7 0.9 %copy.11 = f32[8,16,128]{2,0,1:T(8,128)S(1)} copy(f32[8,16,128]{2,1,0:T(8,128)} %param.3) | data formatting | bytes 131072 | tf_op args[0]
  1.6 0.0 copy-done
  1.6 0.0 copy-done.1
  1.7 6.3 %collective-permute-start = (f32[3,9,8,128]{3,2,1,0:T(8,128)S(1)}, f32[3,9,8,128]{3,2,1,0:T(8,128)S(1)}, u32[]{:S(2)}, u32[]{:S(2)}) collective-permute-start(f32[3,9,8,128]{3,2,1,0:T(8,128)S(1)} %get-tuple-element.48), channel_id=1, source_target_pairs={{8,16},{24,32},{40,48},{56,64},{72,80},{88,96},{104,112},{120,128}... | collective-permute-start | bytes 331784 | tf_op jit(solution)/shard_map/ppermute | solution.py:386
  8.0 1.9 %collective-permute-start.1 = (f32[3,9,8,128]{3,2,1,0:T(8,128)S(1)}, f32[3,9,8,128]{3,2,1,0:T(8,128)S(1)}, u32[]{:S(2)}, u32[]{:S(2)}) collective-permute-start(f32[3,9,8,128]{3,2,1,0:T(8,128)S(1)} %get-tuple-element.49), channel_id=1, source_target_pairs={{0,8},{16,24},{32,40},{48,56},{64,72},{80,88},{96,104},{112,120},{... | collective-permute-start | bytes 331784 | tf_op jit(solution)/shard_map/ppermute | solution.py:386
  9.9 0.9 %collective-permute-done = f32[3,9,8,128]{3,2,1,0:T(8,128)S(1)} collective-permute-done((f32[3,9,8,128]{3,2,1,0:T(8,128)S(1)}, f32[3,9,8,128]{3,2,1,0:T(8,128)S(1)}, u32[]{:S(2)}, u32[]{:S(2)}) %collective-permute-start) | collective-permute-done | bytes 110624 | tf_op jit(solution)/shard_map/ppermute | solution.py:386
  10.8 2.7 %collective-permute-done.1 = f32[3,9,8,128]{3,2,1,0:T(8,128)S(1)} collective-permute-done((f32[3,9,8,128]{3,2,1,0:T(8,128)S(1)}, f32[3,9,8,128]{3,2,1,0:T(8,128)S(1)}, u32[]{:S(2)}, u32[]{:S(2)}) %collective-permute-start.1) | collective-permute-done | bytes 110624 | tf_op jit(solution)/shard_map/ppermute | solution.py:386
  13.5 5.1 %collective-permute-start.3 = (f32[3,34,8,128]{3,2,1,0:T(8,128)S(1)}, f32[3,34,8,128]{3,2,1,0:T(8,128)S(1)}, u32[]{:S(2)}, u32[]{:S(2)}) collective-permute-start(f32[3,34,8,128]{3,2,1,0:T(8,128)S(1)} %pad_maximum_fusion.own), channel_id=1, source_target_pairs={{1,2},{2,1},{3,4},{4,3},{5,6},{6,5},{9,10},{10,9},{11,12},{12,11},... | collective-permute-start | bytes 1253384 | tf_op jit(solution)/shard_map/ppermute | solution.py:392
  18.7 1.9 %collective-permute-start.2 = (f32[3,34,8,128]{3,2,1,0:T(8,128)S(1)}, f32[3,34,8,128]{3,2,1,0:T(8,128)S(1)}, u32[]{:S(2)}, u32[]{:S(2)}) collective-permute-start(f32[3,34,8,128]{3,2,1,0:T(8,128)S(1)} %pad_maximum_fusion.own), channel_id=1, source_target_pairs={{0,1},{1,0},{2,3},{3,2},{4,5},{5,4},{6,7},{7,6},{8,9},{9,8},{10,11... | collective-permute-start | bytes 1253384 | tf_op jit(solution)/shard_map/ppermute | solution.py:338
  20.7 0.1 pad_add_fusion.scal
  20.7 3.6 %collective-permute-done.3.via_b = f32[3,34,8,128]{3,2,1,0:T(8,128)S(1)} collective-permute-done((f32[3,34,8,128]{3,2,1,0:T(8,128)S(1)}, f32[3,34,8,128]{3,2,1,0:T(8,128)S(1)}, u32[]{:S(2)}, u32[]{:S(2)}) %collective-permute-start.3) | collective-permute-done | bytes 417824 | tf_op jit(solution)/shard_map/ppermute | solution.py:392
  24.4 0.0 collective-permute-done.2.via_a
  24.4 1.3 %shard_map.50 = (f32[34,24,128]{2,1,0:T(8,128)S(1)}, f32[34,24,128]{2,1,0:T(8,128)S(1)}, f32[34,24,128]{2,1,0:T(8,128)S(1)}, f32[34,24,128]{2,1,0:T(8,128)S(1)},...) custom-call(s32[4]{0:T(128)S(1)} %pad_add_fusion.scal, ...), custom_call_target="tpu_custom_call" | custom-call | tf_op jit(solution)/shard_map/pallas_call | solution.py:326
  25.7 0.1 broadcast_select_fusion.2
  25.8 11.2 %all_to_all.10 = f32[8,8,8,128]{3,2,1,0:T(8,128)S(1)} all-to-all(f32[8,8,8,128]{3,2,1,0:T(8,128)S(1)} %pad_maximum_fusion.2), channel_id=1, replica_groups=mesh['grp'=96,'dev'=8] {'dev'}, dimensions={0} | all-to-all | bytes 524288 | tf_op jit(solution)/shard_map/all_to_all | solution.py:366
  37.1 1.9 %collective-permute-start.5 = (f32[8,6,8,128]{3,2,1,0:T(8,128)S(1)}, f32[8,6,8,128]{3,2,1,0:T(8,128)S(1)}, u32[]{:S(2)}, u32[]{:S(2)}) collective-permute-start(f32[8,6,8,128]{3,2,1,0:T(8,128)S(1)} %slice.27.here), channel_id=1, source_target_pairs={{17,1},{19,3},{21,5},{23,7},{25,9},{27,11},{29,13},{31,15},{32,16}... | collective-permute-start | bytes 589832 | tf_op jit(solution)/shard_map/ppermute | solution.py:359
  39.0 4.1 %collective-permute-start.4 = (f32[8,6,8,128]{3,2,1,0:T(8,128)S(1)}, f32[8,6,8,128]{3,2,1,0:T(8,128)S(1)}, u32[]{:S(2)}, u32[]{:S(2)}) collective-permute-start(f32[8,6,8,128]{3,2,1,0:T(8,128)S(1)} %slice.27.here), channel_id=1, source_target_pairs={{8,0},{10,2},{12,4},{14,6},{0,8},{17,9},{2,10},{19,11},{4,12},{21,... | collective-permute-start | bytes 589832 | tf_op jit(solution)/shard_map/ppermute | solution.py:359
  43.2 3.8 %collective-permute-done.5 = f32[8,6,8,128]{3,2,1,0:T(8,128)S(1)} collective-permute-done((f32[8,6,8,128]{3,2,1,0:T(8,128)S(1)}, f32[8,6,8,128]{3,2,1,0:T(8,128)S(1)}, u32[]{:S(2)}, u32[]{:S(2)}) %collective-permute-start.5) | collective-permute-done | bytes 196640 | tf_op jit(solution)/shard_map/ppermute | solution.py:359
  46.9 5.1 %collective-permute-done.4 = f32[8,6,8,128]{3,2,1,0:T(8,128)S(1)} collective-permute-done((f32[8,6,8,128]{3,2,1,0:T(8,128)S(1)}, f32[8,6,8,128]{3,2,1,0:T(8,128)S(1)}, u32[]{:S(2)}, u32[]{:S(2)}) %collective-permute-start.4) | collective-permute-done | bytes 196640 | tf_op jit(solution)/shard_map/ppermute | solution.py:359
  52.1 2.3 %collective-permute-start.6 = (f32[2,8,6,8,128]{4,3,2,1,0:T(8,128)S(1)}, f32[2,8,6,8,128]{4,3,2,1,0:T(8,128)S(1)}, u32[]{:S(2)}, u32[]{:S(2)}) collective-permute-start(f32[2,8,6,8,128]{4,3,2,1,0:T(8,128)S(1)} %pad_maximum_fusion.1.near), channel_id=1, source_target_pairs={{0,1},{1,0},{2,3},{3,2},{4,5},{5,4},{6,7},{7,6},{8,9},{9,8},{10,11... | collective-permute-start | bytes 1179656 | tf_op jit(solution)/shard_map/ppermute | solution.py:338
  54.4 1.3 %collective-permute-done.6.swapped = f32[2,8,6,8,128]{4,3,2,1,0:T(8,128)S(1)} collective-permute-done((f32[2,8,6,8,128]{4,3,2,1,0:T(8,128)S(1)}, f32[2,8,6,8,128]{4,3,2,1,0:T(8,128)S(1)}, u32[]{:S(2)}, u32[]{:S(2)}) %collective-permute-start.6) | collective-permute-done | bytes 393248 | tf_op jit(solution)/shard_map/ppermute | solution.py:338
  55.7 4.9 %shard_map.51 = (f32[40,32,128]{2,1,0:T(8,128)S(1)}, f32[40,32,128]{2,1,0:T(8,128)S(1)}, f32[40,32,128]{2,1,0:T(8,128)S(1)}, f32[40,32,128]{2,1,0:T(8,128)S(1)},...) custom-call(s32[4]{0:T(128)S(1)} %pad_add_fusion.scal, ...), custom_call_target="tpu_custom_call" | custom-call | tf_op jit(solution)/shard_map/pallas_call | solution.py:326
  60.6 7.6 %all_to_all.11.here = f32[8,2,8,128]{3,2,1,0:T(8,128)S(1)} all-to-all(f32[8,2,8,128]{3,2,1,0:T(8,128)S(1)} %broadcast_in_dim.33), channel_id=1, replica_groups=mesh['grp'=96,'dev'=8] {'dev'}, dimensions={0} | all-to-all | bytes 131072 | tf_op jit(solution)/shard_map/all_to_all | solution.py:366
  68.2 1.9 %collective-permute-start.8 = (f32[8,2,8,128]{3,2,1,0:T(8,128)S(1)}, f32[8,2,8,128]{3,2,1,0:T(8,128)S(1)}, u32[]{:S(2)}, u32[]{:S(2)}) collective-permute-start(f32[8,2,8,128]{3,2,1,0:T(8,128)S(1)} %all_to_all.11.here), channel_id=1, source_target_pairs={{17,1},{19,3},{21,5},{23,7},{25,9},{27,11},{29,13},{31,15},{32,16}... | collective-permute-start | bytes 196616 | tf_op jit(solution)/shard_map/ppermute | solution.py:359
  70.1 4.0 %collective-permute-start.7 = (f32[8,2,8,128]{3,2,1,0:T(8,128)S(1)}, f32[8,2,8,128]{3,2,1,0:T(8,128)S(1)}, u32[]{:S(2)}, u32[]{:S(2)}) collective-permute-start(f32[8,2,8,128]{3,2,1,0:T(8,128)S(1)} %all_to_all.11.here), channel_id=1, source_target_pairs={{8,0},{10,2},{12,4},{14,6},{0,8},{17,9},{2,10},{19,11},{4,12},{21,... | collective-permute-start | bytes 196616 | tf_op jit(solution)/shard_map/ppermute | solution.py:359
  74.2 0.2 collective-permute-done.8
  74.4 4.5 %collective-permute-done.7 = f32[8,2,8,128]{3,2,1,0:T(8,128)S(1)} collective-permute-done((f32[8,2,8,128]{3,2,1,0:T(8,128)S(1)}, f32[8,2,8,128]{3,2,1,0:T(8,128)S(1)}, u32[]{:S(2)}, u32[]{:S(2)}) %collective-permute-start.7) | collective-permute-done | bytes 65568 | tf_op jit(solution)/shard_map/ppermute | solution.py:359
  79.0 3.1 %collective-permute-start.9 = (f32[2,8,2,8,128]{4,3,2,1,0:T(8,128)S(1)}, f32[2,8,2,8,128]{4,3,2,1,0:T(8,128)S(1)}, u32[]{:S(2)}, u32[]{:S(2)}) collective-permute-start(f32[2,8,2,8,128]{4,3,2,1,0:T(8,128)S(1)} %pad_maximum_fusion.3.near), channel_id=1, source_target_pairs={{0,1},{1,0},{2,3},{3,2},{4,5},{5,4},{6,7},{7,6},{8,9},{9,8},{10,11... | collective-permute-start | bytes 393224 | tf_op jit(solution)/shard_map/ppermute | solution.py:338
  82.1 1.0 %collective-permute-done.9.swapped = f32[2,8,2,8,128]{4,3,2,1,0:T(8,128)S(1)} collective-permute-done((f32[2,8,2,8,128]{4,3,2,1,0:T(8,128)S(1)}, f32[2,8,2,8,128]{4,3,2,1,0:T(8,128)S(1)}, u32[]{:S(2)}, u32[]{:S(2)}) %collective-permute-start.9) | collective-permute-done | bytes 131104 | tf_op jit(solution)/shard_map/ppermute | solution.py:338
  83.0 3.4 %shard_map.52 = (f32[128,128]{1,0:T(8,128)}, f32[128,128]{1,0:T(8,128)}) custom-call(s32[4]{0:T(128)S(1)} %pad_add_fusion.scal, f32[34,24,128]{2,1,0:T(8,128)S(1)} %get-tuple-element.24.src, f32[34,24,128]{2,1,0:T(8,128)S(1)} %get-tuple-element.25.fbx, f32[34,24,128]{2,1,0:T(8,128)S(1)} %get-tuple-element.26.fby, f32[34,24,128]{2,1,0:T(8,128)S(1)} %get-tuple-element.27.fbz, ...), custom_call_target="tpu_custom_call" | custom-call | tf_op jit(solution)/shard_map/pallas_call | solution.py:326
  (14 shorter events, 0.2 us)
Async XLA Ops:
  0.7 0.9 %copy-start = (f32[8,16,128]{2,1,0:T(8,128)S(1)}, f32[8,16,128]{2,1,0:T(8,128)}, u32[]{:S(2)}) copy-start(f32[8,16,128]{2,1,0:T(8,128)} %param.5) | copy-start | bytes 196612
  0.7 0.9 %copy-start.1 = (f32[8,16,128]{2,1,0:T(8,128)S(1)}, f32[8,16,128]{2,1,0:T(8,128)}, u32[]{:S(2)}) copy-start(f32[8,16,128]{2,1,0:T(8,128)} %param.4) | copy-start | bytes 196612
  1.7 9.1 %collective-permute-start = (f32[3,9,8,128]{3,2,1,0:T(8,128)S(1)}, f32[3,9,8,128]{3,2,1,0:T(8,128)S(1)}, u32[]{:S(2)}, u32[]{:S(2)}) collective-permute-start(f32[3,9,8,128]{3,2,1,0:T(8,128)S(1)} %get-tuple-element.48), channel_id=1, source_target_pairs={{8,16},{24,32},{40,48},{56,64},{72,80},{88,96},{104,112},{120,128}... | collective-permute-start | bytes 331784 | tf_op jit(solution)/shard_map/ppermute | solution.py:386
  8.0 5.5 %collective-permute-start.1 = (f32[3,9,8,128]{3,2,1,0:T(8,128)S(1)}, f32[3,9,8,128]{3,2,1,0:T(8,128)S(1)}, u32[]{:S(2)}, u32[]{:S(2)}) collective-permute-start(f32[3,9,8,128]{3,2,1,0:T(8,128)S(1)} %get-tuple-element.49), channel_id=1, source_target_pairs={{0,8},{16,24},{32,40},{48,56},{64,72},{80,88},{96,104},{112,120},{... | collective-permute-start | bytes 331784 | tf_op jit(solution)/shard_map/ppermute | solution.py:386
  13.5 10.8 %collective-permute-start.3 = (f32[3,34,8,128]{3,2,1,0:T(8,128)S(1)}, f32[3,34,8,128]{3,2,1,0:T(8,128)S(1)}, u32[]{:S(2)}, u32[]{:S(2)}) collective-permute-start(f32[3,34,8,128]{3,2,1,0:T(8,128)S(1)} %pad_maximum_fusion.own), channel_id=1, source_target_pairs={{1,2},{2,1},{3,4},{4,3},{5,6},{6,5},{9,10},{10,9},{11,12},{12,11},... | collective-permute-start | bytes 1253384 | tf_op jit(solution)/shard_map/ppermute | solution.py:392
  18.7 5.7 %collective-permute-start.2 = (f32[3,34,8,128]{3,2,1,0:T(8,128)S(1)}, f32[3,34,8,128]{3,2,1,0:T(8,128)S(1)}, u32[]{:S(2)}, u32[]{:S(2)}) collective-permute-start(f32[3,34,8,128]{3,2,1,0:T(8,128)S(1)} %pad_maximum_fusion.own), channel_id=1, source_target_pairs={{0,1},{1,0},{2,3},{3,2},{4,5},{5,4},{6,7},{7,6},{8,9},{9,8},{10,11... | collective-permute-start | bytes 1253384 | tf_op jit(solution)/shard_map/ppermute | solution.py:338
  37.1 9.8 %collective-permute-start.5 = (f32[8,6,8,128]{3,2,1,0:T(8,128)S(1)}, f32[8,6,8,128]{3,2,1,0:T(8,128)S(1)}, u32[]{:S(2)}, u32[]{:S(2)}) collective-permute-start(f32[8,6,8,128]{3,2,1,0:T(8,128)S(1)} %slice.27.here), channel_id=1, source_target_pairs={{17,1},{19,3},{21,5},{23,7},{25,9},{27,11},{29,13},{31,15},{32,16}... | collective-permute-start | bytes 589832 | tf_op jit(solution)/shard_map/ppermute | solution.py:359
  39.0 13.0 %collective-permute-start.4 = (f32[8,6,8,128]{3,2,1,0:T(8,128)S(1)}, f32[8,6,8,128]{3,2,1,0:T(8,128)S(1)}, u32[]{:S(2)}, u32[]{:S(2)}) collective-permute-start(f32[8,6,8,128]{3,2,1,0:T(8,128)S(1)} %slice.27.here), channel_id=1, source_target_pairs={{8,0},{10,2},{12,4},{14,6},{0,8},{17,9},{2,10},{19,11},{4,12},{21,... | collective-permute-start | bytes 589832 | tf_op jit(solution)/shard_map/ppermute | solution.py:359
  52.1 3.6 %collective-permute-start.6 = (f32[2,8,6,8,128]{4,3,2,1,0:T(8,128)S(1)}, f32[2,8,6,8,128]{4,3,2,1,0:T(8,128)S(1)}, u32[]{:S(2)}, u32[]{:S(2)}) collective-permute-start(f32[2,8,6,8,128]{4,3,2,1,0:T(8,128)S(1)} %pad_maximum_fusion.1.near), channel_id=1, source_target_pairs={{0,1},{1,0},{2,3},{3,2},{4,5},{5,4},{6,7},{7,6},{8,9},{9,8},{10,11... | collective-permute-start | bytes 1179656 | tf_op jit(solution)/shard_map/ppermute | solution.py:338
  68.2 6.2 %collective-permute-start.8 = (f32[8,2,8,128]{3,2,1,0:T(8,128)S(1)}, f32[8,2,8,128]{3,2,1,0:T(8,128)S(1)}, u32[]{:S(2)}, u32[]{:S(2)}) collective-permute-start(f32[8,2,8,128]{3,2,1,0:T(8,128)S(1)} %all_to_all.11.here), channel_id=1, source_target_pairs={{17,1},{19,3},{21,5},{23,7},{25,9},{27,11},{29,13},{31,15},{32,16}... | collective-permute-start | bytes 196616 | tf_op jit(solution)/shard_map/ppermute | solution.py:359
  70.1 8.8 %collective-permute-start.7 = (f32[8,2,8,128]{3,2,1,0:T(8,128)S(1)}, f32[8,2,8,128]{3,2,1,0:T(8,128)S(1)}, u32[]{:S(2)}, u32[]{:S(2)}) collective-permute-start(f32[8,2,8,128]{3,2,1,0:T(8,128)S(1)} %all_to_all.11.here), channel_id=1, source_target_pairs={{8,0},{10,2},{12,4},{14,6},{0,8},{17,9},{2,10},{19,11},{4,12},{21,... | collective-permute-start | bytes 196616 | tf_op jit(solution)/shard_map/ppermute | solution.py:359
  79.0 4.0 %collective-permute-start.9 = (f32[2,8,2,8,128]{4,3,2,1,0:T(8,128)S(1)}, f32[2,8,2,8,128]{4,3,2,1,0:T(8,128)S(1)}, u32[]{:S(2)}, u32[]{:S(2)}) collective-permute-start(f32[2,8,2,8,128]{4,3,2,1,0:T(8,128)S(1)} %pad_maximum_fusion.3.near), channel_id=1, source_target_pairs={{0,1},{1,0},{2,3},{3,2},{4,5},{5,4},{6,7},{7,6},{8,9},{9,8},{10,11... | collective-permute-start | bytes 393224 | tf_op jit(solution)/shard_map/ppermute | solution.py:338

commit v4 on v3

--- a/solution.py
+++ b/solution.py
@@ -12,9 +12,9 @@
 ROWS = 16 + 2 * HALO
 FX = 24
 MROWS = 40
-MX = 32
+MX = 16
 LROWS = 20
-LX = 16
+LX = 8
 VMEM_LIMIT = 40 * 1024 * 1024
 
 F32 = jnp.float32
@@ -40,9 +40,26 @@
     return pltpu.roll(value, by, axis)
 
 
+def next_plane(value):
+    value = up(value, 0, 1)
+    last = value[-8:]
+    last = jnp.where(planes((8, 128)) == 7, up(last, 1, 1), last)
+    return last if value.shape[0] == 8 else jnp.concatenate([value[:-8], last])
+
+
+def previous_plane(value):
+    value = down(value, 0, 1)
+    first = value[:8]
+    first = jnp.where(planes((8, 128)) == 0, down(first, 1, 1), first)
+    return first if value.shape[0] == 8 else jnp.concatenate([first, value[8:]])
+
+
 class Level:
-    def __init__(self, bx, by, bz, diag, inv, width):
+    def __init__(self, bx, by, bz, diag, inv, width, folded):
         self.bx, self.by, self.bz, self.diag, self.inv, self.width = bx, by, bz, diag, inv, width
+        self.folded = folded
+        self.next = next_plane if folded else lambda value: up(value, 0, 1)
+        self.previous = previous_plane if folded else lambda value: down(value, 0, 1)
 
     def beside(self, u_ref, y, n):
         u = [u_ref[y - 1 + t] for t in range(n + 2)]
@@ -51,7 +68,7 @@
         acc = []
         for t in range(n):
             here, bx, bz = u[t + 1], self.bx[y + t], self.bz[y + t]
-            x = bx * up(here, 0, 1) + down(bx * here, 0, 1)
+            x = bx * self.next(here) + self.previous(bx * here)
             z = bz * up(here, 1, self.width) + down(bz * here, 1, self.width)
             acc.append((by[t] * u[t] + by[t + 1] * u[t + 2]) + (x + z))
         return u[1:-1], acc
@@ -69,25 +86,27 @@
         u, acc = self.beside(u_ref, y, n)
         return [rhs[y + t] - self.diag[y + t] * u[t] + acc[t] for t in range(n)]
 
-    def build(self, conduct, absorb, lo, hi, spacing, closed):
+    def build(self, conduct, absorb, lo, hi, spacing):
         shape = conduct.shape[1:]
         z, x = lanes(shape), planes(shape)
         half = 0.5 / spacing
+        final = jnp.logical_and(x == shape[0] - 1, z % 2 == 1)
+        initial = jnp.logical_and(x == 0, z % 2 == 0)
 
         def body(y, n):
             c = [conduct[y - 1 + t] for t in range(n + 2)]
             done = []
             for t in range(n):
                 here = c[t + 1]
-                xp, xm = up(here, 0, 1), down(here, 0, 1)
-                if closed:
-                    xp = jnp.where(x == shape[0] - 1, 0.0, xp)
-                    xm = jnp.where(x == 0, 0.0, xm)
+                xp, xm = self.next(here), self.previous(here)
+                if self.folded:
+                    xp = jnp.where(final, 0.0, xp)
+                    xm = jnp.where(initial, 0.0, xm)
                 zp = jnp.where(z >= shape[1] - self.width, 0.0, up(here, 1, self.width))
                 zm = jnp.where(z < self.width, 0.0, down(here, 1, self.width))
                 bx = (here + xp) * half
-                if closed:
-                    bx = jnp.where(x == shape[0] - 1, 0.0, bx)
+                if self.folded:
+                    bx = jnp.where(final, 0.0, bx)
                 by = (here + c[t + 2]) * half
                 bz = jnp.where(z >= shape[1] - self.width, 0.0, (here + zp) * half)
                 a = absorb[y + t]
@@ -149,23 +168,29 @@
     rows(lo, hi, body)
 
 
-def fine_kernel(scal, own, via_a, via_b,
-                src, bx, by, bz, diag, inv, u1, pack, ends,
-                absorb, conduct, u2):
+def join_planes(scal, own, via_a, via_b, arr, dst, lo, hi):
     even = scal[0] == 0
-
-    def join(y, n):
-        for t in range(n):
-            for arr, dst in ((0, src), (1, absorb), (2, conduct)):
-                a, b = via_a[arr, y + t], via_b[arr, y + t]
-                dst[y + t, 0:8, :] = jnp.where(even, b, a)
-                dst[y + t, 8:16, :] = own[arr, y + t]
-                dst[y + t, 16:24, :] = jnp.where(even, a, b)
-
-    rows(0, ROWS, join)
-    level = Level(bx, by, bz, diag, inv, 1)
-    level.build(conduct, absorb, 1, ROWS - 1, 1.0, False)
-    scale(u1, inv, src, 1, ROWS - 1)
+    for y in range(lo, hi):
+        a, b = via_a[arr, y], via_b[arr, y]
+        dst[y, 0:8, :] = jnp.where(even, b, a)
+        dst[y, 8:16, :] = own[arr, y]
+        dst[y, 16:24, :] = jnp.where(even, a, b)
+
+
+def first_kernel(scal, own, near_a, near_b, pack, ends,
+                 src, absorb, conduct, bx, by, bz, diag, inv, u1, u2):
+    even = scal[0] == 0
+    for arr, dst in ((0, src), (1, absorb), (2, conduct)):
+        for i in range(22):
+            y = HALO - 3 + i
+            a, b = near_a[arr, i // 2], near_b[arr, i // 2]
+            left, right = jnp.where(even, b, a), jnp.where(even, a, b)
+            dst[y, 0:8, :] = down(left, 0, 4) if i % 2 == 0 else left
+            dst[y, 8:16, :] = own[arr, y]
+            dst[y, 16:24, :] = right if i % 2 == 0 else down(right, 0, 4)
+    level = Level(bx, by, bz, diag, inv, 1, False)
+    level.build(conduct, absorb, HALO - 2, ROWS - HALO + 2, 1.0)
+    scale(u1, inv, src, HALO - 2, ROWS - HALO + 2)
     for y in range(16):
         for i, x in enumerate((8, 15)):
             ends[i, y:y + 1, :] = u1[HALO + y, x:x + 1, :]
@@ -177,6 +202,28 @@
         pack[i] = t
 
 
+def rim_kernel(scal, own, via_a, via_b, ends,
+               src, bx, by, bz, diag, inv, u2,
+               absorb, conduct, u1):
+    for arr, dst in ((0, src), (1, absorb), (2, conduct)):
+        join_planes(scal, own, via_a, via_b, arr, dst, 0, ROWS)
+    level = Level(bx, by, bz, diag, inv, 1, False)
+    level.build(conduct, absorb, 1, ROWS - 1, 1.0)
+    x = planes((FX, 128))
+    dev = scal[1]
+    left, right = jnp.maximum(dev - 1, 0), jnp.minimum(dev + 1, 7)
+    for y in range(1, ROWS - 1):
+        u = inv[y] * src[y]
+        if 0 <= y - HALO < 16:
+            at = pl.ds(y - HALO, 1)
+            u = jnp.where(x == 0, ends[left, at, :], jnp.where(x == FX - 1, ends[right, at, :], u))
+        u1[y] = u
+    zero = jnp.zeros((FX, 128), F32)
+    for y in (0, 1, ROWS - 2, ROWS - 1):
+        u2[y] = zero
+    level.sweep(u2, u1, src, 2, ROWS - 2)
+
+
 def gather_rows(scal, here, near, swapped, joined, arrays):
     def copy(j, source):
         for t in range(2 * arrays):
@@ -205,10 +252,11 @@
     for j in range(5):
         for k in range(2):
             for a in range(2):
-                v = joined[j, tile + k, pl.ds(a, MX, stride=2), :]
+                v = joined[j, tile + k, pl.ds(a, 2 * MX, stride=2), :]
+                v, w = v[:MX], v[MX:]
                 y = j * 8 + 4 * k + 2 * a
-                dst[y] = jnp.where(z, v, down(v, 1, 1))
-                dst[y + 1] = jnp.where(z, up(v, 1, 1), v)
+                dst[y] = jnp.where(z, v, down(w, 1, 1))
+                dst[y + 1] = jnp.where(z, up(v, 1, 1), w)
 
 
 def coarse(mid, low, rhs, m1, m2, lrhs, l1, l2, tmp, k):
@@ -234,14 +282,17 @@
 def prolong_add(scal, m2, wide, u_ref, dst, lo, hi):
     begin = pl.multiple_of(scal[1] * 8, 8)
     zero = jnp.zeros((8, 128), F32)
+    z = lanes((MX, 128)) % 2 == 0
 
     def body(m, n):
         for t in range(n):
             v = m2[m + t]
+            low, high = jnp.where(z, v, down(v, 1, 1)), jnp.where(z, up(v, 1, 1), v)
             wide[m + t, 0:8, :] = zero
             wide[m + t, 72:80, :] = zero
-            wide[m + t, pl.ds(8, MX, stride=2), :] = v
-            wide[m + t, pl.ds(9, MX, stride=2), :] = v
+            for a in range(2):
+                wide[m + t, pl.ds(8 + a, MX, stride=2), :] = low
+                wide[m + t, pl.ds(40 + a, MX, stride=2), :] = high
 
     rows(lo, hi, body)
 
@@ -257,39 +308,26 @@
     rows(lo, hi, add)
 
 
-def middle_kernel(scal, src, fbx, fby, fbz, fdiag, finv, u1, ends, here, near, swapped,
+def middle_kernel(scal, src, fbx, fby, fbz, fdiag, finv, u2, here, near, swapped,
                   mbx, mby, mbz, mdiag, minv, lbx, lby, lbz, linv, u2_out, pack,
                   joined, rhs, absorb, conduct, m1, m2, lrhs, l1, l2, labsorb, lconduct, tmp, wide, fa, fb):
-    fine = Level(fbx, fby, fbz, fdiag, finv, 1)
-    mid = Level(mbx, mby, mbz, mdiag, minv, 2)
-    low = Level(lbx, lby, lbz, None, linv, 4)
+    fine = Level(fbx, fby, fbz, fdiag, finv, 1, False)
+    mid = Level(mbx, mby, mbz, mdiag, minv, 2, True)
+    low = Level(lbx, lby, lbz, None, linv, 4, True)
     gather_rows(scal, here, near, swapped, joined, 3)
     unpack_rows(joined, 0, rhs)
     unpack_rows(joined, 2, absorb)
     unpack_rows(joined, 4, conduct)
-    mid.build(conduct, absorb, 2, 38, 4.0, True)
+    mid.build(conduct, absorb, 2, 38, 4.0)
     restrict_low(lambda y, n: [absorb[y + t] for t in range(n)], tmp, labsorb, 1, 19)
     restrict_low(lambda y, n: [conduct[y + t] for t in range(n)], tmp, lconduct, 1, 19)
-    low.build(lconduct, labsorb, 2, 18, 16.0, True)
+    low.build(lconduct, labsorb, 2, 18, 16.0)
     coarse(mid, low, rhs, m1, m2, lrhs, l1, l2, tmp, 0)
-    x = planes((FX, 128))
-    dev = scal[1]
-    left, right = jnp.maximum(dev - 1, 0), jnp.minimum(dev + 1, 7)
-
-    for y in range(1, ROWS - 1):
-        u = u1[y]
-        if 0 <= y - HALO < 16:
-            at = pl.ds(y - HALO, 1)
-            u = jnp.where(x == 0, ends[left, at, :], jnp.where(x == FX - 1, ends[right, at, :], u))
-        fa[y] = u
-    zero = jnp.zeros((FX, 128), F32)
-    for y in (0, 1, ROWS - 2, ROWS - 1):
-        fb[y] = zero
-    fine.sweep(fb, fa, src, 2, ROWS - 2)
-    prolong_add(scal, m2, wide, fb, fa, 12, 28)
+    prolong_add(scal, m2, wide, u2, fa, 12, 28)
     fine.sweep(fb, fa, src, 3, ROWS - 3)
     fine.sweep(fa, fb, src, 4, ROWS - 4)
     fine.sweep(fb, fa, src, 5, ROWS - 5)
+    zero = jnp.zeros((FX, 128), F32)
     for y in (*range(6), *range(ROWS - 6, ROWS)):
         u2_out[y] = zero
     fine.sweep(u2_out, fb, src, 6, ROWS - 6)
@@ -302,9 +340,9 @@
                 mbx, mby, mbz, mdiag, minv, lbx, lby, lbz, linv,
                 out, out_res,
                 joined, rhs, m1, m2, lrhs, l1, l2, tmp, wide, fa, fb):
-    fine = Level(fbx, fby, fbz, fdiag, finv, 1)
-    mid = Level(mbx, mby, mbz, mdiag, minv, 2)
-    low = Level(lbx, lby, lbz, None, linv, 4)
+    fine = Level(fbx, fby, fbz, fdiag, finv, 1, False)
+    mid = Level(mbx, mby, mbz, mdiag, minv, 2, True)
+    low = Level(lbx, lby, lbz, None, linv, 4, True)
     gather_rows(scal, here, near, swapped, joined, 1)
     unpack_rows(joined, 0, rhs)
     coarse(mid, low, rhs, m1, m2, lrhs, l1, l2, tmp, 1)
@@ -389,18 +427,24 @@
     two = swap_rows(jnp.where(even, first, last), 1)
     before, after = jnp.where(even, two, one), jnp.where(even, one, two)
     fine = jnp.concatenate([before, fine, after], axis=1)
-    via_b = lax.ppermute(fine, "dev", [(1, 2), (2, 1), (3, 4), (4, 3), (5, 6), (6, 5)])
-    via_a = other_core(fine)
+
+    def other_chip(array):
+        return lax.ppermute(array, "dev", [(1, 2), (2, 1), (3, 4), (4, 3), (5, 6), (6, 5)])
+
+    one, two = fine[:, HALO - 3:ROWS - HALO + 3:2], fine[:, HALO - 2:ROWS - HALO + 3:2]
+    near = [jnp.concatenate([one[:, :, x:x + 4], two[:, :, x:x + 4]], axis=2) for x in (0, 4)]
+    near_a = other_core(jnp.where(core == 0, near[1], near[0]))
+    near_b = other_chip(jnp.where(core == 0, near[0], near[1]))
+    via_a, via_b = other_core(fine), other_chip(fine)
     block, wide_mid, wide_low = (ROWS, FX, 128), (MROWS, MX, 128), (LROWS, LX, 128)
-    *state, u1, pack, ends = call(
-        fine_kernel, [block] * 7 + [(6, 8, 128), (2, 16, 128)], [block] * 3, scal, fine, via_a, via_b
-    )
+    pack, ends = call(first_kernel, [(6, 8, 128), (2, 16, 128)], [block] * 10, scal, fine, near_a, near_b)
     ends, *parts = spread(pack, ends)
+    *state, u2 = call(rim_kernel, [block] * 7, [block] * 3, scal, fine, via_a, via_b, ends)
     *coefs, u2, pack = call(
         middle_kernel,
         [wide_mid] * 5 + [wide_low] * 4 + [block, (2, 8, 128)],
         [(5, 6, 64, 128)] + [wide_mid] * 5 + [wide_low] * 5 + [(20, MX, 128), (MROWS, 80, 128), block, block],
-        scal, *state, u1, ends, *parts,
+        scal, *state, u2, *parts,
     )
     _, *parts = spread(pack)
     out, res = call(

time: 86.9 us -> 82.2 us (0.946)
  the two profiles are of different devices: /device:TPU:513 before, /device:TPU:521 now
where the time goes in v4:
time: 82.2 us; the launch traced here: 81.7 us
  starting transfers between devices  45.4 us (55%)
  blocking collectives  18.5 us (23%)
  Pallas kernels  9 us (11%)
  waiting for transfers between devices  6.28 us (8%)
  local copies, waits for them, and re-layouts  1.06 us (1%)
  between operations  1.03 us (1%)
    all_to_all x2, blocking collectives, spread(): here = lax.all_to_all(here, 'dev', 0, 0)  18.5 us
    ppermute x4, starting transfers between devices, other_core(): return lax.ppermute(array, 'dev', [(i, i ^ 1) for i in range(8)])  15.3 us
    ppermute x4, starting transfers between devices, from_beside(): return lax.ppermute(array, ('grp', 'dev'), pairs)  12.9 us
    pallas_call x4, Pallas kernels, call(): pl.pallas_call(kernel, out_shape=[jax.ShapeDtypeStruct(s, F32) for s in o...  9 us
    ppermute x2, starting transfers between devices, other_chip(): lax.ppermute(array, 'dev', [(1, 2), (2, 1), (3, 4), (4, 3), (5, 6), (6, 5)])  8.9 us
    ppermute x2, starting transfers between devices, swap_rows(): return lax.ppermute(array, 'grp', pairs + [(j, i) for i, j in pairs])  8.37 us
    ppermute x2, waiting for transfers between devices, swap_rows(): return lax.ppermute(array, 'grp', pairs + [(j, i) for i, j in pairs])  2.43 us
  transfers between devices with their start and end apart: 12, of which 5 were waited for; matrix products, arithmetic and copies ran while one was open for 0% of the time, Pallas kernels for 2%

profile of v4, /device:TPU:521, one launch (start us, length us, event | category | flops | bytes accessed | tf_op | source)
XLA Modules:
  0.0 81.7 jit_solution(17173539982011989421)
XLA Ops:
  0.7 0.9 %copy.11 = f32[8,16,128]{2,0,1:T(8,128)S(1)} copy(f32[8,16,128]{2,1,0:T(8,128)} %param.3) | data formatting | bytes 131072 | tf_op args[0]
  1.7 3.2 %collective-permute-start = (f32[3,9,8,128]{3,2,1,0:T(8,128)S(1)}, f32[3,9,8,128]{3,2,1,0:T(8,128)S(1)}, u32[]{:S(2)}, u32[]{:S(2)}) collective-permute-start(f32[3,9,8,128]{3,2,1,0:T(8,128)S(1)} %get-tuple-element.52), channel_id=1, source_target_pairs={{8,16},{24,32},{40,48},{56,64},{72,80},{88,96},{104,112},{120,128}... | collective-permute-start | bytes 331784 | tf_op jit(solution)/shard_map/ppermute | solution.py:424
  4.9 5.2 %collective-permute-start.1 = (f32[3,9,8,128]{3,2,1,0:T(8,128)S(1)}, f32[3,9,8,128]{3,2,1,0:T(8,128)S(1)}, u32[]{:S(2)}, u32[]{:S(2)}) collective-permute-start(f32[3,9,8,128]{3,2,1,0:T(8,128)S(1)} %get-tuple-element.53), channel_id=1, source_target_pairs={{0,8},{16,24},{32,40},{48,56},{64,72},{80,88},{96,104},{112,120},{... | collective-permute-start | bytes 331784 | tf_op jit(solution)/shard_map/ppermute | solution.py:424
  10.1 0.0 collective-permute-done
  10.1 2.4 %collective-permute-done.1 = f32[3,9,8,128]{3,2,1,0:T(8,128)S(1)} collective-permute-done((f32[3,9,8,128]{3,2,1,0:T(8,128)S(1)}, f32[3,9,8,128]{3,2,1,0:T(8,128)S(1)}, u32[]{:S(2)}, u32[]{:S(2)}) %collective-permute-start.1) | collective-permute-done | bytes 110624 | tf_op jit(solution)/shard_map/ppermute | solution.py:424
  12.7 0.1 fusion
  12.8 4.6 %collective-permute-start.5 = (f32[3,11,8,128]{3,2,1,0:T(8,128)S(1)}, f32[3,11,8,128]{3,2,1,0:T(8,128)S(1)}, u32[]{:S(2)}, u32[]{:S(2)}) collective-permute-start(f32[3,11,8,128]{3,2,1,0:T(8,128)S(1)} %get-tuple-element.48), channel_id=1, source_target_pairs={{1,2},{2,1},{3,4},{4,3},{5,6},{6,5},{9,10},{10,9},{11,12},{12,11},... | collective-permute-start | bytes 405512 | tf_op jit(solution)/shard_map/ppermute | solution.py:432
  17.3 1.9 %collective-permute-start.4 = (f32[3,11,8,128]{3,2,1,0:T(8,128)S(1)}, f32[3,11,8,128]{3,2,1,0:T(8,128)S(1)}, u32[]{:S(2)}, u32[]{:S(2)}) collective-permute-start(f32[3,11,8,128]{3,2,1,0:T(8,128)S(1)} %get-tuple-element.49), channel_id=1, source_target_pairs={{0,1},{1,0},{2,3},{3,2},{4,5},{5,4},{6,7},{7,6},{8,9},{9,8},{10,11... | collective-permute-start | bytes 405512 | tf_op jit(solution)/shard_map/ppermute | solution.py:376
  19.3 0.1 pad_add_fusion.scal
  19.4 0.6 collective-permute-done.5.near_b
  20.0 0.6 collective-permute-done.4.near_a
  20.6 1.2 %shard_map.50 = (f32[6,8,128]{2,1,0:T(8,128)S(1)}, f32[2,16,128]{2,1,0:T(8,128)S(1)}) custom-call(s32[4]{0:T(128)S(1)} %pad_add_fusion.scal, f32[3,34,8,128]{3,2,1,0:T(8,128)S(1)} %pad_maximum_fusion.own, f32[3,11,8,128]{3,2,1,0:T(8,128)S(1)} %collective-permute-done.4.near_a, f32[3,11,8,128]{3,2,1,0:T(8,128)S(1)} %collective-permute-done.5.near_b), custom_call_target="tpu_custom_call" | custom-call | tf_op jit(solution)/shard_map/pallas_call | solution.py:364
  21.7 0.1 broadcast_select_fusion.2
  21.9 10.7 %all_to_all.10 = f32[8,8,8,128]{3,2,1,0:T(8,128)S(1)} all-to-all(f32[8,8,8,128]{3,2,1,0:T(8,128)S(1)} %pad_maximum_fusion.2), channel_id=1, replica_groups=mesh['grp'=96,'dev'=8] {'dev'}, dimensions={0} | all-to-all | bytes 524288 | tf_op jit(solution)/shard_map/all_to_all | solution.py:404
  32.5 3.9 %collective-permute-start.7 = (f32[8,6,8,128]{3,2,1,0:T(8,128)S(1)}, f32[8,6,8,128]{3,2,1,0:T(8,128)S(1)}, u32[]{:S(2)}, u32[]{:S(2)}) collective-permute-start(f32[8,6,8,128]{3,2,1,0:T(8,128)S(1)} %slice.55.here), channel_id=1, source_target_pairs={{17,1},{19,3},{21,5},{23,7},{25,9},{27,11},{29,13},{31,15},{32,16}... | collective-permute-start | bytes 589832 | tf_op jit(solution)/shard_map/ppermute | solution.py:397
  36.4 2.8 %collective-permute-start.6 = (f32[8,6,8,128]{3,2,1,0:T(8,128)S(1)}, f32[8,6,8,128]{3,2,1,0:T(8,128)S(1)}, u32[]{:S(2)}, u32[]{:S(2)}) collective-permute-start(f32[8,6,8,128]{3,2,1,0:T(8,128)S(1)} %slice.55.here), channel_id=1, source_target_pairs={{8,0},{10,2},{12,4},{14,6},{0,8},{17,9},{2,10},{19,11},{4,12},{21,... | collective-permute-start | bytes 589832 | tf_op jit(solution)/shard_map/ppermute | solution.py:397
  39.2 4.3 %collective-permute-start.3 = (f32[3,34,8,128]{3,2,1,0:T(8,128)S(1)}, f32[3,34,8,128]{3,2,1,0:T(8,128)S(1)}, u32[]{:S(2)}, u32[]{:S(2)}) collective-permute-start(f32[3,34,8,128]{3,2,1,0:T(8,128)S(1)} %pad_maximum_fusion.own), channel_id=1, source_target_pairs={{1,2},{2,1},{3,4},{4,3},{5,6},{6,5},{9,10},{10,9},{11,12},{12,11},... | collective-permute-start | bytes 1253384 | tf_op jit(solution)/shard_map/ppermute | solution.py:432
  43.6 1.9 %collective-permute-start.2 = (f32[3,34,8,128]{3,2,1,0:T(8,128)S(1)}, f32[3,34,8,128]{3,2,1,0:T(8,128)S(1)}, u32[]{:S(2)}, u32[]{:S(2)}) collective-permute-start(f32[3,34,8,128]{3,2,1,0:T(8,128)S(1)} %pad_maximum_fusion.own), channel_id=1, source_target_pairs={{0,1},{1,0},{2,3},{3,2},{4,5},{5,4},{6,7},{7,6},{8,9},{9,8},{10,11... | collective-permute-start | bytes 1253384 | tf_op jit(solution)/shard_map/ppermute | solution.py:376
  45.5 0.0 collective-permute-done.7
  45.5 0.0 collective-permute-done.6
  45.6 4.4 %collective-permute-start.8 = (f32[2,8,6,8,128]{4,3,2,1,0:T(8,128)S(1)}, f32[2,8,6,8,128]{4,3,2,1,0:T(8,128)S(1)}, u32[]{:S(2)}, u32[]{:S(2)}) collective-permute-start(f32[2,8,6,8,128]{4,3,2,1,0:T(8,128)S(1)} %pad_maximum_fusion.1.near), channel_id=1, source_target_pairs={{0,1},{1,0},{2,3},{3,2},{4,5},{5,4},{6,7},{7,6},{8,9},{9,8},{10,11... | collective-permute-start | bytes 1179656 | tf_op jit(solution)/shard_map/ppermute | solution.py:376
  50.0 0.0 collective-permute-done.3.via_b
  50.1 1.2 %shard_map.51 = (f32[34,24,128]{2,1,0:T(8,128)S(1)}, f32[34,24,128]{2,1,0:T(8,128)S(1)}, f32[34,24,128]{2,1,0:T(8,128)S(1)}, f32[34,24,128]{2,1,0:T(8,128)S(1)},...) custom-call(s32[4]{0:T(128)S(1)} %pad_add_fusion.scal, ...), custom_call_target="tpu_custom_call" | custom-call | tf_op jit(solution)/shard_map/pallas_call | solution.py:364
  51.3 0.1 collective-permute-done.8.swapped
  51.4 3.7 %shard_map.52 = (f32[40,16,128]{2,1,0:T(8,128)S(1)}, f32[40,16,128]{2,1,0:T(8,128)S(1)}, f32[40,16,128]{2,1,0:T(8,128)S(1)}, f32[40,16,128]{2,1,0:T(8,128)S(1)},...) custom-call(s32[4]{0:T(128)S(1)} %pad_add_fusion.scal, ...), custom_call_target="tpu_custom_call" | custom-call | tf_op jit(solution)/shard_map/pallas_call | solution.py:364
  55.1 7.9 %all_to_all.11.here = f32[8,2,8,128]{3,2,1,0:T(8,128)S(1)} all-to-all(f32[8,2,8,128]{3,2,1,0:T(8,128)S(1)} %broadcast_in_dim.33), channel_id=1, replica_groups=mesh['grp'=96,'dev'=8] {'dev'}, dimensions={0} | all-to-all | bytes 131072 | tf_op jit(solution)/shard_map/all_to_all | solution.py:404
  62.9 1.9 %collective-permute-start.10 = (f32[8,2,8,128]{3,2,1,0:T(8,128)S(1)}, f32[8,2,8,128]{3,2,1,0:T(8,128)S(1)}, u32[]{:S(2)}, u32[]{:S(2)}) collective-permute-start(f32[8,2,8,128]{3,2,1,0:T(8,128)S(1)} %all_to_all.11.here), channel_id=1, source_target_pairs={{17,1},{19,3},{21,5},{23,7},{25,9},{27,11},{29,13},{31,15},{32,16}... | collective-permute-start | bytes 196616 | tf_op jit(solution)/shard_map/ppermute | solution.py:397
  64.8 4.3 %collective-permute-start.9 = (f32[8,2,8,128]{3,2,1,0:T(8,128)S(1)}, f32[8,2,8,128]{3,2,1,0:T(8,128)S(1)}, u32[]{:S(2)}, u32[]{:S(2)}) collective-permute-start(f32[8,2,8,128]{3,2,1,0:T(8,128)S(1)} %all_to_all.11.here), channel_id=1, source_target_pairs={{8,0},{10,2},{12,4},{14,6},{0,8},{17,9},{2,10},{19,11},{4,12},{21,... | collective-permute-start | bytes 196616 | tf_op jit(solution)/shard_map/ppermute | solution.py:397
  69.1 1.6 %collective-permute-done.9 = f32[8,2,8,128]{3,2,1,0:T(8,128)S(1)} collective-permute-done((f32[8,2,8,128]{3,2,1,0:T(8,128)S(1)}, f32[8,2,8,128]{3,2,1,0:T(8,128)S(1)}, u32[]{:S(2)}, u32[]{:S(2)}) %collective-permute-start.9) | collective-permute-done | bytes 65568 | tf_op jit(solution)/shard_map/ppermute | solution.py:397
  70.8 7.0 %collective-permute-start.11 = (f32[2,8,2,8,128]{4,3,2,1,0:T(8,128)S(1)}, f32[2,8,2,8,128]{4,3,2,1,0:T(8,128)S(1)}, u32[]{:S(2)}, u32[]{:S(2)}) collective-permute-start(f32[2,8,2,8,128]{4,3,2,1,0:T(8,128)S(1)} %pad_maximum_fusion.5.near), channel_id=1, source_target_pairs={{0,1},{1,0},{2,3},{3,2},{4,5},{5,4},{6,7},{7,6},{8,9},{9,8},{10,11... | collective-permute-start | bytes 393224 | tf_op jit(solution)/shard_map/ppermute | solution.py:376
  77.8 1.0 %collective-permute-done.11.swapped = f32[2,8,2,8,128]{4,3,2,1,0:T(8,128)S(1)} collective-permute-done((f32[2,8,2,8,128]{4,3,2,1,0:T(8,128)S(1)}, f32[2,8,2,8,128]{4,3,2,1,0:T(8,128)S(1)}, u32[]{:S(2)}, u32[]{:S(2)}) %collective-permute-start.11) | collective-permute-done | bytes 131104 | tf_op jit(solution)/shard_map/ppermute | solution.py:376
  78.8 2.9 %shard_map.53 = (f32[128,128]{1,0:T(8,128)}, f32[128,128]{1,0:T(8,128)}) custom-call(s32[4]{0:T(128)S(1)} %pad_add_fusion.scal, f32[34,24,128]{2,1,0:T(8,128)S(1)} %get-tuple-element.26.src, f32[34,24,128]{2,1,0:T(8,128)S(1)} %get-tuple-element.27.fbx, f32[34,24,128]{2,1,0:T(8,128)S(1)} %get-tuple-element.28.fby, f32[34,24,128]{2,1,0:T(8,128)S(1)} %get-tuple-element.29.fbz, ...), custom_call_target="tpu_custom_call" | custom-call | tf_op jit(solution)/shard_map/pallas_call | solution.py:364
  (23 shorter events, 0.3 us)
Async XLA Ops:
  0.7 0.9 %copy-start = (f32[8,16,128]{2,1,0:T(8,128)S(1)}, f32[8,16,128]{2,1,0:T(8,128)}, u32[]{:S(2)}) copy-start(f32[8,16,128]{2,1,0:T(8,128)} %param.5) | copy-start | bytes 196612
  0.7 0.9 %copy-start.1 = (f32[8,16,128]{2,1,0:T(8,128)S(1)}, f32[8,16,128]{2,1,0:T(8,128)}, u32[]{:S(2)}) copy-start(f32[8,16,128]{2,1,0:T(8,128)} %param.4) | copy-start | bytes 196612
  1.7 8.4 %collective-permute-start = (f32[3,9,8,128]{3,2,1,0:T(8,128)S(1)}, f32[3,9,8,128]{3,2,1,0:T(8,128)S(1)}, u32[]{:S(2)}, u32[]{:S(2)}) collective-permute-start(f32[3,9,8,128]{3,2,1,0:T(8,128)S(1)} %get-tuple-element.52), channel_id=1, source_target_pairs={{8,16},{24,32},{40,48},{56,64},{72,80},{88,96},{104,112},{120,128}... | collective-permute-start | bytes 331784 | tf_op jit(solution)/shard_map/ppermute | solution.py:424
  4.9 7.6 %collective-permute-start.1 = (f32[3,9,8,128]{3,2,1,0:T(8,128)S(1)}, f32[3,9,8,128]{3,2,1,0:T(8,128)S(1)}, u32[]{:S(2)}, u32[]{:S(2)}) collective-permute-start(f32[3,9,8,128]{3,2,1,0:T(8,128)S(1)} %get-tuple-element.53), channel_id=1, source_target_pairs={{0,8},{16,24},{32,40},{48,56},{64,72},{80,88},{96,104},{112,120},{... | collective-permute-start | bytes 331784 | tf_op jit(solution)/shard_map/ppermute | solution.py:424
  12.8 7.2 %collective-permute-start.5 = (f32[3,11,8,128]{3,2,1,0:T(8,128)S(1)}, f32[3,11,8,128]{3,2,1,0:T(8,128)S(1)}, u32[]{:S(2)}, u32[]{:S(2)}) collective-permute-start(f32[3,11,8,128]{3,2,1,0:T(8,128)S(1)} %get-tuple-element.48), channel_id=1, source_target_pairs={{1,2},{2,1},{3,4},{4,3},{5,6},{6,5},{9,10},{10,9},{11,12},{12,11},... | collective-permute-start | bytes 405512 | tf_op jit(solution)/shard_map/ppermute | solution.py:432
  17.3 3.2 %collective-permute-start.4 = (f32[3,11,8,128]{3,2,1,0:T(8,128)S(1)}, f32[3,11,8,128]{3,2,1,0:T(8,128)S(1)}, u32[]{:S(2)}, u32[]{:S(2)}) collective-permute-start(f32[3,11,8,128]{3,2,1,0:T(8,128)S(1)} %get-tuple-element.49), channel_id=1, source_target_pairs={{0,1},{1,0},{2,3},{3,2},{4,5},{5,4},{6,7},{7,6},{8,9},{9,8},{10,11... | collective-permute-start | bytes 405512 | tf_op jit(solution)/shard_map/ppermute | solution.py:376
  32.5 13.0 %collective-permute-start.7 = (f32[8,6,8,128]{3,2,1,0:T(8,128)S(1)}, f32[8,6,8,128]{3,2,1,0:T(8,128)S(1)}, u32[]{:S(2)}, u32[]{:S(2)}) collective-permute-start(f32[8,6,8,128]{3,2,1,0:T(8,128)S(1)} %slice.55.here), channel_id=1, source_target_pairs={{17,1},{19,3},{21,5},{23,7},{25,9},{27,11},{29,13},{31,15},{32,16}... | collective-permute-start | bytes 589832 | tf_op jit(solution)/shard_map/ppermute | solution.py:397
  36.4 9.1 %collective-permute-start.6 = (f32[8,6,8,128]{3,2,1,0:T(8,128)S(1)}, f32[8,6,8,128]{3,2,1,0:T(8,128)S(1)}, u32[]{:S(2)}, u32[]{:S(2)}) collective-permute-start(f32[8,6,8,128]{3,2,1,0:T(8,128)S(1)} %slice.55.here), channel_id=1, source_target_pairs={{8,0},{10,2},{12,4},{14,6},{0,8},{17,9},{2,10},{19,11},{4,12},{21,... | collective-permute-start | bytes 589832 | tf_op jit(solution)/shard_map/ppermute | solution.py:397
  39.2 10.8 %collective-permute-start.3 = (f32[3,34,8,128]{3,2,1,0:T(8,128)S(1)}, f32[3,34,8,128]{3,2,1,0:T(8,128)S(1)}, u32[]{:S(2)}, u32[]{:S(2)}) collective-permute-start(f32[3,34,8,128]{3,2,1,0:T(8,128)S(1)} %pad_maximum_fusion.own), channel_id=1, source_target_pairs={{1,2},{2,1},{3,4},{4,3},{5,6},{6,5},{9,10},{10,9},{11,12},{12,11},... | collective-permute-start | bytes 1253384 | tf_op jit(solution)/shard_map/ppermute | solution.py:432
  43.6 6.5 %collective-permute-start.2 = (f32[3,34,8,128]{3,2,1,0:T(8,128)S(1)}, f32[3,34,8,128]{3,2,1,0:T(8,128)S(1)}, u32[]{:S(2)}, u32[]{:S(2)}) collective-permute-start(f32[3,34,8,128]{3,2,1,0:T(8,128)S(1)} %pad_maximum_fusion.own), channel_id=1, source_target_pairs={{0,1},{1,0},{2,3},{3,2},{4,5},{5,4},{6,7},{7,6},{8,9},{9,8},{10,11... | collective-permute-start | bytes 1253384 | tf_op jit(solution)/shard_map/ppermute | solution.py:376
  45.6 5.8 %collective-permute-start.8 = (f32[2,8,6,8,128]{4,3,2,1,0:T(8,128)S(1)}, f32[2,8,6,8,128]{4,3,2,1,0:T(8,128)S(1)}, u32[]{:S(2)}, u32[]{:S(2)}) collective-permute-start(f32[2,8,6,8,128]{4,3,2,1,0:T(8,128)S(1)} %pad_maximum_fusion.1.near), channel_id=1, source_target_pairs={{0,1},{1,0},{2,3},{3,2},{4,5},{5,4},{6,7},{7,6},{8,9},{9,8},{10,11... | collective-permute-start | bytes 1179656 | tf_op jit(solution)/shard_map/ppermute | solution.py:376
  62.9 6.2 %collective-permute-start.10 = (f32[8,2,8,128]{3,2,1,0:T(8,128)S(1)}, f32[8,2,8,128]{3,2,1,0:T(8,128)S(1)}, u32[]{:S(2)}, u32[]{:S(2)}) collective-permute-start(f32[8,2,8,128]{3,2,1,0:T(8,128)S(1)} %all_to_all.11.here), channel_id=1, source_target_pairs={{17,1},{19,3},{21,5},{23,7},{25,9},{27,11},{29,13},{31,15},{32,16}... | collective-permute-start | bytes 196616 | tf_op jit(solution)/shard_map/ppermute | solution.py:397
  64.8 5.9 %collective-permute-start.9 = (f32[8,2,8,128]{3,2,1,0:T(8,128)S(1)}, f32[8,2,8,128]{3,2,1,0:T(8,128)S(1)}, u32[]{:S(2)}, u32[]{:S(2)}) collective-permute-start(f32[8,2,8,128]{3,2,1,0:T(8,128)S(1)} %all_to_all.11.here), channel_id=1, source_target_pairs={{8,0},{10,2},{12,4},{14,6},{0,8},{17,9},{2,10},{19,11},{4,12},{21,... | collective-permute-start | bytes 196616 | tf_op jit(solution)/shard_map/ppermute | solution.py:397
  70.8 8.0 %collective-permute-start.11 = (f32[2,8,2,8,128]{4,3,2,1,0:T(8,128)S(1)}, f32[2,8,2,8,128]{4,3,2,1,0:T(8,128)S(1)}, u32[]{:S(2)}, u32[]{:S(2)}) collective-permute-start(f32[2,8,2,8,128]{4,3,2,1,0:T(8,128)S(1)} %pad_maximum_fusion.5.near), channel_id=1, source_target_pairs={{0,1},{1,0},{2,3},{3,2},{4,5},{5,4},{6,7},{7,6},{8,9},{9,8},{10,11... | collective-permute-start | bytes 393224 | tf_op jit(solution)/shard_map/ppermute | solution.py:376

commit v5 on v4

--- a/solution.py
+++ b/solution.py
@@ -171,7 +171,7 @@
 def join_planes(scal, own, via_a, via_b, arr, dst, lo, hi):
     even = scal[0] == 0
     for y in range(lo, hi):
-        a, b = via_a[arr, y], via_b[arr, y]
+        a, b = via_a[arr * ROWS + y], via_b[arr * ROWS + y]
         dst[y, 0:8, :] = jnp.where(even, b, a)
         dst[y, 8:16, :] = own[arr, y]
         dst[y, 16:24, :] = jnp.where(even, a, b)
@@ -202,7 +202,7 @@
         pack[i] = t
 
 
-def rim_kernel(scal, own, via_a, via_b, ends,
+def rim_kernel(scal, own, via_a, via_b,
                src, bx, by, bz, diag, inv, u2,
                absorb, conduct, u1):
     for arr, dst in ((0, src), (1, absorb), (2, conduct)):
@@ -210,13 +210,14 @@
     level = Level(bx, by, bz, diag, inv, 1, False)
     level.build(conduct, absorb, 1, ROWS - 1, 1.0)
     x = planes((FX, 128))
-    dev = scal[1]
-    left, right = jnp.maximum(dev - 1, 0), jnp.minimum(dev + 1, 7)
+    even = scal[0] == 0
     for y in range(1, ROWS - 1):
         u = inv[y] * src[y]
         if 0 <= y - HALO < 16:
-            at = pl.ds(y - HALO, 1)
-            u = jnp.where(x == 0, ends[left, at, :], jnp.where(x == FX - 1, ends[right, at, :], u))
+            i, at = divmod(y - HALO, 8)
+            a, b = (via[3 * ROWS + i, at:at + 1, :] for via in (via_a, via_b))
+            left, right = jnp.where(even, b, a), jnp.where(even, a, b)
+            u = jnp.where(x == 0, left, jnp.where(x == FX - 1, right, u))
         u1[y] = u
     zero = jnp.zeros((FX, 128), F32)
     for y in (0, 1, ROWS - 2, ROWS - 1):
@@ -384,7 +385,7 @@
     return 2 if g // 2 % 2 != core else -2
 
 
-def spread(pack, ends=None):
+def spread(pack):
     peers, devs = lax.axis_size("grp"), lax.axis_size("dev")
 
     def from_beside(array, by):
@@ -396,17 +397,9 @@
                     pairs.append((there * devs + d, g * devs + d))
         return lax.ppermute(array, ("grp", "dev"), pairs)
 
-    here = jnp.broadcast_to(pack, (devs,) + pack.shape)
-    if ends is not None:
-        d = lax.axis_index("dev")
-        mine = jnp.where(jnp.arange(devs)[:, None, None] < d, ends[0], ends[1])
-        here = jnp.concatenate([here, mine.reshape(devs, 2, 8, 128)], axis=1)
-    here = lax.all_to_all(here, "dev", 0, 0)
-    if ends is not None:
-        ends = here[:, -2:].reshape(devs, 16, 128)
-        here = here[:, :-2]
+    here = lax.all_to_all(jnp.broadcast_to(pack, (devs,) + pack.shape), "dev", 0, 0)
     near = jnp.stack([from_beside(here, one_away), from_beside(here, two_away)])
-    return ends, here, near, other_core(near)
+    return here, near, other_core(near)
 
 
 def local(source, absorb, conduct):
@@ -435,18 +428,20 @@
     near = [jnp.concatenate([one[:, :, x:x + 4], two[:, :, x:x + 4]], axis=2) for x in (0, 4)]
     near_a = other_core(jnp.where(core == 0, near[1], near[0]))
     near_b = other_chip(jnp.where(core == 0, near[0], near[1]))
-    via_a, via_b = other_core(fine), other_chip(fine)
     block, wide_mid, wide_low = (ROWS, FX, 128), (MROWS, MX, 128), (LROWS, LX, 128)
     pack, ends = call(first_kernel, [(6, 8, 128), (2, 16, 128)], [block] * 10, scal, fine, near_a, near_b)
-    ends, *parts = spread(pack, ends)
-    *state, u2 = call(rim_kernel, [block] * 7, [block] * 3, scal, fine, via_a, via_b, ends)
+    parts = spread(pack)
+    whole, ends = fine.reshape(3 * ROWS, 8, 128), ends.reshape(2, 2, 8, 128)
+    via_a = other_core(jnp.concatenate([whole, jnp.where(core == 0, ends[0], ends[1])]))
+    via_b = other_chip(jnp.concatenate([whole, jnp.where(core == 0, ends[1], ends[0])]))
+    *state, u2 = call(rim_kernel, [block] * 7, [block] * 3, scal, fine, via_a, via_b)
     *coefs, u2, pack = call(
         middle_kernel,
         [wide_mid] * 5 + [wide_low] * 4 + [block, (2, 8, 128)],
         [(5, 6, 64, 128)] + [wide_mid] * 5 + [wide_low] * 5 + [(20, MX, 128), (MROWS, 80, 128), block, block],
         scal, *state, u2, *parts,
     )
-    _, *parts = spread(pack)
+    parts = spread(pack)
     out, res = call(
         last_kernel,
         [(128, 128), (128, 128)],

time: 82.2 us -> 81.6 us (level)
  transfers between devices with their start and end apart: 12 -> 12, of which waited for: 5 -> 6; matrix products, arithmetic and copies ran while one was open for 0% -> 0% of each run, Pallas kernels for 2% -> 2%
where the time goes in v5:
time: 81.6 us; the launch traced here: 81 us
  starting transfers between devices  45.1 us (55%)
  blocking collectives  18.3 us (22%)
  Pallas kernels  8.99 us (11%)
  waiting for transfers between devices  6.3 us (8%)
  local copies, waits for them, and re-layouts  1.04 us (1%)
  between operations  1.01 us (1%)
    all_to_all x2, blocking collectives, spread(): lax.all_to_all(jnp.broadcast_to(pack, (devs,) + pack.shape), 'dev', 0, 0)  18.3 us
    ppermute x4, starting transfers between devices, other_core(): return lax.ppermute(array, 'dev', [(i, i ^ 1) for i in range(8)])  15.2 us
    ppermute x4, starting transfers between devices, from_beside(): return lax.ppermute(array, ('grp', 'dev'), pairs)  12.7 us
    pallas_call x4, Pallas kernels, call(): pl.pallas_call(kernel, out_shape=[jax.ShapeDtypeStruct(s, F32) for s in o...  8.99 us
    ppermute x2, starting transfers between devices, other_chip(): lax.ppermute(array, 'dev', [(1, 2), (2, 1), (3, 4), (4, 3), (5, 6), (6, 5)])  8.81 us
    ppermute x2, starting transfers between devices, swap_rows(): return lax.ppermute(array, 'grp', pairs + [(j, i) for i, j in pairs])  8.37 us
    ppermute x2, waiting for transfers between devices, swap_rows(): return lax.ppermute(array, 'grp', pairs + [(j, i) for i, j in pairs])  2.43 us
    ppermute x4, waiting for transfers between devices, from_beside(): return lax.ppermute(array, ('grp', 'dev'), pairs)  1.64 us
  transfers between devices with their start and end apart: 12, of which 6 were waited for; matrix products, arithmetic and copies ran while one was open for 0% of the time, Pallas kernels for 2%

profile of v5, /device:TPU:521, one launch (start us, length us, event | category | flops | bytes accessed | tf_op | source)
XLA Modules:
  0.0 81.0 jit_solution(5618517659652977501)
XLA Ops:
  0.7 0.9 %copy.11 = f32[8,16,128]{2,0,1:T(8,128)S(1)} copy(f32[8,16,128]{2,1,0:T(8,128)} %param.3) | data formatting | bytes 131072 | tf_op args[0]
  1.7 3.2 %collective-permute-start = (f32[3,9,8,128]{3,2,1,0:T(8,128)S(1)}, f32[3,9,8,128]{3,2,1,0:T(8,128)S(1)}, u32[]{:S(2)}, u32[]{:S(2)}) collective-permute-start(f32[3,9,8,128]{3,2,1,0:T(8,128)S(1)} %get-tuple-element.54), channel_id=1, source_target_pairs={{8,16},{24,32},{40,48},{56,64},{72,80},{88,96},{104,112},{120,128}... | collective-permute-start | bytes 331784 | tf_op jit(solution)/shard_map/ppermute | solution.py:417
  4.9 5.2 %collective-permute-start.1 = (f32[3,9,8,128]{3,2,1,0:T(8,128)S(1)}, f32[3,9,8,128]{3,2,1,0:T(8,128)S(1)}, u32[]{:S(2)}, u32[]{:S(2)}) collective-permute-start(f32[3,9,8,128]{3,2,1,0:T(8,128)S(1)} %get-tuple-element.55), channel_id=1, source_target_pairs={{0,8},{16,24},{32,40},{48,56},{64,72},{80,88},{96,104},{112,120},{... | collective-permute-start | bytes 331784 | tf_op jit(solution)/shard_map/ppermute | solution.py:417
  10.1 0.0 collective-permute-done
  10.1 2.4 %collective-permute-done.1 = f32[3,9,8,128]{3,2,1,0:T(8,128)S(1)} collective-permute-done((f32[3,9,8,128]{3,2,1,0:T(8,128)S(1)}, f32[3,9,8,128]{3,2,1,0:T(8,128)S(1)}, u32[]{:S(2)}, u32[]{:S(2)}) %collective-permute-start.1) | collective-permute-done | bytes 110624 | tf_op jit(solution)/shard_map/ppermute | solution.py:417
  12.7 0.1 fusion
  12.8 4.6 %collective-permute-start.3 = (f32[3,11,8,128]{3,2,1,0:T(8,128)S(1)}, f32[3,11,8,128]{3,2,1,0:T(8,128)S(1)}, u32[]{:S(2)}, u32[]{:S(2)}) collective-permute-start(f32[3,11,8,128]{3,2,1,0:T(8,128)S(1)} %get-tuple-element.50), channel_id=1, source_target_pairs={{1,2},{2,1},{3,4},{4,3},{5,6},{6,5},{9,10},{10,9},{11,12},{12,11},... | collective-permute-start | bytes 405512 | tf_op jit(solution)/shard_map/ppermute | solution.py:425
  17.3 1.9 %collective-permute-start.2 = (f32[3,11,8,128]{3,2,1,0:T(8,128)S(1)}, f32[3,11,8,128]{3,2,1,0:T(8,128)S(1)}, u32[]{:S(2)}, u32[]{:S(2)}) collective-permute-start(f32[3,11,8,128]{3,2,1,0:T(8,128)S(1)} %get-tuple-element.51), channel_id=1, source_target_pairs={{0,1},{1,0},{2,3},{3,2},{4,5},{5,4},{6,7},{7,6},{8,9},{9,8},{10,11... | collective-permute-start | bytes 405512 | tf_op jit(solution)/shard_map/ppermute | solution.py:377
  19.3 0.1 pad_add_fusion.scal
  19.4 0.6 collective-permute-done.3.near_b
  20.0 0.6 collective-permute-done.2.near_a
  20.6 1.2 %shard_map.50 = (f32[6,8,128]{2,1,0:T(8,128)S(1)}, f32[2,16,128]{2,1,0:T(8,128)S(1)}) custom-call(s32[4]{0:T(128)S(1)} %pad_add_fusion.scal, f32[3,34,8,128]{3,2,1,0:T(8,128)S(1)} %pad_maximum_fusion.2.own, f32[3,11,8,128]{3,2,1,0:T(8,128)S(1)} %collective-permute-done.2.near_a, f32[3,11,8,128]{3,2,1,0:T(8,128)S(1)} %collective-permute-done.3.near_b), custom_call_target="tpu_custom_call" | custom-call | tf_op jit(solution)/shard_map/pallas_call | solution.py:365
  21.7 10.1 %all_to_all.10.here = f32[8,6,8,128]{3,2,1,0:T(8,128)S(1)} all-to-all(f32[8,6,8,128]{3,2,1,0:T(8,128)S(1)} %broadcast_in_dim.6), channel_id=1, replica_groups=mesh['grp'=96,'dev'=8] {'dev'}, dimensions={0} | all-to-all | bytes 393216 | tf_op jit(solution)/shard_map/all_to_all | solution.py:400
  31.8 3.8 %collective-permute-start.7 = (f32[8,6,8,128]{3,2,1,0:T(8,128)S(1)}, f32[8,6,8,128]{3,2,1,0:T(8,128)S(1)}, u32[]{:S(2)}, u32[]{:S(2)}) collective-permute-start(f32[8,6,8,128]{3,2,1,0:T(8,128)S(1)} %all_to_all.10.here), channel_id=1, source_target_pairs={{17,1},{19,3},{21,5},{23,7},{25,9},{27,11},{29,13},{31,15},{32,16}... | collective-permute-start | bytes 589832 | tf_op jit(solution)/shard_map/ppermute | solution.py:398
  35.6 2.8 %collective-permute-start.6 = (f32[8,6,8,128]{3,2,1,0:T(8,128)S(1)}, f32[8,6,8,128]{3,2,1,0:T(8,128)S(1)}, u32[]{:S(2)}, u32[]{:S(2)}) collective-permute-start(f32[8,6,8,128]{3,2,1,0:T(8,128)S(1)} %all_to_all.10.here), channel_id=1, source_target_pairs={{8,0},{10,2},{12,4},{14,6},{0,8},{17,9},{2,10},{19,11},{4,12},{21,... | collective-permute-start | bytes 589832 | tf_op jit(solution)/shard_map/ppermute | solution.py:398
  38.5 0.1 pad_maximum_fusion.1
  38.6 4.3 %collective-permute-start.5 = (f32[104,8,128]{2,1,0:T(8,128)S(1)}, f32[104,8,128]{2,1,0:T(8,128)S(1)}, u32[]{:S(2)}, u32[]{:S(2)}) collective-permute-start(f32[104,8,128]{2,1,0:T(8,128)S(1)} %get-tuple-element.46), channel_id=1, source_target_pairs={{1,2},{2,1},{3,4},{4,3},{5,6},{6,5},{9,10},{10,9},{11,12},{12,11},... | collective-permute-start | bytes 1277960 | tf_op jit(solution)/shard_map/ppermute | solution.py:425
  42.8 1.9 %collective-permute-start.4 = (f32[104,8,128]{2,1,0:T(8,128)S(1)}, f32[104,8,128]{2,1,0:T(8,128)S(1)}, u32[]{:S(2)}, u32[]{:S(2)}) collective-permute-start(f32[104,8,128]{2,1,0:T(8,128)S(1)} %get-tuple-element.47), channel_id=1, source_target_pairs={{0,1},{1,0},{2,3},{3,2},{4,5},{5,4},{6,7},{7,6},{8,9},{9,8},{10,11... | collective-permute-start | bytes 1277960 | tf_op jit(solution)/shard_map/ppermute | solution.py:377
  44.8 0.0 collective-permute-done.7
  44.8 0.0 collective-permute-done.6
  44.8 4.2 %collective-permute-start.8 = (f32[2,8,6,8,128]{4,3,2,1,0:T(8,128)S(1)}, f32[2,8,6,8,128]{4,3,2,1,0:T(8,128)S(1)}, u32[]{:S(2)}, u32[]{:S(2)}) collective-permute-start(f32[2,8,6,8,128]{4,3,2,1,0:T(8,128)S(1)} %pad_maximum_fusion.3.near), channel_id=1, source_target_pairs={{0,1},{1,0},{2,3},{3,2},{4,5},{5,4},{6,7},{7,6},{8,9},{9,8},{10,11... | collective-permute-start | bytes 1179656 | tf_op jit(solution)/shard_map/ppermute | solution.py:377
  49.0 0.0 collective-permute-done.4.via_a
  49.0 1.2 %shard_map.51 = (f32[34,24,128]{2,1,0:T(8,128)S(1)}, f32[34,24,128]{2,1,0:T(8,128)S(1)}, f32[34,24,128]{2,1,0:T(8,128)S(1)}, f32[34,24,128]{2,1,0:T(8,128)S(1)},...) custom-call(s32[4]{0:T(128)S(1)} %pad_add_fusion.scal, ...), custom_call_target="tpu_custom_call" | custom-call | tf_op jit(solution)/shard_map/pallas_call | solution.py:365
  50.3 0.1 collective-permute-done.8.swapped
  50.3 3.7 %shard_map.52 = (f32[40,16,128]{2,1,0:T(8,128)S(1)}, f32[40,16,128]{2,1,0:T(8,128)S(1)}, f32[40,16,128]{2,1,0:T(8,128)S(1)}, f32[40,16,128]{2,1,0:T(8,128)S(1)},...) custom-call(s32[4]{0:T(128)S(1)} %pad_add_fusion.scal, ...), custom_call_target="tpu_custom_call" | custom-call | tf_op jit(solution)/shard_map/pallas_call | solution.py:365
  54.1 8.2 %all_to_all.11.here = f32[8,2,8,128]{3,2,1,0:T(8,128)S(1)} all-to-all(f32[8,2,8,128]{3,2,1,0:T(8,128)S(1)} %broadcast_in_dim.7), channel_id=1, replica_groups=mesh['grp'=96,'dev'=8] {'dev'}, dimensions={0} | all-to-all | bytes 131072 | tf_op jit(solution)/shard_map/all_to_all | solution.py:400
  62.3 1.9 %collective-permute-start.10 = (f32[8,2,8,128]{3,2,1,0:T(8,128)S(1)}, f32[8,2,8,128]{3,2,1,0:T(8,128)S(1)}, u32[]{:S(2)}, u32[]{:S(2)}) collective-permute-start(f32[8,2,8,128]{3,2,1,0:T(8,128)S(1)} %all_to_all.11.here), channel_id=1, source_target_pairs={{17,1},{19,3},{21,5},{23,7},{25,9},{27,11},{29,13},{31,15},{32,16}... | collective-permute-start | bytes 196616 | tf_op jit(solution)/shard_map/ppermute | solution.py:398
  64.2 4.1 %collective-permute-start.9 = (f32[8,2,8,128]{3,2,1,0:T(8,128)S(1)}, f32[8,2,8,128]{3,2,1,0:T(8,128)S(1)}, u32[]{:S(2)}, u32[]{:S(2)}) collective-permute-start(f32[8,2,8,128]{3,2,1,0:T(8,128)S(1)} %all_to_all.11.here), channel_id=1, source_target_pairs={{8,0},{10,2},{12,4},{14,6},{0,8},{17,9},{2,10},{19,11},{4,12},{21,... | collective-permute-start | bytes 196616 | tf_op jit(solution)/shard_map/ppermute | solution.py:398
  68.3 1.6 %collective-permute-done.9 = f32[8,2,8,128]{3,2,1,0:T(8,128)S(1)} collective-permute-done((f32[8,2,8,128]{3,2,1,0:T(8,128)S(1)}, f32[8,2,8,128]{3,2,1,0:T(8,128)S(1)}, u32[]{:S(2)}, u32[]{:S(2)}) %collective-permute-start.9) | collective-permute-done | bytes 65568 | tf_op jit(solution)/shard_map/ppermute | solution.py:398
  69.9 7.2 %collective-permute-start.11 = (f32[2,8,2,8,128]{4,3,2,1,0:T(8,128)S(1)}, f32[2,8,2,8,128]{4,3,2,1,0:T(8,128)S(1)}, u32[]{:S(2)}, u32[]{:S(2)}) collective-permute-start(f32[2,8,2,8,128]{4,3,2,1,0:T(8,128)S(1)} %pad_maximum_fusion.6.near), channel_id=1, source_target_pairs={{0,1},{1,0},{2,3},{3,2},{4,5},{5,4},{6,7},{7,6},{8,9},{9,8},{10,11... | collective-permute-start | bytes 393224 | tf_op jit(solution)/shard_map/ppermute | solution.py:377
  77.1 1.0 %collective-permute-done.11.swapped = f32[2,8,2,8,128]{4,3,2,1,0:T(8,128)S(1)} collective-permute-done((f32[2,8,2,8,128]{4,3,2,1,0:T(8,128)S(1)}, f32[2,8,2,8,128]{4,3,2,1,0:T(8,128)S(1)}, u32[]{:S(2)}, u32[]{:S(2)}) %collective-permute-start.11) | collective-permute-done | bytes 131104 | tf_op jit(solution)/shard_map/ppermute | solution.py:377
  78.1 2.9 %shard_map.53 = (f32[128,128]{1,0:T(8,128)}, f32[128,128]{1,0:T(8,128)}) custom-call(s32[4]{0:T(128)S(1)} %pad_add_fusion.scal, f32[34,24,128]{2,1,0:T(8,128)S(1)} %get-tuple-element.25.src, f32[34,24,128]{2,1,0:T(8,128)S(1)} %get-tuple-element.26.fbx, f32[34,24,128]{2,1,0:T(8,128)S(1)} %get-tuple-element.27.fby, f32[34,24,128]{2,1,0:T(8,128)S(1)} %get-tuple-element.28.fbz, ...), custom_call_target="tpu_custom_call" | custom-call | tf_op jit(solution)/shard_map/pallas_call | solution.py:365
  (19 shorter events, 0.3 us)
Async XLA Ops:
  0.7 0.9 %copy-start = (f32[8,16,128]{2,1,0:T(8,128)S(1)}, f32[8,16,128]{2,1,0:T(8,128)}, u32[]{:S(2)}) copy-start(f32[8,16,128]{2,1,0:T(8,128)} %param.5) | copy-start | bytes 196612
  0.7 0.9 %copy-start.1 = (f32[8,16,128]{2,1,0:T(8,128)S(1)}, f32[8,16,128]{2,1,0:T(8,128)}, u32[]{:S(2)}) copy-start(f32[8,16,128]{2,1,0:T(8,128)} %param.4) | copy-start | bytes 196612
  1.7 8.4 %collective-permute-start = (f32[3,9,8,128]{3,2,1,0:T(8,128)S(1)}, f32[3,9,8,128]{3,2,1,0:T(8,128)S(1)}, u32[]{:S(2)}, u32[]{:S(2)}) collective-permute-start(f32[3,9,8,128]{3,2,1,0:T(8,128)S(1)} %get-tuple-element.54), channel_id=1, source_target_pairs={{8,16},{24,32},{40,48},{56,64},{72,80},{88,96},{104,112},{120,128}... | collective-permute-start | bytes 331784 | tf_op jit(solution)/shard_map/ppermute | solution.py:417
  4.9 7.6 %collective-permute-start.1 = (f32[3,9,8,128]{3,2,1,0:T(8,128)S(1)}, f32[3,9,8,128]{3,2,1,0:T(8,128)S(1)}, u32[]{:S(2)}, u32[]{:S(2)}) collective-permute-start(f32[3,9,8,128]{3,2,1,0:T(8,128)S(1)} %get-tuple-element.55), channel_id=1, source_target_pairs={{0,8},{16,24},{32,40},{48,56},{64,72},{80,88},{96,104},{112,120},{... | collective-permute-start | bytes 331784 | tf_op jit(solution)/shard_map/ppermute | solution.py:417
  12.8 7.2 %collective-permute-start.3 = (f32[3,11,8,128]{3,2,1,0:T(8,128)S(1)}, f32[3,11,8,128]{3,2,1,0:T(8,128)S(1)}, u32[]{:S(2)}, u32[]{:S(2)}) collective-permute-start(f32[3,11,8,128]{3,2,1,0:T(8,128)S(1)} %get-tuple-element.50), channel_id=1, source_target_pairs={{1,2},{2,1},{3,4},{4,3},{5,6},{6,5},{9,10},{10,9},{11,12},{12,11},... | collective-permute-start | bytes 405512 | tf_op jit(solution)/shard_map/ppermute | solution.py:425
  17.3 3.2 %collective-permute-start.2 = (f32[3,11,8,128]{3,2,1,0:T(8,128)S(1)}, f32[3,11,8,128]{3,2,1,0:T(8,128)S(1)}, u32[]{:S(2)}, u32[]{:S(2)}) collective-permute-start(f32[3,11,8,128]{3,2,1,0:T(8,128)S(1)} %get-tuple-element.51), channel_id=1, source_target_pairs={{0,1},{1,0},{2,3},{3,2},{4,5},{5,4},{6,7},{7,6},{8,9},{9,8},{10,11... | collective-permute-start | bytes 405512 | tf_op jit(solution)/shard_map/ppermute | solution.py:377
  31.8 13.0 %collective-permute-start.7 = (f32[8,6,8,128]{3,2,1,0:T(8,128)S(1)}, f32[8,6,8,128]{3,2,1,0:T(8,128)S(1)}, u32[]{:S(2)}, u32[]{:S(2)}) collective-permute-start(f32[8,6,8,128]{3,2,1,0:T(8,128)S(1)} %all_to_all.10.here), channel_id=1, source_target_pairs={{17,1},{19,3},{21,5},{23,7},{25,9},{27,11},{29,13},{31,15},{32,16}... | collective-permute-start | bytes 589832 | tf_op jit(solution)/shard_map/ppermute | solution.py:398
  35.6 9.1 %collective-permute-start.6 = (f32[8,6,8,128]{3,2,1,0:T(8,128)S(1)}, f32[8,6,8,128]{3,2,1,0:T(8,128)S(1)}, u32[]{:S(2)}, u32[]{:S(2)}) collective-permute-start(f32[8,6,8,128]{3,2,1,0:T(8,128)S(1)} %all_to_all.10.here), channel_id=1, source_target_pairs={{8,0},{10,2},{12,4},{14,6},{0,8},{17,9},{2,10},{19,11},{4,12},{21,... | collective-permute-start | bytes 589832 | tf_op jit(solution)/shard_map/ppermute | solution.py:398
  38.6 10.5 %collective-permute-start.5 = (f32[104,8,128]{2,1,0:T(8,128)S(1)}, f32[104,8,128]{2,1,0:T(8,128)S(1)}, u32[]{:S(2)}, u32[]{:S(2)}) collective-permute-start(f32[104,8,128]{2,1,0:T(8,128)S(1)} %get-tuple-element.46), channel_id=1, source_target_pairs={{1,2},{2,1},{3,4},{4,3},{5,6},{6,5},{9,10},{10,9},{11,12},{12,11},... | collective-permute-start | bytes 1277960 | tf_op jit(solution)/shard_map/ppermute | solution.py:425
  42.8 6.2 %collective-permute-start.4 = (f32[104,8,128]{2,1,0:T(8,128)S(1)}, f32[104,8,128]{2,1,0:T(8,128)S(1)}, u32[]{:S(2)}, u32[]{:S(2)}) collective-permute-start(f32[104,8,128]{2,1,0:T(8,128)S(1)} %get-tuple-element.47), channel_id=1, source_target_pairs={{0,1},{1,0},{2,3},{3,2},{4,5},{5,4},{6,7},{7,6},{8,9},{9,8},{10,11... | collective-permute-start | bytes 1277960 | tf_op jit(solution)/shard_map/ppermute | solution.py:377
  44.8 5.5 %collective-permute-start.8 = (f32[2,8,6,8,128]{4,3,2,1,0:T(8,128)S(1)}, f32[2,8,6,8,128]{4,3,2,1,0:T(8,128)S(1)}, u32[]{:S(2)}, u32[]{:S(2)}) collective-permute-start(f32[2,8,6,8,128]{4,3,2,1,0:T(8,128)S(1)} %pad_maximum_fusion.3.near), channel_id=1, source_target_pairs={{0,1},{1,0},{2,3},{3,2},{4,5},{5,4},{6,7},{7,6},{8,9},{9,8},{10,11... | collective-permute-start | bytes 1179656 | tf_op jit(solution)/shard_map/ppermute | solution.py:377
  62.3 6.0 %collective-permute-start.10 = (f32[8,2,8,128]{3,2,1,0:T(8,128)S(1)}, f32[8,2,8,128]{3,2,1,0:T(8,128)S(1)}, u32[]{:S(2)}, u32[]{:S(2)}) collective-permute-start(f32[8,2,8,128]{3,2,1,0:T(8,128)S(1)} %all_to_all.11.here), channel_id=1, source_target_pairs={{17,1},{19,3},{21,5},{23,7},{25,9},{27,11},{29,13},{31,15},{32,16}... | collective-permute-start | bytes 196616 | tf_op jit(solution)/shard_map/ppermute | solution.py:398
  64.2 5.8 %collective-permute-start.9 = (f32[8,2,8,128]{3,2,1,0:T(8,128)S(1)}, f32[8,2,8,128]{3,2,1,0:T(8,128)S(1)}, u32[]{:S(2)}, u32[]{:S(2)}) collective-permute-start(f32[8,2,8,128]{3,2,1,0:T(8,128)S(1)} %all_to_all.11.here), channel_id=1, source_target_pairs={{8,0},{10,2},{12,4},{14,6},{0,8},{17,9},{2,10},{19,11},{4,12},{21,... | collective-permute-start | bytes 196616 | tf_op jit(solution)/shard_map/ppermute | solution.py:398
  69.9 8.2 %collective-permute-start.11 = (f32[2,8,2,8,128]{4,3,2,1,0:T(8,128)S(1)}, f32[2,8,2,8,128]{4,3,2,1,0:T(8,128)S(1)}, u32[]{:S(2)}, u32[]{:S(2)}) collective-permute-start(f32[2,8,2,8,128]{4,3,2,1,0:T(8,128)S(1)} %pad_maximum_fusion.6.near), channel_id=1, source_target_pairs={{0,1},{1,0},{2,3},{3,2},{4,5},{5,4},{6,7},{7,6},{8,9},{9,8},{10,11... | collective-permute-start | bytes 393224 | tf_op jit(solution)/shard_map/ppermute | solution.py:377

commit v6 on v5

--- a/solution.py
+++ b/solution.py
@@ -159,13 +159,12 @@
     rows(lo, hi, body)
 
 
-def scale(dst, factor, src, lo, hi):
-    def body(y, n):
-        new = [factor[y + t] * src[y + t] for t in range(n)]
-        for t in range(n):
-            dst[y + t] = new[t]
-
-    rows(lo, hi, body)
+class FirstSweep:
+    def __init__(self, level, rhs):
+        self.level, self.rhs = level, rhs
+
+    def __getitem__(self, y):
+        return self.level.inv[y] * self.rhs[y]
 
 
 def join_planes(scal, own, via_a, via_b, arr, dst, lo, hi):
@@ -178,7 +177,7 @@
 
 
 def first_kernel(scal, own, near_a, near_b, pack, ends,
-                 src, absorb, conduct, bx, by, bz, diag, inv, u1, u2):
+                 src, absorb, conduct, bx, by, bz, diag, inv, u2):
     even = scal[0] == 0
     for arr, dst in ((0, src), (1, absorb), (2, conduct)):
         for i in range(22):
@@ -190,10 +189,11 @@
             dst[y, 16:24, :] = right if i % 2 == 0 else down(right, 0, 4)
     level = Level(bx, by, bz, diag, inv, 1, False)
     level.build(conduct, absorb, HALO - 2, ROWS - HALO + 2, 1.0)
-    scale(u1, inv, src, HALO - 2, ROWS - HALO + 2)
+    u1 = FirstSweep(level, src)
     for y in range(16):
-        for i, x in enumerate((8, 15)):
-            ends[i, y:y + 1, :] = u1[HALO + y, x:x + 1, :]
+        own_rows = inv[HALO + y, 8:16, :] * src[HALO + y, 8:16, :]
+        ends[0, y:y + 1, :] = own_rows[0:1]
+        ends[1, y:y + 1, :] = own_rows[7:8]
     level.sweep(u2, u1, src, HALO - 1, ROWS - HALO + 1)
     tiles = restrict_own([r[8:16] for r in level.residual(u2, src, HALO, 16)])
     tiles += restrict_own([absorb[HALO + i, 8:16, :] for i in range(16)])
@@ -261,11 +261,9 @@
 
 
 def coarse(mid, low, rhs, m1, m2, lrhs, l1, l2, tmp, k):
-    scale(m1, mid.inv, rhs, 2 + 2 * k, 38 - 2 * k)
-    mid.sweep(m2, m1, rhs, 3 + 2 * k, 37 - 2 * k)
+    mid.sweep(m2, FirstSweep(mid, rhs), rhs, 3 + 2 * k, 37 - 2 * k)
     restrict_low(functools.partial(mid.residual, m2, rhs), tmp, lrhs, 2 + k, 18 - k)
-    scale(l1, low.inv, lrhs, 2 + k, 18 - k)
-    low.sweep(l2, l1, lrhs, 3 + k, 17 - k)
+    low.sweep(l2, FirstSweep(low, lrhs), lrhs, 3 + k, 17 - k)
     low.sweep(l1, l2, lrhs, 4 + k, 16 - k)
     low.sweep(l2, l1, lrhs, 5 + k, 15 - k)
 
@@ -429,7 +427,7 @@
     near_a = other_core(jnp.where(core == 0, near[1], near[0]))
     near_b = other_chip(jnp.where(core == 0, near[0], near[1]))
     block, wide_mid, wide_low = (ROWS, FX, 128), (MROWS, MX, 128), (LROWS, LX, 128)
-    pack, ends = call(first_kernel, [(6, 8, 128), (2, 16, 128)], [block] * 10, scal, fine, near_a, near_b)
+    pack, ends = call(first_kernel, [(6, 8, 128), (2, 16, 128)], [block] * 9, scal, fine, near_a, near_b)
     parts = spread(pack)
     whole, ends = fine.reshape(3 * ROWS, 8, 128), ends.reshape(2, 2, 8, 128)
     via_a = other_core(jnp.concatenate([whole, jnp.where(core == 0, ends[0], ends[1])]))

time: 81.6 us -> 81.5 us (level)
  no operation moved by 1% of the time
where the time goes in v6:
time: 81.5 us; the launch traced here: 81 us
  starting transfers between devices  45.1 us (55%)
  blocking collectives  18.3 us (22%)
  Pallas kernels  8.97 us (11%)
  waiting for transfers between devices  6.3 us (8%)
  local copies, waits for them, and re-layouts  1.04 us (1%)
  between operations  1.01 us (1%)
    all_to_all x2, blocking collectives, spread(): lax.all_to_all(jnp.broadcast_to(pack, (devs,) + pack.shape), 'dev', 0, 0)  18.3 us
    ppermute x4, starting transfers between devices, other_core(): return lax.ppermute(array, 'dev', [(i, i ^ 1) for i in range(8)])  15.2 us
    ppermute x4, starting transfers between devices, from_beside(): return lax.ppermute(array, ('grp', 'dev'), pairs)  12.7 us
    pallas_call x4, Pallas kernels, call(): pl.pallas_call(kernel, out_shape=[jax.ShapeDtypeStruct(s, F32) for s in o...  8.97 us
    ppermute x2, starting transfers between devices, other_chip(): lax.ppermute(array, 'dev', [(1, 2), (2, 1), (3, 4), (4, 3), (5, 6), (6, 5)])  8.81 us
    ppermute x2, starting transfers between devices, swap_rows(): return lax.ppermute(array, 'grp', pairs + [(j, i) for i, j in pairs])  8.37 us
    ppermute x2, waiting for transfers between devices, swap_rows(): return lax.ppermute(array, 'grp', pairs + [(j, i) for i, j in pairs])  2.43 us
    ppermute x4, waiting for transfers between devices, from_beside(): return lax.ppermute(array, ('grp', 'dev'), pairs)  1.64 us
  transfers between devices with their start and end apart: 12, of which 6 were waited for; matrix products, arithmetic and copies ran while one was open for 0% of the time, Pallas kernels for 2%

profile of v6, /device:TPU:521, one launch (start us, length us, event | category | flops | bytes accessed | tf_op | source)
XLA Modules:
  0.0 81.0 jit_solution(871900572345103469)
XLA Ops:
  0.7 0.9 %copy.11 = f32[8,16,128]{2,0,1:T(8,128)S(1)} copy(f32[8,16,128]{2,1,0:T(8,128)} %param.3) | data formatting | bytes 131072 | tf_op args[0]
  1.7 3.2 %collective-permute-start = (f32[3,9,8,128]{3,2,1,0:T(8,128)S(1)}, f32[3,9,8,128]{3,2,1,0:T(8,128)S(1)}, u32[]{:S(2)}, u32[]{:S(2)}) collective-permute-start(f32[3,9,8,128]{3,2,1,0:T(8,128)S(1)} %get-tuple-element.54), channel_id=1, source_target_pairs={{8,16},{24,32},{40,48},{56,64},{72,80},{88,96},{104,112},{120,128}... | collective-permute-start | bytes 331784 | tf_op jit(solution)/shard_map/ppermute | solution.py:415
  4.9 5.2 %collective-permute-start.1 = (f32[3,9,8,128]{3,2,1,0:T(8,128)S(1)}, f32[3,9,8,128]{3,2,1,0:T(8,128)S(1)}, u32[]{:S(2)}, u32[]{:S(2)}) collective-permute-start(f32[3,9,8,128]{3,2,1,0:T(8,128)S(1)} %get-tuple-element.55), channel_id=1, source_target_pairs={{0,8},{16,24},{32,40},{48,56},{64,72},{80,88},{96,104},{112,120},{... | collective-permute-start | bytes 331784 | tf_op jit(solution)/shard_map/ppermute | solution.py:415
  10.1 0.0 collective-permute-done
  10.1 2.4 %collective-permute-done.1 = f32[3,9,8,128]{3,2,1,0:T(8,128)S(1)} collective-permute-done((f32[3,9,8,128]{3,2,1,0:T(8,128)S(1)}, f32[3,9,8,128]{3,2,1,0:T(8,128)S(1)}, u32[]{:S(2)}, u32[]{:S(2)}) %collective-permute-start.1) | collective-permute-done | bytes 110624 | tf_op jit(solution)/shard_map/ppermute | solution.py:415
  12.7 0.1 fusion
  12.8 4.6 %collective-permute-start.3 = (f32[3,11,8,128]{3,2,1,0:T(8,128)S(1)}, f32[3,11,8,128]{3,2,1,0:T(8,128)S(1)}, u32[]{:S(2)}, u32[]{:S(2)}) collective-permute-start(f32[3,11,8,128]{3,2,1,0:T(8,128)S(1)} %get-tuple-element.50), channel_id=1, source_target_pairs={{1,2},{2,1},{3,4},{4,3},{5,6},{6,5},{9,10},{10,9},{11,12},{12,11},... | collective-permute-start | bytes 405512 | tf_op jit(solution)/shard_map/ppermute | solution.py:423
  17.3 1.9 %collective-permute-start.2 = (f32[3,11,8,128]{3,2,1,0:T(8,128)S(1)}, f32[3,11,8,128]{3,2,1,0:T(8,128)S(1)}, u32[]{:S(2)}, u32[]{:S(2)}) collective-permute-start(f32[3,11,8,128]{3,2,1,0:T(8,128)S(1)} %get-tuple-element.51), channel_id=1, source_target_pairs={{0,1},{1,0},{2,3},{3,2},{4,5},{5,4},{6,7},{7,6},{8,9},{9,8},{10,11... | collective-permute-start | bytes 405512 | tf_op jit(solution)/shard_map/ppermute | solution.py:375
  19.3 0.1 pad_add_fusion.scal
  19.4 0.6 collective-permute-done.3.near_b
  20.0 0.6 collective-permute-done.2.near_a
  20.6 1.1 %shard_map.50 = (f32[6,8,128]{2,1,0:T(8,128)S(1)}, f32[2,16,128]{2,1,0:T(8,128)S(1)}) custom-call(s32[4]{0:T(128)S(1)} %pad_add_fusion.scal, f32[3,34,8,128]{3,2,1,0:T(8,128)S(1)} %pad_maximum_fusion.2.own, f32[3,11,8,128]{3,2,1,0:T(8,128)S(1)} %collective-permute-done.2.near_a, f32[3,11,8,128]{3,2,1,0:T(8,128)S(1)} %collective-permute-done.3.near_b), custom_call_target="tpu_custom_call" | custom-call | tf_op jit(solution)/shard_map/pallas_call | solution.py:363
  21.7 10.1 %all_to_all.10.here = f32[8,6,8,128]{3,2,1,0:T(8,128)S(1)} all-to-all(f32[8,6,8,128]{3,2,1,0:T(8,128)S(1)} %broadcast_in_dim.6), channel_id=1, replica_groups=mesh['grp'=96,'dev'=8] {'dev'}, dimensions={0} | all-to-all | bytes 393216 | tf_op jit(solution)/shard_map/all_to_all | solution.py:398
  31.8 3.8 %collective-permute-start.7 = (f32[8,6,8,128]{3,2,1,0:T(8,128)S(1)}, f32[8,6,8,128]{3,2,1,0:T(8,128)S(1)}, u32[]{:S(2)}, u32[]{:S(2)}) collective-permute-start(f32[8,6,8,128]{3,2,1,0:T(8,128)S(1)} %all_to_all.10.here), channel_id=1, source_target_pairs={{17,1},{19,3},{21,5},{23,7},{25,9},{27,11},{29,13},{31,15},{32,16}... | collective-permute-start | bytes 589832 | tf_op jit(solution)/shard_map/ppermute | solution.py:396
  35.6 2.8 %collective-permute-start.6 = (f32[8,6,8,128]{3,2,1,0:T(8,128)S(1)}, f32[8,6,8,128]{3,2,1,0:T(8,128)S(1)}, u32[]{:S(2)}, u32[]{:S(2)}) collective-permute-start(f32[8,6,8,128]{3,2,1,0:T(8,128)S(1)} %all_to_all.10.here), channel_id=1, source_target_pairs={{8,0},{10,2},{12,4},{14,6},{0,8},{17,9},{2,10},{19,11},{4,12},{21,... | collective-permute-start | bytes 589832 | tf_op jit(solution)/shard_map/ppermute | solution.py:396
  38.5 0.1 pad_maximum_fusion.1
  38.5 4.3 %collective-permute-start.5 = (f32[104,8,128]{2,1,0:T(8,128)S(1)}, f32[104,8,128]{2,1,0:T(8,128)S(1)}, u32[]{:S(2)}, u32[]{:S(2)}) collective-permute-start(f32[104,8,128]{2,1,0:T(8,128)S(1)} %get-tuple-element.46), channel_id=1, source_target_pairs={{1,2},{2,1},{3,4},{4,3},{5,6},{6,5},{9,10},{10,9},{11,12},{12,11},... | collective-permute-start | bytes 1277960 | tf_op jit(solution)/shard_map/ppermute | solution.py:423
  42.8 1.9 %collective-permute-start.4 = (f32[104,8,128]{2,1,0:T(8,128)S(1)}, f32[104,8,128]{2,1,0:T(8,128)S(1)}, u32[]{:S(2)}, u32[]{:S(2)}) collective-permute-start(f32[104,8,128]{2,1,0:T(8,128)S(1)} %get-tuple-element.47), channel_id=1, source_target_pairs={{0,1},{1,0},{2,3},{3,2},{4,5},{5,4},{6,7},{7,6},{8,9},{9,8},{10,11... | collective-permute-start | bytes 1277960 | tf_op jit(solution)/shard_map/ppermute | solution.py:375
  44.7 0.0 collective-permute-done.6
  44.8 4.2 %collective-permute-start.8 = (f32[2,8,6,8,128]{4,3,2,1,0:T(8,128)S(1)}, f32[2,8,6,8,128]{4,3,2,1,0:T(8,128)S(1)}, u32[]{:S(2)}, u32[]{:S(2)}) collective-permute-start(f32[2,8,6,8,128]{4,3,2,1,0:T(8,128)S(1)} %pad_maximum_fusion.3.near), channel_id=1, source_target_pairs={{0,1},{1,0},{2,3},{3,2},{4,5},{5,4},{6,7},{7,6},{8,9},{9,8},{10,11... | collective-permute-start | bytes 1179656 | tf_op jit(solution)/shard_map/ppermute | solution.py:375
  49.0 0.0 collective-permute-done.4.via_a
  49.0 1.2 %shard_map.51 = (f32[34,24,128]{2,1,0:T(8,128)S(1)}, f32[34,24,128]{2,1,0:T(8,128)S(1)}, f32[34,24,128]{2,1,0:T(8,128)S(1)}, f32[34,24,128]{2,1,0:T(8,128)S(1)},...) custom-call(s32[4]{0:T(128)S(1)} %pad_add_fusion.scal, ...), custom_call_target="tpu_custom_call" | custom-call | tf_op jit(solution)/shard_map/pallas_call | solution.py:363
  50.2 0.1 collective-permute-done.8.swapped
  50.3 3.7 %shard_map.52 = (f32[40,16,128]{2,1,0:T(8,128)S(1)}, f32[40,16,128]{2,1,0:T(8,128)S(1)}, f32[40,16,128]{2,1,0:T(8,128)S(1)}, f32[40,16,128]{2,1,0:T(8,128)S(1)},...) custom-call(s32[4]{0:T(128)S(1)} %pad_add_fusion.scal, ...), custom_call_target="tpu_custom_call" | custom-call | tf_op jit(solution)/shard_map/pallas_call | solution.py:363
  54.0 8.2 %all_to_all.11.here = f32[8,2,8,128]{3,2,1,0:T(8,128)S(1)} all-to-all(f32[8,2,8,128]{3,2,1,0:T(8,128)S(1)} %broadcast_in_dim.7), channel_id=1, replica_groups=mesh['grp'=96,'dev'=8] {'dev'}, dimensions={0} | all-to-all | bytes 131072 | tf_op jit(solution)/shard_map/all_to_all | solution.py:398
  62.2 1.9 %collective-permute-start.10 = (f32[8,2,8,128]{3,2,1,0:T(8,128)S(1)}, f32[8,2,8,128]{3,2,1,0:T(8,128)S(1)}, u32[]{:S(2)}, u32[]{:S(2)}) collective-permute-start(f32[8,2,8,128]{3,2,1,0:T(8,128)S(1)} %all_to_all.11.here), channel_id=1, source_target_pairs={{17,1},{19,3},{21,5},{23,7},{25,9},{27,11},{29,13},{31,15},{32,16}... | collective-permute-start | bytes 196616 | tf_op jit(solution)/shard_map/ppermute | solution.py:396
  64.1 4.1 %collective-permute-start.9 = (f32[8,2,8,128]{3,2,1,0:T(8,128)S(1)}, f32[8,2,8,128]{3,2,1,0:T(8,128)S(1)}, u32[]{:S(2)}, u32[]{:S(2)}) collective-permute-start(f32[8,2,8,128]{3,2,1,0:T(8,128)S(1)} %all_to_all.11.here), channel_id=1, source_target_pairs={{8,0},{10,2},{12,4},{14,6},{0,8},{17,9},{2,10},{19,11},{4,12},{21,... | collective-permute-start | bytes 196616 | tf_op jit(solution)/shard_map/ppermute | solution.py:396
  68.2 0.0 collective-permute-done.10
  68.3 1.6 %collective-permute-done.9 = f32[8,2,8,128]{3,2,1,0:T(8,128)S(1)} collective-permute-done((f32[8,2,8,128]{3,2,1,0:T(8,128)S(1)}, f32[8,2,8,128]{3,2,1,0:T(8,128)S(1)}, u32[]{:S(2)}, u32[]{:S(2)}) %collective-permute-start.9) | collective-permute-done | bytes 65568 | tf_op jit(solution)/shard_map/ppermute | solution.py:396
  69.9 7.2 %collective-permute-start.11 = (f32[2,8,2,8,128]{4,3,2,1,0:T(8,128)S(1)}, f32[2,8,2,8,128]{4,3,2,1,0:T(8,128)S(1)}, u32[]{:S(2)}, u32[]{:S(2)}) collective-permute-start(f32[2,8,2,8,128]{4,3,2,1,0:T(8,128)S(1)} %pad_maximum_fusion.6.near), channel_id=1, source_target_pairs={{0,1},{1,0},{2,3},{3,2},{4,5},{5,4},{6,7},{7,6},{8,9},{9,8},{10,11... | collective-permute-start | bytes 393224 | tf_op jit(solution)/shard_map/ppermute | solution.py:375
  77.1 1.0 %collective-permute-done.11.swapped = f32[2,8,2,8,128]{4,3,2,1,0:T(8,128)S(1)} collective-permute-done((f32[2,8,2,8,128]{4,3,2,1,0:T(8,128)S(1)}, f32[2,8,2,8,128]{4,3,2,1,0:T(8,128)S(1)}, u32[]{:S(2)}, u32[]{:S(2)}) %collective-permute-start.11) | collective-permute-done | bytes 131104 | tf_op jit(solution)/shard_map/ppermute | solution.py:375
  78.1 2.9 %shard_map.53 = (f32[128,128]{1,0:T(8,128)}, f32[128,128]{1,0:T(8,128)}) custom-call(s32[4]{0:T(128)S(1)} %pad_add_fusion.scal, f32[34,24,128]{2,1,0:T(8,128)S(1)} %get-tuple-element.25.src, f32[34,24,128]{2,1,0:T(8,128)S(1)} %get-tuple-element.26.fbx, f32[34,24,128]{2,1,0:T(8,128)S(1)} %get-tuple-element.27.fby, f32[34,24,128]{2,1,0:T(8,128)S(1)} %get-tuple-element.28.fbz, ...), custom_call_target="tpu_custom_call" | custom-call | tf_op jit(solution)/shard_map/pallas_call | solution.py:363
  (19 shorter events, 0.3 us)
Async XLA Ops:
  0.7 0.9 %copy-start = (f32[8,16,128]{2,1,0:T(8,128)S(1)}, f32[8,16,128]{2,1,0:T(8,128)}, u32[]{:S(2)}) copy-start(f32[8,16,128]{2,1,0:T(8,128)} %param.5) | copy-start | bytes 196612
  0.7 0.9 %copy-start.1 = (f32[8,16,128]{2,1,0:T(8,128)S(1)}, f32[8,16,128]{2,1,0:T(8,128)}, u32[]{:S(2)}) copy-start(f32[8,16,128]{2,1,0:T(8,128)} %param.4) | copy-start | bytes 196612
  1.7 8.4 %collective-permute-start = (f32[3,9,8,128]{3,2,1,0:T(8,128)S(1)}, f32[3,9,8,128]{3,2,1,0:T(8,128)S(1)}, u32[]{:S(2)}, u32[]{:S(2)}) collective-permute-start(f32[3,9,8,128]{3,2,1,0:T(8,128)S(1)} %get-tuple-element.54), channel_id=1, source_target_pairs={{8,16},{24,32},{40,48},{56,64},{72,80},{88,96},{104,112},{120,128}... | collective-permute-start | bytes 331784 | tf_op jit(solution)/shard_map/ppermute | solution.py:415
  4.9 7.6 %collective-permute-start.1 = (f32[3,9,8,128]{3,2,1,0:T(8,128)S(1)}, f32[3,9,8,128]{3,2,1,0:T(8,128)S(1)}, u32[]{:S(2)}, u32[]{:S(2)}) collective-permute-start(f32[3,9,8,128]{3,2,1,0:T(8,128)S(1)} %get-tuple-element.55), channel_id=1, source_target_pairs={{0,8},{16,24},{32,40},{48,56},{64,72},{80,88},{96,104},{112,120},{... | collective-permute-start | bytes 331784 | tf_op jit(solution)/shard_map/ppermute | solution.py:415
  12.8 7.2 %collective-permute-start.3 = (f32[3,11,8,128]{3,2,1,0:T(8,128)S(1)}, f32[3,11,8,128]{3,2,1,0:T(8,128)S(1)}, u32[]{:S(2)}, u32[]{:S(2)}) collective-permute-start(f32[3,11,8,128]{3,2,1,0:T(8,128)S(1)} %get-tuple-element.50), channel_id=1, source_target_pairs={{1,2},{2,1},{3,4},{4,3},{5,6},{6,5},{9,10},{10,9},{11,12},{12,11},... | collective-permute-start | bytes 405512 | tf_op jit(solution)/shard_map/ppermute | solution.py:423
  17.3 3.2 %collective-permute-start.2 = (f32[3,11,8,128]{3,2,1,0:T(8,128)S(1)}, f32[3,11,8,128]{3,2,1,0:T(8,128)S(1)}, u32[]{:S(2)}, u32[]{:S(2)}) collective-permute-start(f32[3,11,8,128]{3,2,1,0:T(8,128)S(1)} %get-tuple-element.51), channel_id=1, source_target_pairs={{0,1},{1,0},{2,3},{3,2},{4,5},{5,4},{6,7},{7,6},{8,9},{9,8},{10,11... | collective-permute-start | bytes 405512 | tf_op jit(solution)/shard_map/ppermute | solution.py:375
  31.8 13.0 %collective-permute-start.7 = (f32[8,6,8,128]{3,2,1,0:T(8,128)S(1)}, f32[8,6,8,128]{3,2,1,0:T(8,128)S(1)}, u32[]{:S(2)}, u32[]{:S(2)}) collective-permute-start(f32[8,6,8,128]{3,2,1,0:T(8,128)S(1)} %all_to_all.10.here), channel_id=1, source_target_pairs={{17,1},{19,3},{21,5},{23,7},{25,9},{27,11},{29,13},{31,15},{32,16}... | collective-permute-start | bytes 589832 | tf_op jit(solution)/shard_map/ppermute | solution.py:396
  35.6 9.1 %collective-permute-start.6 = (f32[8,6,8,128]{3,2,1,0:T(8,128)S(1)}, f32[8,6,8,128]{3,2,1,0:T(8,128)S(1)}, u32[]{:S(2)}, u32[]{:S(2)}) collective-permute-start(f32[8,6,8,128]{3,2,1,0:T(8,128)S(1)} %all_to_all.10.here), channel_id=1, source_target_pairs={{8,0},{10,2},{12,4},{14,6},{0,8},{17,9},{2,10},{19,11},{4,12},{21,... | collective-permute-start | bytes 589832 | tf_op jit(solution)/shard_map/ppermute | solution.py:396
  38.5 10.5 %collective-permute-start.5 = (f32[104,8,128]{2,1,0:T(8,128)S(1)}, f32[104,8,128]{2,1,0:T(8,128)S(1)}, u32[]{:S(2)}, u32[]{:S(2)}) collective-permute-start(f32[104,8,128]{2,1,0:T(8,128)S(1)} %get-tuple-element.46), channel_id=1, source_target_pairs={{1,2},{2,1},{3,4},{4,3},{5,6},{6,5},{9,10},{10,9},{11,12},{12,11},... | collective-permute-start | bytes 1277960 | tf_op jit(solution)/shard_map/ppermute | solution.py:423
  42.8 6.2 %collective-permute-start.4 = (f32[104,8,128]{2,1,0:T(8,128)S(1)}, f32[104,8,128]{2,1,0:T(8,128)S(1)}, u32[]{:S(2)}, u32[]{:S(2)}) collective-permute-start(f32[104,8,128]{2,1,0:T(8,128)S(1)} %get-tuple-element.47), channel_id=1, source_target_pairs={{0,1},{1,0},{2,3},{3,2},{4,5},{5,4},{6,7},{7,6},{8,9},{9,8},{10,11... | collective-permute-start | bytes 1277960 | tf_op jit(solution)/shard_map/ppermute | solution.py:375
  44.8 5.5 %collective-permute-start.8 = (f32[2,8,6,8,128]{4,3,2,1,0:T(8,128)S(1)}, f32[2,8,6,8,128]{4,3,2,1,0:T(8,128)S(1)}, u32[]{:S(2)}, u32[]{:S(2)}) collective-permute-start(f32[2,8,6,8,128]{4,3,2,1,0:T(8,128)S(1)} %pad_maximum_fusion.3.near), channel_id=1, source_target_pairs={{0,1},{1,0},{2,3},{3,2},{4,5},{5,4},{6,7},{7,6},{8,9},{9,8},{10,11... | collective-permute-start | bytes 1179656 | tf_op jit(solution)/shard_map/ppermute | solution.py:375
  62.2 6.0 %collective-permute-start.10 = (f32[8,2,8,128]{3,2,1,0:T(8,128)S(1)}, f32[8,2,8,128]{3,2,1,0:T(8,128)S(1)}, u32[]{:S(2)}, u32[]{:S(2)}) collective-permute-start(f32[8,2,8,128]{3,2,1,0:T(8,128)S(1)} %all_to_all.11.here), channel_id=1, source_target_pairs={{17,1},{19,3},{21,5},{23,7},{25,9},{27,11},{29,13},{31,15},{32,16}... | collective-permute-start | bytes 196616 | tf_op jit(solution)/shard_map/ppermute | solution.py:396
  64.1 5.7 %collective-permute-start.9 = (f32[8,2,8,128]{3,2,1,0:T(8,128)S(1)}, f32[8,2,8,128]{3,2,1,0:T(8,128)S(1)}, u32[]{:S(2)}, u32[]{:S(2)}) collective-permute-start(f32[8,2,8,128]{3,2,1,0:T(8,128)S(1)} %all_to_all.11.here), channel_id=1, source_target_pairs={{8,0},{10,2},{12,4},{14,6},{0,8},{17,9},{2,10},{19,11},{4,12},{21,... | collective-permute-start | bytes 196616 | tf_op jit(solution)/shard_map/ppermute | solution.py:396
  69.9 8.2 %collective-permute-start.11 = (f32[2,8,2,8,128]{4,3,2,1,0:T(8,128)S(1)}, f32[2,8,2,8,128]{4,3,2,1,0:T(8,128)S(1)}, u32[]{:S(2)}, u32[]{:S(2)}) collective-permute-start(f32[2,8,2,8,128]{4,3,2,1,0:T(8,128)S(1)} %pad_maximum_fusion.6.near), channel_id=1, source_target_pairs={{0,1},{1,0},{2,3},{3,2},{4,5},{5,4},{6,7},{7,6},{8,9},{9,8},{10,11... | collective-permute-start | bytes 393224 | tf_op jit(solution)/shard_map/ppermute | solution.py:375

commit v7 on v6

--- a/solution.py
+++ b/solution.py
@@ -226,25 +226,38 @@
 
 
 def gather_rows(scal, here, near, swapped, joined, arrays):
-    def copy(j, source):
-        for t in range(2 * arrays):
+    tiles = 2 * arrays
+    held = near.shape[0] - 8
+    zero = jnp.zeros((8, 128), F32)
+
+    def one_away(j, source):
+        for t in range(tiles):
             for dev in range(8):
-                joined[j, t, 8 * dev:8 * dev + 8, :] = source[dev, t]
-
-    copy(2, here)
-    for i in range(2):
-        after, before = 3 + i, 1 - i
-        near_after = scal[2 + i] != 0
-
-        @pl.when(near_after)
+                joined[j, t, 8 * dev:8 * dev + 8, :] = source[held + dev, t]
+
+    def two_away(j, source):
+        for t in range(tiles):
+            for dev in range(held):
+                at = pl.ds(pl.multiple_of(8 * (scal[4] + dev), 8) if held < 8 else 8 * dev, 8)
+                joined[j, t, at, :] = source[dev, t]
+
+    for t in range(tiles):
+        for dev in range(8):
+            joined[2, t, 8 * dev:8 * dev + 8, :] = here[dev, t]
+            if held < 8:
+                joined[0, t, 8 * dev:8 * dev + 8, :] = zero
+                joined[4, t, 8 * dev:8 * dev + 8, :] = zero
+    for flag, put, after, before in ((scal[2], one_away, 3, 1), (scal[3], two_away, 4, 0)):
+
+        @pl.when(flag != 0)
         def _():
-            copy(after, near.at[i])
-            copy(before, swapped.at[i])
-
-        @pl.when(jnp.logical_not(near_after))
+            put(after, near)
+            put(before, swapped)
+
+        @pl.when(flag == 0)
         def _():
-            copy(after, swapped.at[i])
-            copy(before, near.at[i])
+            put(after, swapped)
+            put(before, near)
 
 
 def unpack_rows(joined, tile, dst):
@@ -383,7 +396,7 @@
     return 2 if g // 2 % 2 != core else -2
 
 
-def spread(pack):
+def spread(pack, later=None):
     peers, devs = lax.axis_size("grp"), lax.axis_size("dev")
 
     def from_beside(array, by):
@@ -396,15 +409,19 @@
         return lax.ppermute(array, ("grp", "dev"), pairs)
 
     here = lax.all_to_all(jnp.broadcast_to(pack, (devs,) + pack.shape), "dev", 0, 0)
-    near = jnp.stack([from_beside(here, one_away), from_beside(here, two_away)])
-    return here, near, other_core(near)
+    some = here
+    if later is not None:
+        here, later = lax.optimization_barrier((here, later))
+        some = jnp.where(lax.axis_index("dev") < 4, here[:6], here[2:])
+    near = jnp.concatenate([from_beside(some, two_away), from_beside(here, one_away)])
+    return later, here, near, other_core(near)
 
 
 def local(source, absorb, conduct):
     peers = lax.axis_size("grp")
     d = lax.axis_index("dev")
     g, core = lax.axis_index("grp"), d % 2
-    scal = jnp.stack([core, d, g % 2 == core, g // 2 % 2 != core]).astype(jnp.int32)
+    scal = jnp.stack([core, d, g % 2 == core, g // 2 % 2 != core, jnp.where(d < 4, 0, 2)]).astype(jnp.int32)
 
     fine = jnp.stack([source, absorb, conduct]).transpose(0, 2, 1, 3)
     even = g % 2 == 0
@@ -428,7 +445,7 @@
     near_b = other_chip(jnp.where(core == 0, near[0], near[1]))
     block, wide_mid, wide_low = (ROWS, FX, 128), (MROWS, MX, 128), (LROWS, LX, 128)
     pack, ends = call(first_kernel, [(6, 8, 128), (2, 16, 128)], [block] * 9, scal, fine, near_a, near_b)
-    parts = spread(pack)
+    ends, *parts = spread(pack, ends)
     whole, ends = fine.reshape(3 * ROWS, 8, 128), ends.reshape(2, 2, 8, 128)
     via_a = other_core(jnp.concatenate([whole, jnp.where(core == 0, ends[0], ends[1])]))
     via_b = other_chip(jnp.concatenate([whole, jnp.where(core == 0, ends[1], ends[0])]))
@@ -439,7 +456,7 @@
         [(5, 6, 64, 128)] + [wide_mid] * 5 + [wide_low] * 5 + [(20, MX, 128), (MROWS, 80, 128), block, block],
         scal, *state, u2, *parts,
     )
-    parts = spread(pack)
+    _, *parts = spread(pack)
     out, res = call(
         last_kernel,
         [(128, 128), (128, 128)],

time: 81.5 us -> 82.2 us (level)
    ppermute x4, starting transfers between devices: 12.7 us -> 10.7 us  [from_beside(): return lax.ppermute(array, ('grp', 'dev'), pairs)]
    ppermute x4, starting transfers between devices: 15.2 us -> 16.9 us  [other_core(): return lax.ppermute(array, 'dev', [(i, i ^ 1) for i in range(8)])]
    ppermute x4, waiting for transfers between devices: 1.64 us -> 2.48 us  [from_beside(): return lax.ppermute(array, ('grp', 'dev'), pairs)]
where the time goes in v7:
time: 82.2 us; the launch traced here: 81.7 us
  starting transfers between devices  45.6 us (55%)
  blocking collectives  17.6 us (21%)
  Pallas kernels  9 us (11%)
  waiting for transfers between devices  7.07 us (9%)
  local copies, waits for them, and re-layouts  1.16 us (1%)
  between operations  1.03 us (1%)
    all_to_all x2, blocking collectives, spread(): lax.all_to_all(jnp.broadcast_to(pack, (devs,) + pack.shape), 'dev', 0, 0)  17.6 us
    ppermute x4, starting transfers between devices, other_core(): return lax.ppermute(array, 'dev', [(i, i ^ 1) for i in range(8)])  16.9 us
    ppermute x4, starting transfers between devices, from_beside(): return lax.ppermute(array, ('grp', 'dev'), pairs)  10.7 us
    ppermute x2, starting transfers between devices, other_chip(): lax.ppermute(array, 'dev', [(1, 2), (2, 1), (3, 4), (4, 3), (5, 6), (6, 5)])  9.57 us
    pallas_call x4, Pallas kernels, call(): pl.pallas_call(kernel, out_shape=[jax.ShapeDtypeStruct(s, F32) for s in o...  9 us
    ppermute x2, starting transfers between devices, swap_rows(): return lax.ppermute(array, 'grp', pairs + [(j, i) for i, j in pairs])  8.37 us
    ppermute x4, waiting for transfers between devices, from_beside(): return lax.ppermute(array, ('grp', 'dev'), pairs)  2.48 us
    ppermute x2, waiting for transfers between devices, swap_rows(): return lax.ppermute(array, 'grp', pairs + [(j, i) for i, j in pairs])  2.43 us
  transfers between devices with their start and end apart: 12, of which 6 were waited for; matrix products, arithmetic and copies ran while one was open for 0% of the time, Pallas kernels for 2%

profile of v7, /device:TPU:521, one launch (start us, length us, event | category | flops | bytes accessed | tf_op | source)
XLA Modules:
  0.0 81.7 jit_solution(7511804557288088214)
XLA Ops:
  0.7 0.9 %copy.11 = f32[8,16,128]{2,0,1:T(8,128)S(1)} copy(f32[8,16,128]{2,1,0:T(8,128)} %param.3) | data formatting | bytes 131072 | tf_op args[0]
  1.7 3.2 %collective-permute-start = (f32[3,9,8,128]{3,2,1,0:T(8,128)S(1)}, f32[3,9,8,128]{3,2,1,0:T(8,128)S(1)}, u32[]{:S(2)}, u32[]{:S(2)}) collective-permute-start(f32[3,9,8,128]{3,2,1,0:T(8,128)S(1)} %get-tuple-element.58), channel_id=1, source_target_pairs={{8,16},{24,32},{40,48},{56,64},{72,80},{88,96},{104,112},{120,128}... | collective-permute-start | bytes 331784 | tf_op jit(solution)/shard_map/ppermute | solution.py:432
  4.9 5.2 %collective-permute-start.1 = (f32[3,9,8,128]{3,2,1,0:T(8,128)S(1)}, f32[3,9,8,128]{3,2,1,0:T(8,128)S(1)}, u32[]{:S(2)}, u32[]{:S(2)}) collective-permute-start(f32[3,9,8,128]{3,2,1,0:T(8,128)S(1)} %get-tuple-element.59), channel_id=1, source_target_pairs={{0,8},{16,24},{32,40},{48,56},{64,72},{80,88},{96,104},{112,120},{... | collective-permute-start | bytes 331784 | tf_op jit(solution)/shard_map/ppermute | solution.py:432
  10.1 0.0 collective-permute-done
  10.1 2.4 %collective-permute-done.1 = f32[3,9,8,128]{3,2,1,0:T(8,128)S(1)} collective-permute-done((f32[3,9,8,128]{3,2,1,0:T(8,128)S(1)}, f32[3,9,8,128]{3,2,1,0:T(8,128)S(1)}, u32[]{:S(2)}, u32[]{:S(2)}) %collective-permute-start.1) | collective-permute-done | bytes 110624 | tf_op jit(solution)/shard_map/ppermute | solution.py:432
  12.7 0.1 fusion
  12.8 4.6 %collective-permute-start.3 = (f32[3,11,8,128]{3,2,1,0:T(8,128)S(1)}, f32[3,11,8,128]{3,2,1,0:T(8,128)S(1)}, u32[]{:S(2)}, u32[]{:S(2)}) collective-permute-start(f32[3,11,8,128]{3,2,1,0:T(8,128)S(1)} %get-tuple-element.54), channel_id=1, source_target_pairs={{1,2},{2,1},{3,4},{4,3},{5,6},{6,5},{9,10},{10,9},{11,12},{12,11},... | collective-permute-start | bytes 405512 | tf_op jit(solution)/shard_map/ppermute | solution.py:440
  17.3 1.9 %collective-permute-start.2 = (f32[3,11,8,128]{3,2,1,0:T(8,128)S(1)}, f32[3,11,8,128]{3,2,1,0:T(8,128)S(1)}, u32[]{:S(2)}, u32[]{:S(2)}) collective-permute-start(f32[3,11,8,128]{3,2,1,0:T(8,128)S(1)} %get-tuple-element.55), channel_id=1, source_target_pairs={{0,1},{1,0},{2,3},{3,2},{4,5},{5,4},{6,7},{7,6},{8,9},{9,8},{10,11... | collective-permute-start | bytes 405512 | tf_op jit(solution)/shard_map/ppermute | solution.py:388
  19.3 0.1 stack.43.scal
  19.4 0.6 collective-permute-done.3.near_b
  20.0 0.6 collective-permute-done.2.near_a
  20.6 1.1 %shard_map.50 = (f32[6,8,128]{2,1,0:T(8,128)S(1)}, f32[2,16,128]{2,1,0:T(8,128)S(1)}) custom-call(s32[5]{0:T(128)S(1)} %stack.43.scal, f32[3,34,8,128]{3,2,1,0:T(8,128)S(1)} %pad_maximum_fusion.2.own, f32[3,11,8,128]{3,2,1,0:T(8,128)S(1)} %collective-permute-done.2.near_a, f32[3,11,8,128]{3,2,1,0:T(8,128)S(1)} %collective-permute-done.3.near_b), custom_call_target="tpu_custom_call" | custom-call | tf_op jit(solution)/shard_map/pallas_call | solution.py:376
  21.7 10.1 %all_to_all.10.here = f32[8,6,8,128]{3,2,1,0:T(8,128)S(1)} all-to-all(f32[8,6,8,128]{3,2,1,0:T(8,128)S(1)} %broadcast_in_dim.6), channel_id=1, replica_groups=mesh['grp'=96,'dev'=8] {'dev'}, dimensions={0} | all-to-all | bytes 393216 | tf_op jit(solution)/shard_map/all_to_all | solution.py:411
  31.8 2.5 %collective-permute-start.7 = (f32[8,6,8,128]{3,2,1,0:T(8,128)S(1)}, f32[8,6,8,128]{3,2,1,0:T(8,128)S(1)}, u32[]{:S(2)}, u32[]{:S(2)}) collective-permute-start(f32[8,6,8,128]{3,2,1,0:T(8,128)S(1)} %all_to_all.10.here), channel_id=1, source_target_pairs={{8,0},{10,2},{12,4},{14,6},{0,8},{17,9},{2,10},{19,11},{4,12},{21,... | collective-permute-start | bytes 589832 | tf_op jit(solution)/shard_map/ppermute | solution.py:409
  34.2 3.5 %collective-permute-start.6 = (f32[6,6,8,128]{3,2,1,0:T(8,128)S(1)}, f32[6,6,8,128]{3,2,1,0:T(8,128)S(1)}, u32[]{:S(2)}, u32[]{:S(2)}) collective-permute-start(f32[6,6,8,128]{3,2,1,0:T(8,128)S(1)} %slice_select_fusion), channel_id=1, source_target_pairs={{17,1},{19,3},{21,5},{23,7},{25,9},{27,11},{29,13},{31,15},{32,16}... | collective-permute-start | bytes 442376 | tf_op jit(solution)/shard_map/ppermute | solution.py:409
  37.7 0.1 pad_maximum_fusion.1
  37.8 5.0 %collective-permute-start.5 = (f32[104,8,128]{2,1,0:T(8,128)S(1)}, f32[104,8,128]{2,1,0:T(8,128)S(1)}, u32[]{:S(2)}, u32[]{:S(2)}) collective-permute-start(f32[104,8,128]{2,1,0:T(8,128)S(1)} %get-tuple-element.50), channel_id=1, source_target_pairs={{1,2},{2,1},{3,4},{4,3},{5,6},{6,5},{9,10},{10,9},{11,12},{12,11},... | collective-permute-start | bytes 1277960 | tf_op jit(solution)/shard_map/ppermute | solution.py:440
  42.8 1.9 %collective-permute-start.4 = (f32[104,8,128]{2,1,0:T(8,128)S(1)}, f32[104,8,128]{2,1,0:T(8,128)S(1)}, u32[]{:S(2)}, u32[]{:S(2)}) collective-permute-start(f32[104,8,128]{2,1,0:T(8,128)S(1)} %get-tuple-element.51), channel_id=1, source_target_pairs={{0,1},{1,0},{2,3},{3,2},{4,5},{5,4},{6,7},{7,6},{8,9},{9,8},{10,11... | collective-permute-start | bytes 1277960 | tf_op jit(solution)/shard_map/ppermute | solution.py:388
  44.7 0.0 collective-permute-done.6
  44.8 6.1 %collective-permute-start.8 = (f32[14,6,8,128]{3,2,1,0:T(8,128)S(1)}, f32[14,6,8,128]{3,2,1,0:T(8,128)S(1)}, u32[]{:S(2)}, u32[]{:S(2)}) collective-permute-start(f32[14,6,8,128]{3,2,1,0:T(8,128)S(1)} %constant_dynamic-update-slice_fusion.near), channel_id=1, source_target_pairs={{0,1},{1,0},{2,3},{3,2},{4,5},{5,4},{6,7},{7,6},{8,9},{9,8},{10,11... | collective-permute-start | bytes 1032200 | tf_op jit(solution)/shard_map/ppermute | solution.py:388
  50.9 0.0 collective-permute-done.5.via_b
  50.9 1.2 %shard_map.51 = (f32[34,24,128]{2,1,0:T(8,128)S(1)}, f32[34,24,128]{2,1,0:T(8,128)S(1)}, f32[34,24,128]{2,1,0:T(8,128)S(1)}, f32[34,24,128]{2,1,0:T(8,128)S(1)},...) custom-call(s32[5]{0:T(128)S(1)} %stack.43.scal, ...), custom_call_target="tpu_custom_call" | custom-call | tf_op jit(solution)/shard_map/pallas_call | solution.py:376
  52.2 0.0 collective-permute-done.8.swapped
  52.2 3.7 %shard_map.52 = (f32[40,16,128]{2,1,0:T(8,128)S(1)}, f32[40,16,128]{2,1,0:T(8,128)S(1)}, f32[40,16,128]{2,1,0:T(8,128)S(1)}, f32[40,16,128]{2,1,0:T(8,128)S(1)},...) custom-call(s32[5]{0:T(128)S(1)} %stack.43.scal, ...), custom_call_target="tpu_custom_call" | custom-call | tf_op jit(solution)/shard_map/pallas_call | solution.py:376
  55.9 7.6 %all_to_all.11.here = f32[8,2,8,128]{3,2,1,0:T(8,128)S(1)} all-to-all(f32[8,2,8,128]{3,2,1,0:T(8,128)S(1)} %broadcast_in_dim.7), channel_id=1, replica_groups=mesh['grp'=96,'dev'=8] {'dev'}, dimensions={0} | all-to-all | bytes 131072 | tf_op jit(solution)/shard_map/all_to_all | solution.py:411
  63.5 1.9 %collective-permute-start.9 = (f32[8,2,8,128]{3,2,1,0:T(8,128)S(1)}, f32[8,2,8,128]{3,2,1,0:T(8,128)S(1)}, u32[]{:S(2)}, u32[]{:S(2)}) collective-permute-start(f32[8,2,8,128]{3,2,1,0:T(8,128)S(1)} %all_to_all.11.here), channel_id=1, source_target_pairs={{17,1},{19,3},{21,5},{23,7},{25,9},{27,11},{29,13},{31,15},{32,16}... | collective-permute-start | bytes 196616 | tf_op jit(solution)/shard_map/ppermute | solution.py:409
  65.4 2.9 %collective-permute-start.10 = (f32[8,2,8,128]{3,2,1,0:T(8,128)S(1)}, f32[8,2,8,128]{3,2,1,0:T(8,128)S(1)}, u32[]{:S(2)}, u32[]{:S(2)}) collective-permute-start(f32[8,2,8,128]{3,2,1,0:T(8,128)S(1)} %all_to_all.11.here), channel_id=1, source_target_pairs={{8,0},{10,2},{12,4},{14,6},{0,8},{17,9},{2,10},{19,11},{4,12},{21,... | collective-permute-start | bytes 196616 | tf_op jit(solution)/shard_map/ppermute | solution.py:409
  68.3 1.8 %collective-permute-done.9 = f32[8,2,8,128]{3,2,1,0:T(8,128)S(1)} collective-permute-done((f32[8,2,8,128]{3,2,1,0:T(8,128)S(1)}, f32[8,2,8,128]{3,2,1,0:T(8,128)S(1)}, u32[]{:S(2)}, u32[]{:S(2)}) %collective-permute-start.9) | collective-permute-done | bytes 65568 | tf_op jit(solution)/shard_map/ppermute | solution.py:409
  70.1 0.7 collective-permute-done.10
  70.8 7.0 %collective-permute-start.11 = (f32[16,2,8,128]{3,2,1,0:T(8,128)S(1)}, f32[16,2,8,128]{3,2,1,0:T(8,128)S(1)}, u32[]{:S(2)}, u32[]{:S(2)}) collective-permute-start(f32[16,2,8,128]{3,2,1,0:T(8,128)S(1)} %constant_dynamic-update-slice_fusion.2.near), channel_id=1, source_target_pairs={{0,1},{1,0},{2,3},{3,2},{4,5},{5,4},{6,7},{7,6},{8,9},{9,8},{10,11... | collective-permute-start | bytes 393224 | tf_op jit(solution)/shard_map/ppermute | solution.py:388
  77.8 1.0 %collective-permute-done.11.swapped = f32[16,2,8,128]{3,2,1,0:T(8,128)S(1)} collective-permute-done((f32[16,2,8,128]{3,2,1,0:T(8,128)S(1)}, f32[16,2,8,128]{3,2,1,0:T(8,128)S(1)}, u32[]{:S(2)}, u32[]{:S(2)}) %collective-permute-start.11) | collective-permute-done | bytes 131104 | tf_op jit(solution)/shard_map/ppermute | solution.py:388
  78.8 2.9 %shard_map.53 = (f32[128,128]{1,0:T(8,128)}, f32[128,128]{1,0:T(8,128)}) custom-call(s32[5]{0:T(128)S(1)} %stack.43.scal, f32[34,24,128]{2,1,0:T(8,128)S(1)} %get-tuple-element.29.src, f32[34,24,128]{2,1,0:T(8,128)S(1)} %get-tuple-element.30.fbx, f32[34,24,128]{2,1,0:T(8,128)S(1)} %get-tuple-element.31.fby, f32[34,24,128]{2,1,0:T(8,128)S(1)} %get-tuple-element.32.fbz, ...), custom_call_target="tpu_custom_call" | custom-call | tf_op jit(solution)/shard_map/pallas_call | solution.py:376
  (22 shorter events, 0.3 us)
Async XLA Ops:
  0.7 0.9 %copy-start = (f32[8,16,128]{2,1,0:T(8,128)S(1)}, f32[8,16,128]{2,1,0:T(8,128)}, u32[]{:S(2)}) copy-start(f32[8,16,128]{2,1,0:T(8,128)} %param.5) | copy-start | bytes 196612
  0.7 0.9 %copy-start.1 = (f32[8,16,128]{2,1,0:T(8,128)S(1)}, f32[8,16,128]{2,1,0:T(8,128)}, u32[]{:S(2)}) copy-start(f32[8,16,128]{2,1,0:T(8,128)} %param.4) | copy-start | bytes 196612
  1.7 8.4 %collective-permute-start = (f32[3,9,8,128]{3,2,1,0:T(8,128)S(1)}, f32[3,9,8,128]{3,2,1,0:T(8,128)S(1)}, u32[]{:S(2)}, u32[]{:S(2)}) collective-permute-start(f32[3,9,8,128]{3,2,1,0:T(8,128)S(1)} %get-tuple-element.58), channel_id=1, source_target_pairs={{8,16},{24,32},{40,48},{56,64},{72,80},{88,96},{104,112},{120,128}... | collective-permute-start | bytes 331784 | tf_op jit(solution)/shard_map/ppermute | solution.py:432
  4.9 7.6 %collective-permute-start.1 = (f32[3,9,8,128]{3,2,1,0:T(8,128)S(1)}, f32[3,9,8,128]{3,2,1,0:T(8,128)S(1)}, u32[]{:S(2)}, u32[]{:S(2)}) collective-permute-start(f32[3,9,8,128]{3,2,1,0:T(8,128)S(1)} %get-tuple-element.59), channel_id=1, source_target_pairs={{0,8},{16,24},{32,40},{48,56},{64,72},{80,88},{96,104},{112,120},{... | collective-permute-start | bytes 331784 | tf_op jit(solution)/shard_map/ppermute | solution.py:432
  12.8 7.2 %collective-permute-start.3 = (f32[3,11,8,128]{3,2,1,0:T(8,128)S(1)}, f32[3,11,8,128]{3,2,1,0:T(8,128)S(1)}, u32[]{:S(2)}, u32[]{:S(2)}) collective-permute-start(f32[3,11,8,128]{3,2,1,0:T(8,128)S(1)} %get-tuple-element.54), channel_id=1, source_target_pairs={{1,2},{2,1},{3,4},{4,3},{5,6},{6,5},{9,10},{10,9},{11,12},{12,11},... | collective-permute-start | bytes 405512 | tf_op jit(solution)/shard_map/ppermute | solution.py:440
  17.3 3.2 %collective-permute-start.2 = (f32[3,11,8,128]{3,2,1,0:T(8,128)S(1)}, f32[3,11,8,128]{3,2,1,0:T(8,128)S(1)}, u32[]{:S(2)}, u32[]{:S(2)}) collective-permute-start(f32[3,11,8,128]{3,2,1,0:T(8,128)S(1)} %get-tuple-element.55), channel_id=1, source_target_pairs={{0,1},{1,0},{2,3},{3,2},{4,5},{5,4},{6,7},{7,6},{8,9},{9,8},{10,11... | collective-permute-start | bytes 405512 | tf_op jit(solution)/shard_map/ppermute | solution.py:388
  31.8 13.0 %collective-permute-start.7 = (f32[8,6,8,128]{3,2,1,0:T(8,128)S(1)}, f32[8,6,8,128]{3,2,1,0:T(8,128)S(1)}, u32[]{:S(2)}, u32[]{:S(2)}) collective-permute-start(f32[8,6,8,128]{3,2,1,0:T(8,128)S(1)} %all_to_all.10.here), channel_id=1, source_target_pairs={{8,0},{10,2},{12,4},{14,6},{0,8},{17,9},{2,10},{19,11},{4,12},{21,... | collective-permute-start | bytes 589832 | tf_op jit(solution)/shard_map/ppermute | solution.py:409
  34.2 10.5 %collective-permute-start.6 = (f32[6,6,8,128]{3,2,1,0:T(8,128)S(1)}, f32[6,6,8,128]{3,2,1,0:T(8,128)S(1)}, u32[]{:S(2)}, u32[]{:S(2)}) collective-permute-start(f32[6,6,8,128]{3,2,1,0:T(8,128)S(1)} %slice_select_fusion), channel_id=1, source_target_pairs={{17,1},{19,3},{21,5},{23,7},{25,9},{27,11},{29,13},{31,15},{32,16}... | collective-permute-start | bytes 442376 | tf_op jit(solution)/shard_map/ppermute | solution.py:409
  37.8 13.1 %collective-permute-start.5 = (f32[104,8,128]{2,1,0:T(8,128)S(1)}, f32[104,8,128]{2,1,0:T(8,128)S(1)}, u32[]{:S(2)}, u32[]{:S(2)}) collective-permute-start(f32[104,8,128]{2,1,0:T(8,128)S(1)} %get-tuple-element.50), channel_id=1, source_target_pairs={{1,2},{2,1},{3,4},{4,3},{5,6},{6,5},{9,10},{10,9},{11,12},{12,11},... | collective-permute-start | bytes 1277960 | tf_op jit(solution)/shard_map/ppermute | solution.py:440
  42.8 8.1 %collective-permute-start.4 = (f32[104,8,128]{2,1,0:T(8,128)S(1)}, f32[104,8,128]{2,1,0:T(8,128)S(1)}, u32[]{:S(2)}, u32[]{:S(2)}) collective-permute-start(f32[104,8,128]{2,1,0:T(8,128)S(1)} %get-tuple-element.51), channel_id=1, source_target_pairs={{0,1},{1,0},{2,3},{3,2},{4,5},{5,4},{6,7},{7,6},{8,9},{9,8},{10,11... | collective-permute-start | bytes 1277960 | tf_op jit(solution)/shard_map/ppermute | solution.py:388
  44.8 7.4 %collective-permute-start.8 = (f32[14,6,8,128]{3,2,1,0:T(8,128)S(1)}, f32[14,6,8,128]{3,2,1,0:T(8,128)S(1)}, u32[]{:S(2)}, u32[]{:S(2)}) collective-permute-start(f32[14,6,8,128]{3,2,1,0:T(8,128)S(1)} %constant_dynamic-update-slice_fusion.near), channel_id=1, source_target_pairs={{0,1},{1,0},{2,3},{3,2},{4,5},{5,4},{6,7},{7,6},{8,9},{9,8},{10,11... | collective-permute-start | bytes 1032200 | tf_op jit(solution)/shard_map/ppermute | solution.py:388
  63.5 6.6 %collective-permute-start.9 = (f32[8,2,8,128]{3,2,1,0:T(8,128)S(1)}, f32[8,2,8,128]{3,2,1,0:T(8,128)S(1)}, u32[]{:S(2)}, u32[]{:S(2)}) collective-permute-start(f32[8,2,8,128]{3,2,1,0:T(8,128)S(1)} %all_to_all.11.here), channel_id=1, source_target_pairs={{17,1},{19,3},{21,5},{23,7},{25,9},{27,11},{29,13},{31,15},{32,16}... | collective-permute-start | bytes 196616 | tf_op jit(solution)/shard_map/ppermute | solution.py:409
  65.4 5.4 %collective-permute-start.10 = (f32[8,2,8,128]{3,2,1,0:T(8,128)S(1)}, f32[8,2,8,128]{3,2,1,0:T(8,128)S(1)}, u32[]{:S(2)}, u32[]{:S(2)}) collective-permute-start(f32[8,2,8,128]{3,2,1,0:T(8,128)S(1)} %all_to_all.11.here), channel_id=1, source_target_pairs={{8,0},{10,2},{12,4},{14,6},{0,8},{17,9},{2,10},{19,11},{4,12},{21,... | collective-permute-start | bytes 196616 | tf_op jit(solution)/shard_map/ppermute | solution.py:409
  70.8 8.0 %collective-permute-start.11 = (f32[16,2,8,128]{3,2,1,0:T(8,128)S(1)}, f32[16,2,8,128]{3,2,1,0:T(8,128)S(1)}, u32[]{:S(2)}, u32[]{:S(2)}) collective-permute-start(f32[16,2,8,128]{3,2,1,0:T(8,128)S(1)} %constant_dynamic-update-slice_fusion.2.near), channel_id=1, source_target_pairs={{0,1},{1,0},{2,3},{3,2},{4,5},{5,4},{6,7},{7,6},{8,9},{9,8},{10,11... | collective-permute-start | bytes 393224 | tf_op jit(solution)/shard_map/ppermute | solution.py:388

commit v8 on v6

--- a/solution.py
+++ b/solution.py
@@ -181,23 +181,22 @@
     even = scal[0] == 0
     for arr, dst in ((0, src), (1, absorb), (2, conduct)):
         for i in range(22):
-            y = HALO - 3 + i
+            y, half = HALO - 3 + i, 4 * (i % 2)
             a, b = near_a[arr, i // 2], near_b[arr, i // 2]
-            left, right = jnp.where(even, b, a), jnp.where(even, a, b)
-            dst[y, 0:8, :] = down(left, 0, 4) if i % 2 == 0 else left
-            dst[y, 8:16, :] = own[arr, y]
-            dst[y, 16:24, :] = right if i % 2 == 0 else down(right, 0, 4)
+            dst[y, 0:4, :] = jnp.where(even, b, a)[half:half + 4]
+            dst[y, 4:12, :] = own[arr, y]
+            dst[y, 12:16, :] = jnp.where(even, a, b)[half:half + 4]
     level = Level(bx, by, bz, diag, inv, 1, False)
     level.build(conduct, absorb, HALO - 2, ROWS - HALO + 2, 1.0)
     u1 = FirstSweep(level, src)
     for y in range(16):
-        own_rows = inv[HALO + y, 8:16, :] * src[HALO + y, 8:16, :]
+        own_rows = inv[HALO + y, 4:12, :] * src[HALO + y, 4:12, :]
         ends[0, y:y + 1, :] = own_rows[0:1]
         ends[1, y:y + 1, :] = own_rows[7:8]
     level.sweep(u2, u1, src, HALO - 1, ROWS - HALO + 1)
-    tiles = restrict_own([r[8:16] for r in level.residual(u2, src, HALO, 16)])
-    tiles += restrict_own([absorb[HALO + i, 8:16, :] for i in range(16)])
-    tiles += restrict_own([conduct[HALO + i, 8:16, :] for i in range(16)])
+    tiles = restrict_own([r[4:12] for r in level.residual(u2, src, HALO, 16)])
+    tiles += restrict_own([own[1, HALO + i] for i in range(16)])
+    tiles += restrict_own([own[2, HALO + i] for i in range(16)])
     for i, t in enumerate(tiles):
         pack[i] = t
 
@@ -427,7 +426,7 @@
     near_a = other_core(jnp.where(core == 0, near[1], near[0]))
     near_b = other_chip(jnp.where(core == 0, near[0], near[1]))
     block, wide_mid, wide_low = (ROWS, FX, 128), (MROWS, MX, 128), (LROWS, LX, 128)
-    pack, ends = call(first_kernel, [(6, 8, 128), (2, 16, 128)], [block] * 9, scal, fine, near_a, near_b)
+    pack, ends = call(first_kernel, [(6, 8, 128), (2, 16, 128)], [(ROWS, 16, 128)] * 9, scal, fine, near_a, near_b)
     parts = spread(pack)
     whole, ends = fine.reshape(3 * ROWS, 8, 128), ends.reshape(2, 2, 8, 128)
     via_a = other_core(jnp.concatenate([whole, jnp.where(core == 0, ends[0], ends[1])]))

time: 81.5 us -> 81.5 us (level)
  no operation moved by 1% of the time
where the time goes in v8:
time: 81.5 us; the launch traced here: 81 us
  starting transfers between devices  45.1 us (55%)
  blocking collectives  18.3 us (22%)
  Pallas kernels  8.93 us (11%)
  waiting for transfers between devices  6.3 us (8%)
  local copies, waits for them, and re-layouts  1.04 us (1%)
  between operations  1.01 us (1%)
    all_to_all x2, blocking collectives, spread(): lax.all_to_all(jnp.broadcast_to(pack, (devs,) + pack.shape), 'dev', 0, 0)  18.3 us
    ppermute x4, starting transfers between devices, other_core(): return lax.ppermute(array, 'dev', [(i, i ^ 1) for i in range(8)])  15.2 us
    ppermute x4, starting transfers between devices, from_beside(): return lax.ppermute(array, ('grp', 'dev'), pairs)  12.7 us
    pallas_call x4, Pallas kernels, call(): pl.pallas_call(kernel, out_shape=[jax.ShapeDtypeStruct(s, F32) for s in o...  8.93 us
    ppermute x2, starting transfers between devices, other_chip(): lax.ppermute(array, 'dev', [(1, 2), (2, 1), (3, 4), (4, 3), (5, 6), (6, 5)])  8.81 us
    ppermute x2, starting transfers between devices, swap_rows(): return lax.ppermute(array, 'grp', pairs + [(j, i) for i, j in pairs])  8.37 us
    ppermute x2, waiting for transfers between devices, swap_rows(): return lax.ppermute(array, 'grp', pairs + [(j, i) for i, j in pairs])  2.43 us
    ppermute x4, waiting for transfers between devices, from_beside(): return lax.ppermute(array, ('grp', 'dev'), pairs)  1.64 us
  transfers between devices with their start and end apart: 12, of which 6 were waited for; matrix products, arithmetic and copies ran while one was open for 0% of the time, Pallas kernels for 2%

profile of v8, /device:TPU:521, one launch (start us, length us, event | category | flops | bytes accessed | tf_op | source)
XLA Modules:
  0.0 81.0 jit_solution(18234486410460966530)
XLA Ops:
  0.7 0.9 %copy.11 = f32[8,16,128]{2,0,1:T(8,128)S(1)} copy(f32[8,16,128]{2,1,0:T(8,128)} %param.3) | data formatting | bytes 131072 | tf_op args[0]
  1.7 3.2 %collective-permute-start = (f32[3,9,8,128]{3,2,1,0:T(8,128)S(1)}, f32[3,9,8,128]{3,2,1,0:T(8,128)S(1)}, u32[]{:S(2)}, u32[]{:S(2)}) collective-permute-start(f32[3,9,8,128]{3,2,1,0:T(8,128)S(1)} %get-tuple-element.54), channel_id=1, source_target_pairs={{8,16},{24,32},{40,48},{56,64},{72,80},{88,96},{104,112},{120,128}... | collective-permute-start | bytes 331784 | tf_op jit(solution)/shard_map/ppermute | solution.py:414
  4.9 5.2 %collective-permute-start.1 = (f32[3,9,8,128]{3,2,1,0:T(8,128)S(1)}, f32[3,9,8,128]{3,2,1,0:T(8,128)S(1)}, u32[]{:S(2)}, u32[]{:S(2)}) collective-permute-start(f32[3,9,8,128]{3,2,1,0:T(8,128)S(1)} %get-tuple-element.55), channel_id=1, source_target_pairs={{0,8},{16,24},{32,40},{48,56},{64,72},{80,88},{96,104},{112,120},{... | collective-permute-start | bytes 331784 | tf_op jit(solution)/shard_map/ppermute | solution.py:414
  10.1 0.0 collective-permute-done
  10.1 2.4 %collective-permute-done.1 = f32[3,9,8,128]{3,2,1,0:T(8,128)S(1)} collective-permute-done((f32[3,9,8,128]{3,2,1,0:T(8,128)S(1)}, f32[3,9,8,128]{3,2,1,0:T(8,128)S(1)}, u32[]{:S(2)}, u32[]{:S(2)}) %collective-permute-start.1) | collective-permute-done | bytes 110624 | tf_op jit(solution)/shard_map/ppermute | solution.py:414
  12.7 0.1 fusion
  12.8 4.6 %collective-permute-start.3 = (f32[3,11,8,128]{3,2,1,0:T(8,128)S(1)}, f32[3,11,8,128]{3,2,1,0:T(8,128)S(1)}, u32[]{:S(2)}, u32[]{:S(2)}) collective-permute-start(f32[3,11,8,128]{3,2,1,0:T(8,128)S(1)} %get-tuple-element.50), channel_id=1, source_target_pairs={{1,2},{2,1},{3,4},{4,3},{5,6},{6,5},{9,10},{10,9},{11,12},{12,11},... | collective-permute-start | bytes 405512 | tf_op jit(solution)/shard_map/ppermute | solution.py:422
  17.3 1.9 %collective-permute-start.2 = (f32[3,11,8,128]{3,2,1,0:T(8,128)S(1)}, f32[3,11,8,128]{3,2,1,0:T(8,128)S(1)}, u32[]{:S(2)}, u32[]{:S(2)}) collective-permute-start(f32[3,11,8,128]{3,2,1,0:T(8,128)S(1)} %get-tuple-element.51), channel_id=1, source_target_pairs={{0,1},{1,0},{2,3},{3,2},{4,5},{5,4},{6,7},{7,6},{8,9},{9,8},{10,11... | collective-permute-start | bytes 405512 | tf_op jit(solution)/shard_map/ppermute | solution.py:374
  19.3 0.1 pad_add_fusion.scal
  19.4 0.6 collective-permute-done.3.near_b
  20.0 0.6 collective-permute-done.2.near_a
  20.6 1.1 %shard_map.50 = (f32[6,8,128]{2,1,0:T(8,128)S(1)}, f32[2,16,128]{2,1,0:T(8,128)S(1)}) custom-call(s32[4]{0:T(128)S(1)} %pad_add_fusion.scal, f32[3,34,8,128]{3,2,1,0:T(8,128)S(1)} %pad_maximum_fusion.2.own, f32[3,11,8,128]{3,2,1,0:T(8,128)S(1)} %collective-permute-done.2.near_a, f32[3,11,8,128]{3,2,1,0:T(8,128)S(1)} %collective-permute-done.3.near_b), custom_call_target="tpu_custom_call" | custom-call | tf_op jit(solution)/shard_map/pallas_call | solution.py:362
  21.7 10.1 %all_to_all.10.here = f32[8,6,8,128]{3,2,1,0:T(8,128)S(1)} all-to-all(f32[8,6,8,128]{3,2,1,0:T(8,128)S(1)} %broadcast_in_dim.6), channel_id=1, replica_groups=mesh['grp'=96,'dev'=8] {'dev'}, dimensions={0} | all-to-all | bytes 393216 | tf_op jit(solution)/shard_map/all_to_all | solution.py:397
  31.7 3.8 %collective-permute-start.7 = (f32[8,6,8,128]{3,2,1,0:T(8,128)S(1)}, f32[8,6,8,128]{3,2,1,0:T(8,128)S(1)}, u32[]{:S(2)}, u32[]{:S(2)}) collective-permute-start(f32[8,6,8,128]{3,2,1,0:T(8,128)S(1)} %all_to_all.10.here), channel_id=1, source_target_pairs={{17,1},{19,3},{21,5},{23,7},{25,9},{27,11},{29,13},{31,15},{32,16}... | collective-permute-start | bytes 589832 | tf_op jit(solution)/shard_map/ppermute | solution.py:395
  35.6 2.8 %collective-permute-start.6 = (f32[8,6,8,128]{3,2,1,0:T(8,128)S(1)}, f32[8,6,8,128]{3,2,1,0:T(8,128)S(1)}, u32[]{:S(2)}, u32[]{:S(2)}) collective-permute-start(f32[8,6,8,128]{3,2,1,0:T(8,128)S(1)} %all_to_all.10.here), channel_id=1, source_target_pairs={{8,0},{10,2},{12,4},{14,6},{0,8},{17,9},{2,10},{19,11},{4,12},{21,... | collective-permute-start | bytes 589832 | tf_op jit(solution)/shard_map/ppermute | solution.py:395
  38.4 0.1 pad_maximum_fusion.1
  38.5 4.3 %collective-permute-start.5 = (f32[104,8,128]{2,1,0:T(8,128)S(1)}, f32[104,8,128]{2,1,0:T(8,128)S(1)}, u32[]{:S(2)}, u32[]{:S(2)}) collective-permute-start(f32[104,8,128]{2,1,0:T(8,128)S(1)} %get-tuple-element.46), channel_id=1, source_target_pairs={{1,2},{2,1},{3,4},{4,3},{5,6},{6,5},{9,10},{10,9},{11,12},{12,11},... | collective-permute-start | bytes 1277960 | tf_op jit(solution)/shard_map/ppermute | solution.py:422
  42.8 1.9 %collective-permute-start.4 = (f32[104,8,128]{2,1,0:T(8,128)S(1)}, f32[104,8,128]{2,1,0:T(8,128)S(1)}, u32[]{:S(2)}, u32[]{:S(2)}) collective-permute-start(f32[104,8,128]{2,1,0:T(8,128)S(1)} %get-tuple-element.47), channel_id=1, source_target_pairs={{0,1},{1,0},{2,3},{3,2},{4,5},{5,4},{6,7},{7,6},{8,9},{9,8},{10,11... | collective-permute-start | bytes 1277960 | tf_op jit(solution)/shard_map/ppermute | solution.py:374
  44.7 0.0 collective-permute-done.7
  44.7 0.0 collective-permute-done.6
  44.7 4.2 %collective-permute-start.8 = (f32[2,8,6,8,128]{4,3,2,1,0:T(8,128)S(1)}, f32[2,8,6,8,128]{4,3,2,1,0:T(8,128)S(1)}, u32[]{:S(2)}, u32[]{:S(2)}) collective-permute-start(f32[2,8,6,8,128]{4,3,2,1,0:T(8,128)S(1)} %pad_maximum_fusion.3.near), channel_id=1, source_target_pairs={{0,1},{1,0},{2,3},{3,2},{4,5},{5,4},{6,7},{7,6},{8,9},{9,8},{10,11... | collective-permute-start | bytes 1179656 | tf_op jit(solution)/shard_map/ppermute | solution.py:374
  48.9 0.0 collective-permute-done.5.via_b
  49.0 1.2 %shard_map.51 = (f32[34,24,128]{2,1,0:T(8,128)S(1)}, f32[34,24,128]{2,1,0:T(8,128)S(1)}, f32[34,24,128]{2,1,0:T(8,128)S(1)}, f32[34,24,128]{2,1,0:T(8,128)S(1)},...) custom-call(s32[4]{0:T(128)S(1)} %pad_add_fusion.scal, ...), custom_call_target="tpu_custom_call" | custom-call | tf_op jit(solution)/shard_map/pallas_call | solution.py:362
  50.2 0.1 collective-permute-done.8.swapped
  50.3 3.7 %shard_map.52 = (f32[40,16,128]{2,1,0:T(8,128)S(1)}, f32[40,16,128]{2,1,0:T(8,128)S(1)}, f32[40,16,128]{2,1,0:T(8,128)S(1)}, f32[40,16,128]{2,1,0:T(8,128)S(1)},...) custom-call(s32[4]{0:T(128)S(1)} %pad_add_fusion.scal, ...), custom_call_target="tpu_custom_call" | custom-call | tf_op jit(solution)/shard_map/pallas_call | solution.py:362
  54.0 8.2 %all_to_all.11.here = f32[8,2,8,128]{3,2,1,0:T(8,128)S(1)} all-to-all(f32[8,2,8,128]{3,2,1,0:T(8,128)S(1)} %broadcast_in_dim.7), channel_id=1, replica_groups=mesh['grp'=96,'dev'=8] {'dev'}, dimensions={0} | all-to-all | bytes 131072 | tf_op jit(solution)/shard_map/all_to_all | solution.py:397
  62.2 1.9 %collective-permute-start.10 = (f32[8,2,8,128]{3,2,1,0:T(8,128)S(1)}, f32[8,2,8,128]{3,2,1,0:T(8,128)S(1)}, u32[]{:S(2)}, u32[]{:S(2)}) collective-permute-start(f32[8,2,8,128]{3,2,1,0:T(8,128)S(1)} %all_to_all.11.here), channel_id=1, source_target_pairs={{17,1},{19,3},{21,5},{23,7},{25,9},{27,11},{29,13},{31,15},{32,16}... | collective-permute-start | bytes 196616 | tf_op jit(solution)/shard_map/ppermute | solution.py:395
  64.1 4.1 %collective-permute-start.9 = (f32[8,2,8,128]{3,2,1,0:T(8,128)S(1)}, f32[8,2,8,128]{3,2,1,0:T(8,128)S(1)}, u32[]{:S(2)}, u32[]{:S(2)}) collective-permute-start(f32[8,2,8,128]{3,2,1,0:T(8,128)S(1)} %all_to_all.11.here), channel_id=1, source_target_pairs={{8,0},{10,2},{12,4},{14,6},{0,8},{17,9},{2,10},{19,11},{4,12},{21,... | collective-permute-start | bytes 196616 | tf_op jit(solution)/shard_map/ppermute | solution.py:395
  68.2 1.6 %collective-permute-done.9 = f32[8,2,8,128]{3,2,1,0:T(8,128)S(1)} collective-permute-done((f32[8,2,8,128]{3,2,1,0:T(8,128)S(1)}, f32[8,2,8,128]{3,2,1,0:T(8,128)S(1)}, u32[]{:S(2)}, u32[]{:S(2)}) %collective-permute-start.9) | collective-permute-done | bytes 65568 | tf_op jit(solution)/shard_map/ppermute | solution.py:395
  69.9 7.2 %collective-permute-start.11 = (f32[2,8,2,8,128]{4,3,2,1,0:T(8,128)S(1)}, f32[2,8,2,8,128]{4,3,2,1,0:T(8,128)S(1)}, u32[]{:S(2)}, u32[]{:S(2)}) collective-permute-start(f32[2,8,2,8,128]{4,3,2,1,0:T(8,128)S(1)} %pad_maximum_fusion.6.near), channel_id=1, source_target_pairs={{0,1},{1,0},{2,3},{3,2},{4,5},{5,4},{6,7},{7,6},{8,9},{9,8},{10,11... | collective-permute-start | bytes 393224 | tf_op jit(solution)/shard_map/ppermute | solution.py:374
  77.1 1.0 %collective-permute-done.11.swapped = f32[2,8,2,8,128]{4,3,2,1,0:T(8,128)S(1)} collective-permute-done((f32[2,8,2,8,128]{4,3,2,1,0:T(8,128)S(1)}, f32[2,8,2,8,128]{4,3,2,1,0:T(8,128)S(1)}, u32[]{:S(2)}, u32[]{:S(2)}) %collective-permute-start.11) | collective-permute-done | bytes 131104 | tf_op jit(solution)/shard_map/ppermute | solution.py:374
  78.0 2.9 %shard_map.53 = (f32[128,128]{1,0:T(8,128)}, f32[128,128]{1,0:T(8,128)}) custom-call(s32[4]{0:T(128)S(1)} %pad_add_fusion.scal, f32[34,24,128]{2,1,0:T(8,128)S(1)} %get-tuple-element.25.src, f32[34,24,128]{2,1,0:T(8,128)S(1)} %get-tuple-element.26.fbx, f32[34,24,128]{2,1,0:T(8,128)S(1)} %get-tuple-element.27.fby, f32[34,24,128]{2,1,0:T(8,128)S(1)} %get-tuple-element.28.fbz, ...), custom_call_target="tpu_custom_call" | custom-call | tf_op jit(solution)/shard_map/pallas_call | solution.py:362
  (19 shorter events, 0.3 us)
Async XLA Ops:
  0.7 0.9 %copy-start = (f32[8,16,128]{2,1,0:T(8,128)S(1)}, f32[8,16,128]{2,1,0:T(8,128)}, u32[]{:S(2)}) copy-start(f32[8,16,128]{2,1,0:T(8,128)} %param.5) | copy-start | bytes 196612
  0.7 0.9 %copy-start.1 = (f32[8,16,128]{2,1,0:T(8,128)S(1)}, f32[8,16,128]{2,1,0:T(8,128)}, u32[]{:S(2)}) copy-start(f32[8,16,128]{2,1,0:T(8,128)} %param.4) | copy-start | bytes 196612
  1.7 8.4 %collective-permute-start = (f32[3,9,8,128]{3,2,1,0:T(8,128)S(1)}, f32[3,9,8,128]{3,2,1,0:T(8,128)S(1)}, u32[]{:S(2)}, u32[]{:S(2)}) collective-permute-start(f32[3,9,8,128]{3,2,1,0:T(8,128)S(1)} %get-tuple-element.54), channel_id=1, source_target_pairs={{8,16},{24,32},{40,48},{56,64},{72,80},{88,96},{104,112},{120,128}... | collective-permute-start | bytes 331784 | tf_op jit(solution)/shard_map/ppermute | solution.py:414
  4.9 7.6 %collective-permute-start.1 = (f32[3,9,8,128]{3,2,1,0:T(8,128)S(1)}, f32[3,9,8,128]{3,2,1,0:T(8,128)S(1)}, u32[]{:S(2)}, u32[]{:S(2)}) collective-permute-start(f32[3,9,8,128]{3,2,1,0:T(8,128)S(1)} %get-tuple-element.55), channel_id=1, source_target_pairs={{0,8},{16,24},{32,40},{48,56},{64,72},{80,88},{96,104},{112,120},{... | collective-permute-start | bytes 331784 | tf_op jit(solution)/shard_map/ppermute | solution.py:414
  12.8 7.2 %collective-permute-start.3 = (f32[3,11,8,128]{3,2,1,0:T(8,128)S(1)}, f32[3,11,8,128]{3,2,1,0:T(8,128)S(1)}, u32[]{:S(2)}, u32[]{:S(2)}) collective-permute-start(f32[3,11,8,128]{3,2,1,0:T(8,128)S(1)} %get-tuple-element.50), channel_id=1, source_target_pairs={{1,2},{2,1},{3,4},{4,3},{5,6},{6,5},{9,10},{10,9},{11,12},{12,11},... | collective-permute-start | bytes 405512 | tf_op jit(solution)/shard_map/ppermute | solution.py:422
  17.3 3.2 %collective-permute-start.2 = (f32[3,11,8,128]{3,2,1,0:T(8,128)S(1)}, f32[3,11,8,128]{3,2,1,0:T(8,128)S(1)}, u32[]{:S(2)}, u32[]{:S(2)}) collective-permute-start(f32[3,11,8,128]{3,2,1,0:T(8,128)S(1)} %get-tuple-element.51), channel_id=1, source_target_pairs={{0,1},{1,0},{2,3},{3,2},{4,5},{5,4},{6,7},{7,6},{8,9},{9,8},{10,11... | collective-permute-start | bytes 405512 | tf_op jit(solution)/shard_map/ppermute | solution.py:374
  31.7 13.0 %collective-permute-start.7 = (f32[8,6,8,128]{3,2,1,0:T(8,128)S(1)}, f32[8,6,8,128]{3,2,1,0:T(8,128)S(1)}, u32[]{:S(2)}, u32[]{:S(2)}) collective-permute-start(f32[8,6,8,128]{3,2,1,0:T(8,128)S(1)} %all_to_all.10.here), channel_id=1, source_target_pairs={{17,1},{19,3},{21,5},{23,7},{25,9},{27,11},{29,13},{31,15},{32,16}... | collective-permute-start | bytes 589832 | tf_op jit(solution)/shard_map/ppermute | solution.py:395
  35.6 9.1 %collective-permute-start.6 = (f32[8,6,8,128]{3,2,1,0:T(8,128)S(1)}, f32[8,6,8,128]{3,2,1,0:T(8,128)S(1)}, u32[]{:S(2)}, u32[]{:S(2)}) collective-permute-start(f32[8,6,8,128]{3,2,1,0:T(8,128)S(1)} %all_to_all.10.here), channel_id=1, source_target_pairs={{8,0},{10,2},{12,4},{14,6},{0,8},{17,9},{2,10},{19,11},{4,12},{21,... | collective-permute-start | bytes 589832 | tf_op jit(solution)/shard_map/ppermute | solution.py:395
  38.5 10.5 %collective-permute-start.5 = (f32[104,8,128]{2,1,0:T(8,128)S(1)}, f32[104,8,128]{2,1,0:T(8,128)S(1)}, u32[]{:S(2)}, u32[]{:S(2)}) collective-permute-start(f32[104,8,128]{2,1,0:T(8,128)S(1)} %get-tuple-element.46), channel_id=1, source_target_pairs={{1,2},{2,1},{3,4},{4,3},{5,6},{6,5},{9,10},{10,9},{11,12},{12,11},... | collective-permute-start | bytes 1277960 | tf_op jit(solution)/shard_map/ppermute | solution.py:422
  42.8 6.2 %collective-permute-start.4 = (f32[104,8,128]{2,1,0:T(8,128)S(1)}, f32[104,8,128]{2,1,0:T(8,128)S(1)}, u32[]{:S(2)}, u32[]{:S(2)}) collective-permute-start(f32[104,8,128]{2,1,0:T(8,128)S(1)} %get-tuple-element.47), channel_id=1, source_target_pairs={{0,1},{1,0},{2,3},{3,2},{4,5},{5,4},{6,7},{7,6},{8,9},{9,8},{10,11... | collective-permute-start | bytes 1277960 | tf_op jit(solution)/shard_map/ppermute | solution.py:374
  44.7 5.5 %collective-permute-start.8 = (f32[2,8,6,8,128]{4,3,2,1,0:T(8,128)S(1)}, f32[2,8,6,8,128]{4,3,2,1,0:T(8,128)S(1)}, u32[]{:S(2)}, u32[]{:S(2)}) collective-permute-start(f32[2,8,6,8,128]{4,3,2,1,0:T(8,128)S(1)} %pad_maximum_fusion.3.near), channel_id=1, source_target_pairs={{0,1},{1,0},{2,3},{3,2},{4,5},{5,4},{6,7},{7,6},{8,9},{9,8},{10,11... | collective-permute-start | bytes 1179656 | tf_op jit(solution)/shard_map/ppermute | solution.py:374
  62.2 6.0 %collective-permute-start.10 = (f32[8,2,8,128]{3,2,1,0:T(8,128)S(1)}, f32[8,2,8,128]{3,2,1,0:T(8,128)S(1)}, u32[]{:S(2)}, u32[]{:S(2)}) collective-permute-start(f32[8,2,8,128]{3,2,1,0:T(8,128)S(1)} %all_to_all.11.here), channel_id=1, source_target_pairs={{17,1},{19,3},{21,5},{23,7},{25,9},{27,11},{29,13},{31,15},{32,16}... | collective-permute-start | bytes 196616 | tf_op jit(solution)/shard_map/ppermute | solution.py:395
  64.1 5.7 %collective-permute-start.9 = (f32[8,2,8,128]{3,2,1,0:T(8,128)S(1)}, f32[8,2,8,128]{3,2,1,0:T(8,128)S(1)}, u32[]{:S(2)}, u32[]{:S(2)}) collective-permute-start(f32[8,2,8,128]{3,2,1,0:T(8,128)S(1)} %all_to_all.11.here), channel_id=1, source_target_pairs={{8,0},{10,2},{12,4},{14,6},{0,8},{17,9},{2,10},{19,11},{4,12},{21,... | collective-permute-start | bytes 196616 | tf_op jit(solution)/shard_map/ppermute | solution.py:395
  69.9 8.2 %collective-permute-start.11 = (f32[2,8,2,8,128]{4,3,2,1,0:T(8,128)S(1)}, f32[2,8,2,8,128]{4,3,2,1,0:T(8,128)S(1)}, u32[]{:S(2)}, u32[]{:S(2)}) collective-permute-start(f32[2,8,2,8,128]{4,3,2,1,0:T(8,128)S(1)} %pad_maximum_fusion.6.near), channel_id=1, source_target_pairs={{0,1},{1,0},{2,3},{3,2},{4,5},{5,4},{6,7},{7,6},{8,9},{9,8},{10,11... | collective-permute-start | bytes 393224 | tf_op jit(solution)/shard_map/ppermute | solution.py:374

commit v9 on v8

--- a/solution.py
+++ b/solution.py
@@ -379,7 +379,7 @@
 
 
 def two_away(g, core):
-    return 2 if g // 2 % 2 != core else -2
+    return 2 if g // 2 % 2 == core else -2
 
 
 def spread(pack):
@@ -403,7 +403,7 @@
     peers = lax.axis_size("grp")
     d = lax.axis_index("dev")
     g, core = lax.axis_index("grp"), d % 2
-    scal = jnp.stack([core, d, g % 2 == core, g // 2 % 2 != core]).astype(jnp.int32)
+    scal = jnp.stack([core, d, g % 2 == core, g // 2 % 2 == core]).astype(jnp.int32)
 
     fine = jnp.stack([source, absorb, conduct]).transpose(0, 2, 1, 3)
     even = g % 2 == 0

time: 81.5 us -> 81.1 us (level)
  the two profiles are of different devices: /device:TPU:521 before, /device:TPU:513 now
where the time goes in v9:
time: 81.1 us; the launch traced here: 80.6 us
  starting transfers between devices  38.2 us (47%)
  blocking collectives  17 us (21%)
  waiting for transfers between devices  14.1 us (17%)
  Pallas kernels  8.94 us (11%)
  local copies, waits for them, and re-layouts  1.04 us (1%)
  between operations  0.97 us (1%)
    all_to_all x2, blocking collectives, spread(): lax.all_to_all(jnp.broadcast_to(pack, (devs,) + pack.shape), 'dev', 0, 0)  17 us
    ppermute x4, starting transfers between devices, from_beside(): return lax.ppermute(array, ('grp', 'dev'), pairs)  15.3 us
    pallas_call x4, Pallas kernels, call(): pl.pallas_call(kernel, out_shape=[jax.ShapeDtypeStruct(s, F32) for s in o...  8.94 us
    ppermute x2, starting transfers between devices, swap_rows(): return lax.ppermute(array, 'grp', pairs + [(j, i) for i, j in pairs])  8.22 us
    ppermute x4, starting transfers between devices, other_core(): return lax.ppermute(array, 'dev', [(i, i ^ 1) for i in range(8)])  7.68 us
    ppermute x2, starting transfers between devices, other_chip(): lax.ppermute(array, 'dev', [(1, 2), (2, 1), (3, 4), (4, 3), (5, 6), (6, 5)])  7.03 us
    ppermute x4, waiting for transfers between devices, from_beside(): return lax.ppermute(array, ('grp', 'dev'), pairs)  5.88 us
    ppermute x2, waiting for transfers between devices, swap_rows(): return lax.ppermute(array, 'grp', pairs + [(j, i) for i, j in pairs])  3.55 us
  transfers between devices with their start and end apart: 12, of which 9 were waited for; matrix products, arithmetic and copies ran while one was open for 0% of the time, Pallas kernels for 2%

profile of v9, /device:TPU:513, one launch (start us, length us, event | category | flops | bytes accessed | tf_op | source)
XLA Modules:
  0.0 80.6 jit_solution(13155686369109794766)
XLA Ops:
  0.7 0.9 %copy.11 = f32[8,16,128]{2,0,1:T(8,128)S(1)} copy(f32[8,16,128]{2,1,0:T(8,128)} %param.3) | data formatting | bytes 131072 | tf_op args[0]
  1.7 6.3 %collective-permute-start = (f32[3,9,8,128]{3,2,1,0:T(8,128)S(1)}, f32[3,9,8,128]{3,2,1,0:T(8,128)S(1)}, u32[]{:S(2)}, u32[]{:S(2)}) collective-permute-start(f32[3,9,8,128]{3,2,1,0:T(8,128)S(1)} %get-tuple-element.54), channel_id=1, source_target_pairs={{8,16},{24,32},{40,48},{56,64},{72,80},{88,96},{104,112},{120,128}... | collective-permute-start | bytes 331784 | tf_op jit(solution)/shard_map/ppermute | solution.py:414
  8.0 1.9 %collective-permute-start.1 = (f32[3,9,8,128]{3,2,1,0:T(8,128)S(1)}, f32[3,9,8,128]{3,2,1,0:T(8,128)S(1)}, u32[]{:S(2)}, u32[]{:S(2)}) collective-permute-start(f32[3,9,8,128]{3,2,1,0:T(8,128)S(1)} %get-tuple-element.55), channel_id=1, source_target_pairs={{0,8},{16,24},{32,40},{48,56},{64,72},{80,88},{96,104},{112,120},{... | collective-permute-start | bytes 331784 | tf_op jit(solution)/shard_map/ppermute | solution.py:414
  9.9 0.9 %collective-permute-done = f32[3,9,8,128]{3,2,1,0:T(8,128)S(1)} collective-permute-done((f32[3,9,8,128]{3,2,1,0:T(8,128)S(1)}, f32[3,9,8,128]{3,2,1,0:T(8,128)S(1)}, u32[]{:S(2)}, u32[]{:S(2)}) %collective-permute-start) | collective-permute-done | bytes 110624 | tf_op jit(solution)/shard_map/ppermute | solution.py:414
  10.8 2.7 %collective-permute-done.1 = f32[3,9,8,128]{3,2,1,0:T(8,128)S(1)} collective-permute-done((f32[3,9,8,128]{3,2,1,0:T(8,128)S(1)}, f32[3,9,8,128]{3,2,1,0:T(8,128)S(1)}, u32[]{:S(2)}, u32[]{:S(2)}) %collective-permute-start.1) | collective-permute-done | bytes 110624 | tf_op jit(solution)/shard_map/ppermute | solution.py:414
  13.6 0.1 fusion
  13.7 5.1 %collective-permute-start.3 = (f32[3,11,8,128]{3,2,1,0:T(8,128)S(1)}, f32[3,11,8,128]{3,2,1,0:T(8,128)S(1)}, u32[]{:S(2)}, u32[]{:S(2)}) collective-permute-start(f32[3,11,8,128]{3,2,1,0:T(8,128)S(1)} %get-tuple-element.50), channel_id=1, source_target_pairs={{1,2},{2,1},{3,4},{4,3},{5,6},{6,5},{9,10},{10,9},{11,12},{12,11},... | collective-permute-start | bytes 405512 | tf_op jit(solution)/shard_map/ppermute | solution.py:422
  18.8 1.9 %collective-permute-start.2 = (f32[3,11,8,128]{3,2,1,0:T(8,128)S(1)}, f32[3,11,8,128]{3,2,1,0:T(8,128)S(1)}, u32[]{:S(2)}, u32[]{:S(2)}) collective-permute-start(f32[3,11,8,128]{3,2,1,0:T(8,128)S(1)} %get-tuple-element.51), channel_id=1, source_target_pairs={{0,1},{1,0},{2,3},{3,2},{4,5},{5,4},{6,7},{7,6},{8,9},{9,8},{10,11... | collective-permute-start | bytes 405512 | tf_op jit(solution)/shard_map/ppermute | solution.py:374
  20.8 0.1 pad_add_fusion.scal
  20.9 0.6 collective-permute-done.3.near_b
  21.5 0.6 collective-permute-done.2.near_a
  22.1 1.1 %shard_map.50 = (f32[6,8,128]{2,1,0:T(8,128)S(1)}, f32[2,16,128]{2,1,0:T(8,128)S(1)}) custom-call(s32[4]{0:T(128)S(1)} %pad_add_fusion.scal, f32[3,34,8,128]{3,2,1,0:T(8,128)S(1)} %pad_maximum_fusion.2.own, f32[3,11,8,128]{3,2,1,0:T(8,128)S(1)} %collective-permute-done.2.near_a, f32[3,11,8,128]{3,2,1,0:T(8,128)S(1)} %collective-permute-done.3.near_b), custom_call_target="tpu_custom_call" | custom-call | tf_op jit(solution)/shard_map/pallas_call | solution.py:362
  23.2 10.1 %all_to_all.10.here = f32[8,6,8,128]{3,2,1,0:T(8,128)S(1)} all-to-all(f32[8,6,8,128]{3,2,1,0:T(8,128)S(1)} %broadcast_in_dim.6), channel_id=1, replica_groups=mesh['grp'=96,'dev'=8] {'dev'}, dimensions={0} | all-to-all | bytes 393216 | tf_op jit(solution)/shard_map/all_to_all | solution.py:397
  33.2 3.8 %collective-permute-start.7 = (f32[8,6,8,128]{3,2,1,0:T(8,128)S(1)}, f32[8,6,8,128]{3,2,1,0:T(8,128)S(1)}, u32[]{:S(2)}, u32[]{:S(2)}) collective-permute-start(f32[8,6,8,128]{3,2,1,0:T(8,128)S(1)} %all_to_all.10.here), channel_id=1, source_target_pairs={{16,0},{18,2},{20,4},{22,6},{24,8},{26,10},{28,12},{30,14},{0,16},... | collective-permute-start | bytes 589832 | tf_op jit(solution)/shard_map/ppermute | solution.py:395
  37.0 4.3 %collective-permute-start.6 = (f32[8,6,8,128]{3,2,1,0:T(8,128)S(1)}, f32[8,6,8,128]{3,2,1,0:T(8,128)S(1)}, u32[]{:S(2)}, u32[]{:S(2)}) collective-permute-start(f32[8,6,8,128]{3,2,1,0:T(8,128)S(1)} %all_to_all.10.here), channel_id=1, source_target_pairs={{8,0},{10,2},{12,4},{14,6},{0,8},{17,9},{2,10},{19,11},{4,12},{21,... | collective-permute-start | bytes 589832 | tf_op jit(solution)/shard_map/ppermute | solution.py:395
  41.3 0.1 pad_maximum_fusion.1
  41.4 1.9 %collective-permute-start.5 = (f32[104,8,128]{2,1,0:T(8,128)S(1)}, f32[104,8,128]{2,1,0:T(8,128)S(1)}, u32[]{:S(2)}, u32[]{:S(2)}) collective-permute-start(f32[104,8,128]{2,1,0:T(8,128)S(1)} %get-tuple-element.46), channel_id=1, source_target_pairs={{1,2},{2,1},{3,4},{4,3},{5,6},{6,5},{9,10},{10,9},{11,12},{12,11},... | collective-permute-start | bytes 1277960 | tf_op jit(solution)/shard_map/ppermute | solution.py:422
  43.3 1.9 %collective-permute-start.4 = (f32[104,8,128]{2,1,0:T(8,128)S(1)}, f32[104,8,128]{2,1,0:T(8,128)S(1)}, u32[]{:S(2)}, u32[]{:S(2)}) collective-permute-start(f32[104,8,128]{2,1,0:T(8,128)S(1)} %get-tuple-element.47), channel_id=1, source_target_pairs={{0,1},{1,0},{2,3},{3,2},{4,5},{5,4},{6,7},{7,6},{8,9},{9,8},{10,11... | collective-permute-start | bytes 1277960 | tf_op jit(solution)/shard_map/ppermute | solution.py:374
  45.3 1.4 %collective-permute-done.6 = f32[8,6,8,128]{3,2,1,0:T(8,128)S(1)} collective-permute-done((f32[8,6,8,128]{3,2,1,0:T(8,128)S(1)}, f32[8,6,8,128]{3,2,1,0:T(8,128)S(1)}, u32[]{:S(2)}, u32[]{:S(2)}) %collective-permute-start.6) | collective-permute-done | bytes 196640 | tf_op jit(solution)/shard_map/ppermute | solution.py:395
  46.8 1.9 %collective-permute-start.8 = (f32[2,8,6,8,128]{4,3,2,1,0:T(8,128)S(1)}, f32[2,8,6,8,128]{4,3,2,1,0:T(8,128)S(1)}, u32[]{:S(2)}, u32[]{:S(2)}) collective-permute-start(f32[2,8,6,8,128]{4,3,2,1,0:T(8,128)S(1)} %pad_maximum_fusion.3.near), channel_id=1, source_target_pairs={{0,1},{1,0},{2,3},{3,2},{4,5},{5,4},{6,7},{7,6},{8,9},{9,8},{10,11... | collective-permute-start | bytes 1179656 | tf_op jit(solution)/shard_map/ppermute | solution.py:374
  48.7 2.2 %collective-permute-done.5.via_b = f32[104,8,128]{2,1,0:T(8,128)S(1)} collective-permute-done((f32[104,8,128]{2,1,0:T(8,128)S(1)}, f32[104,8,128]{2,1,0:T(8,128)S(1)}, u32[]{:S(2)}, u32[]{:S(2)}) %collective-permute-start.5) | collective-permute-done | bytes 426016 | tf_op jit(solution)/shard_map/ppermute | solution.py:422
  50.9 0.0 collective-permute-done.4.via_a
  50.9 1.2 %shard_map.51 = (f32[34,24,128]{2,1,0:T(8,128)S(1)}, f32[34,24,128]{2,1,0:T(8,128)S(1)}, f32[34,24,128]{2,1,0:T(8,128)S(1)}, f32[34,24,128]{2,1,0:T(8,128)S(1)},...) custom-call(s32[4]{0:T(128)S(1)} %pad_add_fusion.scal, ...), custom_call_target="tpu_custom_call" | custom-call | tf_op jit(solution)/shard_map/pallas_call | solution.py:362
  52.1 3.7 %shard_map.52 = (f32[40,16,128]{2,1,0:T(8,128)S(1)}, f32[40,16,128]{2,1,0:T(8,128)S(1)}, f32[40,16,128]{2,1,0:T(8,128)S(1)}, f32[40,16,128]{2,1,0:T(8,128)S(1)},...) custom-call(s32[4]{0:T(128)S(1)} %pad_add_fusion.scal, ...), custom_call_target="tpu_custom_call" | custom-call | tf_op jit(solution)/shard_map/pallas_call | solution.py:362
  55.8 6.9 %all_to_all.11.here = f32[8,2,8,128]{3,2,1,0:T(8,128)S(1)} all-to-all(f32[8,2,8,128]{3,2,1,0:T(8,128)S(1)} %broadcast_in_dim.7), channel_id=1, replica_groups=mesh['grp'=96,'dev'=8] {'dev'}, dimensions={0} | all-to-all | bytes 131072 | tf_op jit(solution)/shard_map/all_to_all | solution.py:397
  62.8 3.3 %collective-permute-start.10 = (f32[8,2,8,128]{3,2,1,0:T(8,128)S(1)}, f32[8,2,8,128]{3,2,1,0:T(8,128)S(1)}, u32[]{:S(2)}, u32[]{:S(2)}) collective-permute-start(f32[8,2,8,128]{3,2,1,0:T(8,128)S(1)} %all_to_all.11.here), channel_id=1, source_target_pairs={{16,0},{18,2},{20,4},{22,6},{24,8},{26,10},{28,12},{30,14},{0,16},... | collective-permute-start | bytes 196616 | tf_op jit(solution)/shard_map/ppermute | solution.py:395
  66.1 3.9 %collective-permute-start.9 = (f32[8,2,8,128]{3,2,1,0:T(8,128)S(1)}, f32[8,2,8,128]{3,2,1,0:T(8,128)S(1)}, u32[]{:S(2)}, u32[]{:S(2)}) collective-permute-start(f32[8,2,8,128]{3,2,1,0:T(8,128)S(1)} %all_to_all.11.here), channel_id=1, source_target_pairs={{8,0},{10,2},{12,4},{14,6},{0,8},{17,9},{2,10},{19,11},{4,12},{21,... | collective-permute-start | bytes 196616 | tf_op jit(solution)/shard_map/ppermute | solution.py:395
  70.0 2.1 %collective-permute-done.10 = f32[8,2,8,128]{3,2,1,0:T(8,128)S(1)} collective-permute-done((f32[8,2,8,128]{3,2,1,0:T(8,128)S(1)}, f32[8,2,8,128]{3,2,1,0:T(8,128)S(1)}, u32[]{:S(2)}, u32[]{:S(2)}) %collective-permute-start.10) | collective-permute-done | bytes 65568 | tf_op jit(solution)/shard_map/ppermute | solution.py:395
  72.1 2.3 %collective-permute-done.9 = f32[8,2,8,128]{3,2,1,0:T(8,128)S(1)} collective-permute-done((f32[8,2,8,128]{3,2,1,0:T(8,128)S(1)}, f32[8,2,8,128]{3,2,1,0:T(8,128)S(1)}, u32[]{:S(2)}, u32[]{:S(2)}) %collective-permute-start.9) | collective-permute-done | bytes 65568 | tf_op jit(solution)/shard_map/ppermute | solution.py:395
  74.4 1.9 %collective-permute-start.11 = (f32[2,8,2,8,128]{4,3,2,1,0:T(8,128)S(1)}, f32[2,8,2,8,128]{4,3,2,1,0:T(8,128)S(1)}, u32[]{:S(2)}, u32[]{:S(2)}) collective-permute-start(f32[2,8,2,8,128]{4,3,2,1,0:T(8,128)S(1)} %pad_maximum_fusion.6.near), channel_id=1, source_target_pairs={{0,1},{1,0},{2,3},{3,2},{4,5},{5,4},{6,7},{7,6},{8,9},{9,8},{10,11... | collective-permute-start | bytes 393224 | tf_op jit(solution)/shard_map/ppermute | solution.py:374
  76.4 1.3 %collective-permute-done.11.swapped = f32[2,8,2,8,128]{4,3,2,1,0:T(8,128)S(1)} collective-permute-done((f32[2,8,2,8,128]{4,3,2,1,0:T(8,128)S(1)}, f32[2,8,2,8,128]{4,3,2,1,0:T(8,128)S(1)}, u32[]{:S(2)}, u32[]{:S(2)}) %collective-permute-start.11) | collective-permute-done | bytes 131104 | tf_op jit(solution)/shard_map/ppermute | solution.py:374
  77.7 2.9 %shard_map.53 = (f32[128,128]{1,0:T(8,128)}, f32[128,128]{1,0:T(8,128)}) custom-call(s32[4]{0:T(128)S(1)} %pad_add_fusion.scal, f32[34,24,128]{2,1,0:T(8,128)S(1)} %get-tuple-element.25.src, f32[34,24,128]{2,1,0:T(8,128)S(1)} %get-tuple-element.26.fbx, f32[34,24,128]{2,1,0:T(8,128)S(1)} %get-tuple-element.27.fby, f32[34,24,128]{2,1,0:T(8,128)S(1)} %get-tuple-element.28.fbz, ...), custom_call_target="tpu_custom_call" | custom-call | tf_op jit(solution)/shard_map/pallas_call | solution.py:362
  (19 shorter events, 0.3 us)
Async XLA Ops:
  0.7 0.9 %copy-start = (f32[8,16,128]{2,1,0:T(8,128)S(1)}, f32[8,16,128]{2,1,0:T(8,128)}, u32[]{:S(2)}) copy-start(f32[8,16,128]{2,1,0:T(8,128)} %param.5) | copy-start | bytes 196612
  0.7 0.9 %copy-start.1 = (f32[8,16,128]{2,1,0:T(8,128)S(1)}, f32[8,16,128]{2,1,0:T(8,128)}, u32[]{:S(2)}) copy-start(f32[8,16,128]{2,1,0:T(8,128)} %param.4) | copy-start | bytes 196612
  1.7 9.1 %collective-permute-start = (f32[3,9,8,128]{3,2,1,0:T(8,128)S(1)}, f32[3,9,8,128]{3,2,1,0:T(8,128)S(1)}, u32[]{:S(2)}, u32[]{:S(2)}) collective-permute-start(f32[3,9,8,128]{3,2,1,0:T(8,128)S(1)} %get-tuple-element.54), channel_id=1, source_target_pairs={{8,16},{24,32},{40,48},{56,64},{72,80},{88,96},{104,112},{120,128}... | collective-permute-start | bytes 331784 | tf_op jit(solution)/shard_map/ppermute | solution.py:414
  8.0 5.5 %collective-permute-start.1 = (f32[3,9,8,128]{3,2,1,0:T(8,128)S(1)}, f32[3,9,8,128]{3,2,1,0:T(8,128)S(1)}, u32[]{:S(2)}, u32[]{:S(2)}) collective-permute-start(f32[3,9,8,128]{3,2,1,0:T(8,128)S(1)} %get-tuple-element.55), channel_id=1, source_target_pairs={{0,8},{16,24},{32,40},{48,56},{64,72},{80,88},{96,104},{112,120},{... | collective-permute-start | bytes 331784 | tf_op jit(solution)/shard_map/ppermute | solution.py:414
  13.7 7.8 %collective-permute-start.3 = (f32[3,11,8,128]{3,2,1,0:T(8,128)S(1)}, f32[3,11,8,128]{3,2,1,0:T(8,128)S(1)}, u32[]{:S(2)}, u32[]{:S(2)}) collective-permute-start(f32[3,11,8,128]{3,2,1,0:T(8,128)S(1)} %get-tuple-element.50), channel_id=1, source_target_pairs={{1,2},{2,1},{3,4},{4,3},{5,6},{6,5},{9,10},{10,9},{11,12},{12,11},... | collective-permute-start | bytes 405512 | tf_op jit(solution)/shard_map/ppermute | solution.py:422
  18.8 3.2 %collective-permute-start.2 = (f32[3,11,8,128]{3,2,1,0:T(8,128)S(1)}, f32[3,11,8,128]{3,2,1,0:T(8,128)S(1)}, u32[]{:S(2)}, u32[]{:S(2)}) collective-permute-start(f32[3,11,8,128]{3,2,1,0:T(8,128)S(1)} %get-tuple-element.51), channel_id=1, source_target_pairs={{0,1},{1,0},{2,3},{3,2},{4,5},{5,4},{6,7},{7,6},{8,9},{9,8},{10,11... | collective-permute-start | bytes 405512 | tf_op jit(solution)/shard_map/ppermute | solution.py:374
  33.2 12.0 %collective-permute-start.7 = (f32[8,6,8,128]{3,2,1,0:T(8,128)S(1)}, f32[8,6,8,128]{3,2,1,0:T(8,128)S(1)}, u32[]{:S(2)}, u32[]{:S(2)}) collective-permute-start(f32[8,6,8,128]{3,2,1,0:T(8,128)S(1)} %all_to_all.10.here), channel_id=1, source_target_pairs={{16,0},{18,2},{20,4},{22,6},{24,8},{26,10},{28,12},{30,14},{0,16},... | collective-permute-start | bytes 589832 | tf_op jit(solution)/shard_map/ppermute | solution.py:395
  37.0 9.7 %collective-permute-start.6 = (f32[8,6,8,128]{3,2,1,0:T(8,128)S(1)}, f32[8,6,8,128]{3,2,1,0:T(8,128)S(1)}, u32[]{:S(2)}, u32[]{:S(2)}) collective-permute-start(f32[8,6,8,128]{3,2,1,0:T(8,128)S(1)} %all_to_all.10.here), channel_id=1, source_target_pairs={{8,0},{10,2},{12,4},{14,6},{0,8},{17,9},{2,10},{19,11},{4,12},{21,... | collective-permute-start | bytes 589832 | tf_op jit(solution)/shard_map/ppermute | solution.py:395
  41.4 9.4 %collective-permute-start.5 = (f32[104,8,128]{2,1,0:T(8,128)S(1)}, f32[104,8,128]{2,1,0:T(8,128)S(1)}, u32[]{:S(2)}, u32[]{:S(2)}) collective-permute-start(f32[104,8,128]{2,1,0:T(8,128)S(1)} %get-tuple-element.46), channel_id=1, source_target_pairs={{1,2},{2,1},{3,4},{4,3},{5,6},{6,5},{9,10},{10,9},{11,12},{12,11},... | collective-permute-start | bytes 1277960 | tf_op jit(solution)/shard_map/ppermute | solution.py:422
  43.3 7.5 %collective-permute-start.4 = (f32[104,8,128]{2,1,0:T(8,128)S(1)}, f32[104,8,128]{2,1,0:T(8,128)S(1)}, u32[]{:S(2)}, u32[]{:S(2)}) collective-permute-start(f32[104,8,128]{2,1,0:T(8,128)S(1)} %get-tuple-element.47), channel_id=1, source_target_pairs={{0,1},{1,0},{2,3},{3,2},{4,5},{5,4},{6,7},{7,6},{8,9},{9,8},{10,11... | collective-permute-start | bytes 1277960 | tf_op jit(solution)/shard_map/ppermute | solution.py:374
  46.8 5.4 %collective-permute-start.8 = (f32[2,8,6,8,128]{4,3,2,1,0:T(8,128)S(1)}, f32[2,8,6,8,128]{4,3,2,1,0:T(8,128)S(1)}, u32[]{:S(2)}, u32[]{:S(2)}) collective-permute-start(f32[2,8,6,8,128]{4,3,2,1,0:T(8,128)S(1)} %pad_maximum_fusion.3.near), channel_id=1, source_target_pairs={{0,1},{1,0},{2,3},{3,2},{4,5},{5,4},{6,7},{7,6},{8,9},{9,8},{10,11... | collective-permute-start | bytes 1179656 | tf_op jit(solution)/shard_map/ppermute | solution.py:374
  62.8 9.3 %collective-permute-start.10 = (f32[8,2,8,128]{3,2,1,0:T(8,128)S(1)}, f32[8,2,8,128]{3,2,1,0:T(8,128)S(1)}, u32[]{:S(2)}, u32[]{:S(2)}) collective-permute-start(f32[8,2,8,128]{3,2,1,0:T(8,128)S(1)} %all_to_all.11.here), channel_id=1, source_target_pairs={{16,0},{18,2},{20,4},{22,6},{24,8},{26,10},{28,12},{30,14},{0,16},... | collective-permute-start | bytes 196616 | tf_op jit(solution)/shard_map/ppermute | solution.py:395
  66.1 8.3 %collective-permute-start.9 = (f32[8,2,8,128]{3,2,1,0:T(8,128)S(1)}, f32[8,2,8,128]{3,2,1,0:T(8,128)S(1)}, u32[]{:S(2)}, u32[]{:S(2)}) collective-permute-start(f32[8,2,8,128]{3,2,1,0:T(8,128)S(1)} %all_to_all.11.here), channel_id=1, source_target_pairs={{8,0},{10,2},{12,4},{14,6},{0,8},{17,9},{2,10},{19,11},{4,12},{21,... | collective-permute-start | bytes 196616 | tf_op jit(solution)/shard_map/ppermute | solution.py:395
  74.4 3.2 %collective-permute-start.11 = (f32[2,8,2,8,128]{4,3,2,1,0:T(8,128)S(1)}, f32[2,8,2,8,128]{4,3,2,1,0:T(8,128)S(1)}, u32[]{:S(2)}, u32[]{:S(2)}) collective-permute-start(f32[2,8,2,8,128]{4,3,2,1,0:T(8,128)S(1)} %pad_maximum_fusion.6.near), channel_id=1, source_target_pairs={{0,1},{1,0},{2,3},{3,2},{4,5},{5,4},{6,7},{7,6},{8,9},{9,8},{10,11... | collective-permute-start | bytes 393224 | tf_op jit(solution)/shard_map/ppermute | solution.py:374
